TPU v7x, 32 devices: a whole 2x2x4 slice. The times are simulated.
32 devices in a mesh: row: 4 (over y, x), col: 8 (over z, core).
Axes of the slice: x: 2, y: 2, z: 4, core: 2. Of those that a mesh axis runs over, the one named last changes fastest.
Arguments:
- pair_act: bfloat16 [512, 512, 128], P('row', 'col'), may hold values from -6 to 6
- out_grad: bfloat16 [512, 512, 128], P('row', 'col'), may hold values from -6 to 6
- tri_bias: bfloat16 [4, 512, 512], P(None, 'row', 'col'), may hold values from -6 to 250
- w_query: bfloat16 [128, 128], replicated, may hold values from -0.5 to 0.5
- w_key: bfloat16 [128, 128], replicated, may hold values from -0.5 to 0.5
- w_value: bfloat16 [128, 128], replicated, may hold values from -0.5 to 0.5
- w_gate: bfloat16 [128, 128], replicated, may hold values from -0.5 to 0.5
- w_out: bfloat16 [128, 128], replicated, may hold values from -0.5 to 0.5
- key_blocks: int32 [4, 3], replicated, may hold values from 0 to 3, as said below
- list_len: int32 [4], replicated, may hold values from 1 to 3, as said below
Outputs:
- d_pair: bfloat16 [512, 512, 128], P('row', 'col')
- d_bias: float32 [4, 512, 512], P(None, 'row', 'col')
- d_w_query: float32 [128, 128], replicated
- d_w_key: float32 [128, 128], replicated
- d_w_value: float32 [128, 128], replicated
- d_w_gate: float32 [128, 128], replicated
- d_w_out: float32 [128, 128], replicated
Inputs may be any that keep to these rules, and one draw needn't show every extreme that they name: `key_blocks`: entry 0 of query block b's list is b itself; its first list_len[b] entries are distinct; entries past list_len[b] are block numbers that must be ignored. `list_len`: some query block lists 3 key blocks.
All inputs are finite; a program needn't handle non-finite values.
Results may differ from a plain program's by a relative error of at most 0.015.
Values may be sent and summed in bfloat16 or wider, within the bound.
No kernel may reach another device: no remote copies, remote signals or barrier semaphores. Data moves between devices by JAX's collectives and lax.ppermute only.
A program may use at most 192 MiB of HBM per device.

v0:
```python
import jax
import jax.numpy as jnp
from jax import lax
from jax.sharding import PartitionSpec as P


def on_device(
    pair_act, out_grad, tri_bias, w_query, w_key, w_value, w_gate, w_out, key_blocks, list_len
):
    row_count = lax.axis_size("row")
    col_count = lax.axis_size("col")
    tile_rows, tile_cols, chan_width = pair_act.shape
    head_count = tri_bias.shape[0]
    query_tile = tri_bias.shape[2]
    proj_width = w_query.shape[1]
    head_dim = proj_width // head_count
    block_count, slot_count = key_blocks.shape
    token_count = tile_rows * row_count
    block_size = token_count // block_count
    col_width = tile_cols // row_count
    score_scale = head_dim ** (-0.5)
    highest = lax.Precision.HIGHEST
    col_acts, col_grads = (
        lax.all_to_all(pair_act, "row", split_axis=1, concat_axis=0, tiled=True),
        lax.all_to_all(out_grad, "row", split_axis=1, concat_axis=0, tiled=True),
    )
    stacked = lax.all_gather(tri_bias, ("row", "col"), axis=1, tiled=True)
    bias_full = stacked.reshape(head_count, row_count, col_count, tile_rows, query_tile)
    bias_full = jnp.transpose(bias_full, (0, 1, 3, 2, 4)).reshape(
        head_count, token_count, token_count
    )
    bias_blocks = bias_full.reshape(head_count, block_count, block_size, block_count, block_size)
    flat_acts = col_acts.reshape(-1, chan_width)
    flat_grads = col_grads.reshape(-1, chan_width)
    w_all = jnp.concatenate([w_query, w_key, w_value, w_gate], axis=1)
    projected = jnp.dot(flat_acts, w_all, preferred_element_type=jnp.float32)
    queries = (projected[:, :proj_width] * score_scale).astype(jnp.bfloat16)
    key_proj = projected[:, proj_width : 2 * proj_width].astype(jnp.bfloat16)
    values = projected[:, 2 * proj_width : 3 * proj_width].astype(jnp.bfloat16)
    gate_act = jax.nn.sigmoid(projected[:, 3 * proj_width :])
    d_gated = lax.dot_general(
        flat_grads, w_out, (((1,), (1,)), ((), ())), preferred_element_type=jnp.float32
    )
    block_shape = (block_count, block_size, col_width, head_count, head_dim)
    key_all = key_proj.reshape(block_shape)
    value_all = values.reshape(block_shape)
    slot_ids = jnp.arange(slot_count)
    scan_inputs = (
        queries.reshape(block_shape),
        gate_act.reshape(block_shape),
        d_gated.reshape(block_shape),
        jnp.arange(block_count, dtype=jnp.int32),
    )

    def per_block(running, inputs):
        dk_acc, dv_acc = running
        q_blk, g_blk, dg_blk, q_index = inputs
        chosen = key_blocks[q_index]
        live_slots = slot_ids < list_len[q_index]
        k_sel = jnp.take(key_all, chosen, axis=0)
        v_sel = jnp.take(value_all, chosen, axis=0)
        b_col = lax.dynamic_index_in_dim(bias_blocks, q_index, axis=3, keepdims=False)
        b_sel = jnp.take(b_col, chosen, axis=1)
        b_term = jnp.transpose(b_sel, (0, 3, 1, 2)).astype(jnp.float32)
        scores = (
            jnp.einsum("iwhd,ekwhd->whiek", q_blk, k_sel, preferred_element_type=jnp.float32)
            + b_term[None]
        )
        scores = jnp.where(live_slots[None, None, None, :, None], scores, -jnp.inf)
        row_peak = jnp.max(scores, axis=(3, 4), keepdims=True)
        exp_scores = jnp.exp(scores - row_peak)
        att_probs = exp_scores / jnp.sum(exp_scores, axis=(3, 4), keepdims=True)
        probs_low = att_probs.astype(jnp.bfloat16)
        attended = jnp.einsum(
            "whiek,ekwhd->iwhd", probs_low, v_sel, preferred_element_type=jnp.float32
        )
        gated = (g_blk * attended).astype(jnp.bfloat16)
        d_att = (dg_blk * g_blk).astype(jnp.bfloat16)
        d_gpre = (dg_blk * attended * g_blk * (1.0 - g_blk)).astype(jnp.bfloat16)
        d_probs = jnp.einsum("iwhd,ekwhd->whiek", d_att, v_sel, preferred_element_type=jnp.float32)
        delta_sum = jnp.sum(d_att.astype(jnp.float32) * attended, axis=-1)
        delta_sum = jnp.transpose(delta_sum, (1, 2, 0))[..., None, None]
        d_scores = att_probs * (d_probs - delta_sum)
        ds_low = d_scores.astype(jnp.bfloat16)
        d_query = (
            jnp.einsum("whiek,ekwhd->iwhd", ds_low, k_sel, preferred_element_type=jnp.float32)
            * score_scale
        ).astype(jnp.bfloat16)
        dk_part = jnp.einsum("whiek,iwhd->ekwhd", ds_low, q_blk, preferred_element_type=jnp.float32)
        dv_part = jnp.einsum(
            "whiek,iwhd->ekwhd", probs_low, d_att, preferred_element_type=jnp.float32
        )
        dk_acc = dk_acc.at[chosen].add(dk_part)
        dv_acc = dv_acc.at[chosen].add(dv_part)
        bias_part = jnp.transpose(jnp.sum(d_scores, axis=0), (2, 0, 3, 1))
        return ((dk_acc, dv_acc), (gated, d_query, d_gpre, bias_part))

    start = (jnp.zeros(block_shape, jnp.float32), jnp.zeros(block_shape, jnp.float32))
    (dk_acc, dv_acc), (gated, d_query, d_gpre, bias_parts) = lax.scan(per_block, start, scan_inputs)
    grads_all = jnp.concatenate(
        [
            d_query.reshape(-1, proj_width),
            dk_acc.astype(jnp.bfloat16).reshape(-1, proj_width),
            dv_acc.astype(jnp.bfloat16).reshape(-1, proj_width),
            d_gpre.reshape(-1, proj_width),
        ],
        axis=1,
    )
    d_flat = lax.dot_general(
        grads_all, w_all, (((1,), (1,)), ((), ())), preferred_element_type=jnp.float32
    ).astype(jnp.bfloat16)
    d_cols = d_flat.reshape(token_count, col_width, chan_width)
    d_pair = lax.all_to_all(d_cols, "row", split_axis=0, concat_axis=1, tiled=True)
    w_grad = lax.dot_general(
        flat_acts, grads_all, (((0,), (0,)), ((), ())), preferred_element_type=jnp.float32
    )
    o_grad = lax.dot_general(
        gated.reshape(-1, proj_width),
        flat_grads,
        (((0,), (0,)), ((), ())),
        preferred_element_type=jnp.float32,
    )
    block_match = (key_blocks[:, :, None] == jnp.arange(block_count)[None, None, :]).astype(
        jnp.float32
    )
    slot_form = jnp.transpose(bias_parts, (1, 2, 3, 0, 4)).reshape(
        slot_count, head_count, block_size, token_count
    )
    slot_cols = lax.psum_scatter(
        slot_form.astype(jnp.bfloat16), "col", scatter_dimension=3, tiled=True
    ).astype(jnp.float32)
    query_ids = lax.axis_index("col") * query_tile + jnp.arange(query_tile, dtype=jnp.int32)
    query_hit = ((query_ids // block_size)[:, None] == jnp.arange(block_count)[None, :]).astype(
        jnp.float32
    )
    slot_hit = jnp.einsum("iq,qeb->ebi", query_hit, block_match, precision=highest)
    expanded = jnp.einsum("ebi,ehki->hbki", slot_hit, slot_cols, precision=highest)
    expanded = expanded.reshape(head_count, token_count, query_tile)
    bias_grad = lax.psum_scatter(
        expanded.astype(jnp.bfloat16), "row", scatter_dimension=1, tiled=True
    ).astype(jnp.float32)
    w_sum, o_sum = lax.psum((w_grad, o_grad), ("row", "col"))
    return (
        d_pair,
        bias_grad,
        w_sum[:, :proj_width],
        w_sum[:, proj_width : 2 * proj_width],
        w_sum[:, 2 * proj_width : 3 * proj_width],
        w_sum[:, 3 * proj_width :],
        o_sum,
    )


def solution(mesh):
    in_specs = (
        P("row", "col", None),
        P("row", "col", None),
        P(None, "row", "col"),
        P(),
        P(),
        P(),
        P(),
        P(),
        P(),
        P(),
    )
    out_specs = (P("row", "col", None), P(None, "row", "col"), P(), P(), P(), P(), P())
    return jax.shard_map(
        on_device, mesh=mesh, in_specs=in_specs, out_specs=out_specs, check_vma=False
    )
```

profile of v0, /device:TPU:0, one launch (start us, length us, event | category | flops | bytes accessed | tf_op | source)
XLA Modules:
  0.0 1055.3 jit_solution(10759303191822516893)
XLA Ops:
  22.9 19.4 %all-to-all-done = bf16[128,64,128]{2,0,1:T(8,128)(2,1)S(1)} async-done(((bf16[128,64,128]{2,0,1:T(8,128)(2,1)}), bf16[128,64,128]{2,0,1:T(8,128)(2,1)S(1)}, u32[]{:S(2)}, u32[]{:S(2)}) %all-to-all-start) | async-done | bytes 2097184 | tf_op jit(solution)/shard_map/all_to_all | solution.py:24
  65.4 12.9 %reshape.133 = f32[4,128,16,4,32]{4,3,2,1,0:T(4,128)} reshape(f32[8192,128]{1,0:T(8,128)} %copy.131) | data formatting | bytes 8388608 | tf_op jit(solution)/shard_map/reshape | solution.py:50
  78.2 15.7 %copy.135 = f32[4,128,16,4,32]{1,4,3,2,0:T(8,128)} copy(f32[4,128,16,4,32]{4,3,2,1,0:T(4,128)} %reshape.133) | data formatting | bytes 8388608
  98.0 11.8 %reshape.130 = bf16[4,128,16,4,32]{4,3,2,1,0:T(4,128)(2,1)} reshape(bf16[8192,128]{1,0:T(8,128)(2,1)} %copy.127) | data formatting | bytes 4194304 | tf_op jit(solution)/shard_map/reshape | solution.py:49
  109.8 13.6 %copy.133 = bf16[4,128,16,4,32]{1,4,3,2,0:T(8,128)(2,1)} copy(bf16[4,128,16,4,32]{4,3,2,1,0:T(4,128)(2,1)} %reshape.130) | data formatting | bytes 4194304
  132.1 11.7 %reshape.131 = bf16[4,128,16,4,32]{4,3,2,1,0:T(4,128)(2,1)} reshape(bf16[8192,128]{1,0:T(8,128)(2,1)} %copy.128) | data formatting | bytes 4194304 | tf_op jit(solution)/shard_map/reshape | solution.py:45
  147.9 11.8 %reshape.134 = bf16[4,128,16,4,32]{4,3,2,1,0:T(4,128)(2,1)} reshape(bf16[8192,128]{1,0:T(8,128)(2,1)} %copy.132) | data formatting | bytes 4194304 | tf_op jit(solution)/shard_map/reshape | solution.py:46
  174.4 573.1 %while.21 = (s32[]{:T(128)}, f32[4,128,16,4,32]{1,4,3,2,0:T(8,128)}, f32[4,128,16,4,32]{1,4,3,2,0:T(8,128)}, bf16[4,128,16,4,32]{1,4,3,2,0:T(8,128)(2,1)}, bf16[...) while((s32[]{:T(128)}, ...), condition=%wide.region_7.9_spmd.clone, body=%wide.region_0.8_spmd.clone.sunk | while | flops 1295165440 | bytes 193833968 | solution.py:99
  194.6 10.6 %gather_fusion.1 = bf16[3,128,16,4,32]{4,3,2,1,0:T(4,128)(2,1)} fusion(bf16[4,128,16,4,32]{4,3,2,1,0:T(4,128)(2,1)} %get-tuple-element.465, s32[1024]{0:T(1024)S(1)} %pad_clamp_fusion.4), kind=kCustom, calls=%fused_computation.1.clone.clone.1 | custom fusion | bytes 3145740 | tf_op jit(solution)/shard_map/while/body/eval_jaxpr/jit(_take)/gather | solution.py:61
  205.2 10.7 %gather_fusion = bf16[3,128,16,4,32]{4,3,2,1,0:T(4,128)(2,1)} fusion(bf16[4,128,16,4,32]{4,3,2,1,0:T(4,128)(2,1)} %get-tuple-element.461, s32[1024]{0:T(1024)S(1)} %pad_clamp_fusion.4), kind=kCustom, calls=%fused_computation.clone.clone.1 | custom fusion | bytes 3145740 | tf_op jit(solution)/shard_map/while/body/eval_jaxpr/jit(_take)/gather | solution.py:60
  215.9 12.9 %broadcast_select_fusion.3 = (bf16[3,128,16,4,32]{4,3,2,1,0:T(4,128)(2,1)}, bf16[3,128,16,4,32]{4,3,2,1,0:T(4,128)(2,1)}) fusion(bf16[3,128,16,4,32]{4,3,2,1,0:T(4,128)(2,1)} %gather_fusion, pred[3]{0:T(512)(128)(4,1)S(1)} %get-tuple-element.400, bf16[3,128,16,4,32]{4,3,2,1,0:T(4,128)(2,1)} %gather_fusion.1), kind=kLoop, calls=%fused_computation.13.clone.1 | loop fusion | flops 1572864 | bytes 6291459 | tf_op jit(solution)/shard_map/while/body/eval_jaxpr/jit(_take)/select_n | solution.py:60
  228.8 9.5 copy.206
  257.6 10.6 %copy.205 = bf16[3,128,16,4,32]{1,4,0,3,2:T(8,128)(2,1)} copy(bf16[3,128,16,4,32]{4,3,2,1,0:T(4,128)(2,1)} %get-tuple-element.401) | data formatting | bytes 3145728 | tf_op jit(solution)/shard_map/while/body/eval_jaxpr/jit(_take)/select_n | solution.py:61
  268.2 9.8 multiply_reduce_fusion.2
  278.0 9.3 fusion.118
  331.3 10.6 %gather_fusion.1 = bf16[3,128,16,4,32]{4,3,2,1,0:T(4,128)(2,1)} fusion(bf16[4,128,16,4,32]{4,3,2,1,0:T(4,128)(2,1)} %get-tuple-element.465, s32[1024]{0:T(1024)S(1)} %pad_clamp_fusion.4), kind=kCustom, calls=%fused_computation.1.clone.clone.1 | custom fusion | bytes 3145740 | tf_op jit(solution)/shard_map/while/body/eval_jaxpr/jit(_take)/gather | solution.py:61
  342.0 10.7 %gather_fusion = bf16[3,128,16,4,32]{4,3,2,1,0:T(4,128)(2,1)} fusion(bf16[4,128,16,4,32]{4,3,2,1,0:T(4,128)(2,1)} %get-tuple-element.461, s32[1024]{0:T(1024)S(1)} %pad_clamp_fusion.4), kind=kCustom, calls=%fused_computation.clone.clone.1 | custom fusion | bytes 3145740 | tf_op jit(solution)/shard_map/while/body/eval_jaxpr/jit(_take)/gather | solution.py:60
  352.7 12.9 %broadcast_select_fusion.3 = (bf16[3,128,16,4,32]{4,3,2,1,0:T(4,128)(2,1)}, bf16[3,128,16,4,32]{4,3,2,1,0:T(4,128)(2,1)}) fusion(bf16[3,128,16,4,32]{4,3,2,1,0:T(4,128)(2,1)} %gather_fusion, pred[3]{0:T(512)(128)(4,1)S(1)} %get-tuple-element.400, bf16[3,128,16,4,32]{4,3,2,1,0:T(4,128)(2,1)} %gather_fusion.1), kind=kLoop, calls=%fused_computation.13.clone.1 | loop fusion | flops 1572864 | bytes 6291459 | tf_op jit(solution)/shard_map/while/body/eval_jaxpr/jit(_take)/select_n | solution.py:60
  365.6 9.5 copy.206
  394.4 10.6 %copy.205 = bf16[3,128,16,4,32]{1,4,0,3,2:T(8,128)(2,1)} copy(bf16[3,128,16,4,32]{4,3,2,1,0:T(4,128)(2,1)} %get-tuple-element.401) | data formatting | bytes 3145728 | tf_op jit(solution)/shard_map/while/body/eval_jaxpr/jit(_take)/select_n | solution.py:61
  405.0 9.8 multiply_reduce_fusion.2
  414.8 9.3 fusion.118
  468.1 10.6 %gather_fusion.1 = bf16[3,128,16,4,32]{4,3,2,1,0:T(4,128)(2,1)} fusion(bf16[4,128,16,4,32]{4,3,2,1,0:T(4,128)(2,1)} %get-tuple-element.465, s32[1024]{0:T(1024)S(1)} %pad_clamp_fusion.4), kind=kCustom, calls=%fused_computation.1.clone.clone.1 | custom fusion | bytes 3145740 | tf_op jit(solution)/shard_map/while/body/eval_jaxpr/jit(_take)/gather | solution.py:61
  478.7 10.7 %gather_fusion = bf16[3,128,16,4,32]{4,3,2,1,0:T(4,128)(2,1)} fusion(bf16[4,128,16,4,32]{4,3,2,1,0:T(4,128)(2,1)} %get-tuple-element.461, s32[1024]{0:T(1024)S(1)} %pad_clamp_fusion.4), kind=kCustom, calls=%fused_computation.clone.clone.1 | custom fusion | bytes 3145740 | tf_op jit(solution)/shard_map/while/body/eval_jaxpr/jit(_take)/gather | solution.py:60
  489.4 12.9 %broadcast_select_fusion.3 = (bf16[3,128,16,4,32]{4,3,2,1,0:T(4,128)(2,1)}, bf16[3,128,16,4,32]{4,3,2,1,0:T(4,128)(2,1)}) fusion(bf16[3,128,16,4,32]{4,3,2,1,0:T(4,128)(2,1)} %gather_fusion, pred[3]{0:T(512)(128)(4,1)S(1)} %get-tuple-element.400, bf16[3,128,16,4,32]{4,3,2,1,0:T(4,128)(2,1)} %gather_fusion.1), kind=kLoop, calls=%fused_computation.13.clone.1 | loop fusion | flops 1572864 | bytes 6291459 | tf_op jit(solution)/shard_map/while/body/eval_jaxpr/jit(_take)/select_n | solution.py:60
  502.3 9.5 copy.206
  531.2 10.6 %copy.205 = bf16[3,128,16,4,32]{1,4,0,3,2:T(8,128)(2,1)} copy(bf16[3,128,16,4,32]{4,3,2,1,0:T(4,128)(2,1)} %get-tuple-element.401) | data formatting | bytes 3145728 | tf_op jit(solution)/shard_map/while/body/eval_jaxpr/jit(_take)/select_n | solution.py:61
  541.7 9.8 multiply_reduce_fusion.2
  551.5 9.3 fusion.118
  604.9 10.6 %gather_fusion.1 = bf16[3,128,16,4,32]{4,3,2,1,0:T(4,128)(2,1)} fusion(bf16[4,128,16,4,32]{4,3,2,1,0:T(4,128)(2,1)} %get-tuple-element.465, s32[1024]{0:T(1024)S(1)} %pad_clamp_fusion.4), kind=kCustom, calls=%fused_computation.1.clone.clone.1 | custom fusion | bytes 3145740 | tf_op jit(solution)/shard_map/while/body/eval_jaxpr/jit(_take)/gather | solution.py:61
  615.5 10.7 %gather_fusion = bf16[3,128,16,4,32]{4,3,2,1,0:T(4,128)(2,1)} fusion(bf16[4,128,16,4,32]{4,3,2,1,0:T(4,128)(2,1)} %get-tuple-element.461, s32[1024]{0:T(1024)S(1)} %pad_clamp_fusion.4), kind=kCustom, calls=%fused_computation.clone.clone.1 | custom fusion | bytes 3145740 | tf_op jit(solution)/shard_map/while/body/eval_jaxpr/jit(_take)/gather | solution.py:60
  626.2 12.9 %broadcast_select_fusion.3 = (bf16[3,128,16,4,32]{4,3,2,1,0:T(4,128)(2,1)}, bf16[3,128,16,4,32]{4,3,2,1,0:T(4,128)(2,1)}) fusion(bf16[3,128,16,4,32]{4,3,2,1,0:T(4,128)(2,1)} %gather_fusion, pred[3]{0:T(512)(128)(4,1)S(1)} %get-tuple-element.400, bf16[3,128,16,4,32]{4,3,2,1,0:T(4,128)(2,1)} %gather_fusion.1), kind=kLoop, calls=%fused_computation.13.clone.1 | loop fusion | flops 1572864 | bytes 6291459 | tf_op jit(solution)/shard_map/while/body/eval_jaxpr/jit(_take)/select_n | solution.py:60
  639.1 9.5 copy.206
  667.9 10.6 %copy.205 = bf16[3,128,16,4,32]{1,4,0,3,2:T(8,128)(2,1)} copy(bf16[3,128,16,4,32]{4,3,2,1,0:T(4,128)(2,1)} %get-tuple-element.401) | data formatting | bytes 3145728 | tf_op jit(solution)/shard_map/while/body/eval_jaxpr/jit(_take)/select_n | solution.py:61
  678.5 9.8 multiply_reduce_fusion.2
  688.3 9.3 fusion.118
  747.4 13.4 %copy.136 = bf16[4,128,16,4,32]{4,3,2,1,0:T(4,128)(2,1)} copy(bf16[4,128,16,4,32]{1,4,3,2,0:T(8,128)(2,1)} %get-tuple-element.100) | data formatting | bytes 4194304 | tf_op jit(solution)/shard_map/while | solution.py:99
  760.8 9.5 reshape.135
  773.8 10.3 copy.137
  784.2 10.5 reshape.136
  797.5 10.3 copy.138
  807.8 10.7 %reshape.137 = bf16[8192,128]{1,0:T(8,128)(2,1)} reshape(bf16[4,128,16,4,32]{4,3,2,1,0:T(4,128)(2,1)} %copy.138) | data formatting | bytes 4194304 | tf_op jit(solution)/shard_map/reshape | solution.py:104
  823.3 10.3 copy.139
  833.6 10.7 %reshape.138 = bf16[8192,128]{1,0:T(8,128)(2,1)} reshape(bf16[4,128,16,4,32]{4,3,2,1,0:T(4,128)(2,1)} %copy.139) | data formatting | bytes 4194304 | tf_op jit(solution)/shard_map/reshape | solution.py:105
  844.4 10.3 copy.146
  854.7 9.5 reshape.140
  891.9 126.3 %all-reduce.3.cloned.1.call-done = (f32[128,512]{0,1:T(8,128)}, f32[128,128]{1,0:T(8,128)}) async-done(((f32[128,512]{0,1:T(8,128)}, f32[128,128]{1,0:T(8,128)}), (f32[128,512]{0,1:T(8,128)}, f32[128,128]{1,0:T(8,128)})) %all-reduce.3.cloned.1.call-update) | async-done | bytes 327696 | tf_op jit(solution)/shard_map/psum | solution.py:142
  1025.7 20.4 %reduce-scatter.7.cloned.1.call-done = bf16[128,256]{1,0:T(8,128)(2,1)} async-done(((bf16[512,256]{1,0:T(8,128)(2,1)}), bf16[128,256]{1,0:T(8,128)(2,1)}) %reduce-scatter.7.cloned.1.call-update) | async-done | bytes 65552
  (210 shorter events, 364.3 us)
Async XLA Ops:
  7.2 155.2 %copy-start = (bf16[128,128]{1,0:T(8,128)(2,1)S(1)}, bf16[128,128]{1,0:T(8,128)(2,1)}, u32[]{:S(2)}) copy-start(bf16[128,128]{1,0:T(8,128)(2,1)} %param.21) | copy-start | bytes 98308
  11.4 10.4 copy-start.20
  11.4 11.4 %copy-start.16 = (bf16[128,128]{1,0:T(8,128)(2,1)S(1)}, bf16[128,128]{1,0:T(8,128)(2,1)}, u32[]{:S(2)}) copy-start(bf16[128,128]{1,0:T(8,128)(2,1)} %param.17) | copy-start | bytes 98308
  11.4 11.4 %copy-start.17 = (bf16[128,128]{1,0:T(8,128)(2,1)S(1)}, bf16[128,128]{1,0:T(8,128)(2,1)}, u32[]{:S(2)}) copy-start(bf16[128,128]{1,0:T(8,128)(2,1)} %param.18) | copy-start | bytes 98308
  11.4 11.4 %copy-start.18 = (bf16[128,128]{1,0:T(8,128)(2,1)S(1)}, bf16[128,128]{1,0:T(8,128)(2,1)}, u32[]{:S(2)}) copy-start(bf16[128,128]{1,0:T(8,128)(2,1)} %param.19) | copy-start | bytes 98308
  11.4 11.5 %copy-start.19 = (bf16[128,128]{1,0:T(8,128)(2,1)S(1)}, bf16[128,128]{1,0:T(8,128)(2,1)}, u32[]{:S(2)}) copy-start(bf16[128,128]{1,0:T(8,128)(2,1)} %param.20) | copy-start | bytes 98308
  11.5 30.9 %all-to-all-start = ((bf16[128,64,128]{2,0,1:T(8,128)(2,1)}), bf16[128,64,128]{2,0,1:T(8,128)(2,1)S(1)}, u32[]{:S(2)}, u32[]{:S(2)}) async-start(bf16[128,64,128]{2,0,1:T(8,128)(2,1)} %copy.124), calls=%async_computation | async-start | bytes 4194304 | tf_op jit(solution)/shard_map/all_to_all | solution.py:24
  16.8 148.3 %all-gather.2.cloned.1.call-start = ((), (), s32[]{:S(2)}) async-start(), calls=%async_computation.5 | async-start | bytes 2162688 | tf_op jit(solution)/shard_map/all_gather | solution.py:27
  22.9 33.0 %copy-start.12 = (bf16[128,512]{1,0:T(8,128)(2,1)}, bf16[128,512]{1,0:T(8,128)(2,1)S(1)}, u32[]{:S(2)}) copy-start(bf16[128,512]{1,0:T(8,128)(2,1)S(1)} %constant_dynamic-update-slice_fusion.1) | copy-start | bytes 393220
  42.3 1.3 copy-start.7
  43.6 116.0 %all-to-all-start.1 = ((bf16[128,64,128]{2,0,1:T(8,128)(2,1)}), bf16[128,64,128]{2,0,1:T(8,128)(2,1)S(1)}, u32[]{:S(2)}, u32[]{:S(2)}) async-start(bf16[128,64,128]{2,0,1:T(8,128)(2,1)} %copy.130), calls=%async_computation.1 | async-start | bytes 4194304 | tf_op jit(solution)/shard_map/all_to_all | solution.py:25
  47.2 841.7 %reduce-scatter.5.cloned.1.call-start = ((), (), s32[]{:S(2)}) async-start(), calls=%async_computation.6 | async-start | bytes 1769472 | tf_op jit(solution)/shard_map/reduce_scatter | solution.py:129
  50.2 5.7 copy-start.8
  169.3 5.1 copy-start.21
  268.2 9.8 copy-start.4
  287.3 2.6 copy-start.2
  405.0 9.8 copy-start.4
  424.1 2.6 copy-start.2
  541.7 9.8 copy-start.4
  560.8 2.6 copy-start.2
  678.5 9.8 copy-start.4
  697.6 2.6 copy-start.2
  770.3 2.9 copy-start.3
  807.8 10.7 %copy-start.5 = (bf16[8192,128]{1,0:T(8,128)(2,1)S(1)}, bf16[8192,128]{1,0:T(8,128)(2,1)}, u32[]{:S(2)}) copy-start(bf16[8192,128]{1,0:T(8,128)(2,1)} %reshape.136) | copy-start | bytes 6291460
  818.6 2.3 copy-start.6
  820.9 2.3 copy-start.10
  833.6 10.7 %copy-start.11 = (bf16[4,128,16,4,32]{1,4,3,2,0:T(8,128)(2,1)S(1)}, bf16[4,128,16,4,32]{1,4,3,2,0:T(8,128)(2,1)}, u32[]{:S(2)}) copy-start(bf16[4,128,16,4,32]{1,4,3,2,0:T(8,128)(2,1)} %get-tuple-element.105) | copy-start | bytes 6291460
  864.2 3.2 copy-start.13
  874.4 147.7 %all-to-all-start.2 = ((bf16[512,16,128]{2,1,0:T(8,128)(2,1)}), bf16[512,16,128]{2,1,0:T(8,128)(2,1)}, u32[]{:S(2)}, u32[]{:S(2)}) async-start(bf16[512,16,128]{2,1,0:T(8,128)(2,1)} %bitcast.249), calls=%async_computation.2 | async-start | bytes 4194304 | tf_op jit(solution)/shard_map/all_to_all | solution.py:113
  878.9 139.3 %all-reduce.3.cloned.1.call-start = ((), (), s32[]{:S(2)}) async-start(), calls=%async_computation.8 | async-start | bytes 655360 | tf_op jit(solution)/shard_map/psum | solution.py:142
  879.2 3.1 copy-start.9
  882.3 6.6 copy-start.14
  888.9 159.6 %copy-start.1 = (bf16[128,128]{1,0:T(8,128)(2,1)S(1)}, bf16[128,128]{1,0:T(8,128)(2,1)}, u32[]{:S(2)}) copy-start(bf16[128,128]{1,0:T(8,128)(2,1)} %param.21) | copy-start | bytes 98308
  888.9 157.2 %reduce-scatter.7.cloned.1.call-start = ((), (), s32[]{:S(2)}) async-start(), calls=%async_computation.7 | async-start | bytes 327680
  1018.2 29.7 %copy-start.15 = (f32[128,128]{1,0:T(8,128)S(1)}, f32[128,128]{1,0:T(8,128)}, u32[]{:S(2)}) copy-start(f32[128,128]{1,0:T(8,128)} %get-tuple-element.475) | copy-start | bytes 196612
Sparse Core Ops, SparseCore 0:
  20.5 72.6 all-gather.1
  818.7 35.5 reduce-scatter.4
  889.0 129.1 all-reduce.2
  1021.0 25.0 reduce-scatter.6
where the time goes:
time: 1070 us; the launch traced here: 1060 us
  local copies, waits for them, and re-layouts  460 us (43%)
  matrix products  201 us (19%)
  waiting for transfers between devices  167 us (16%)
  other arithmetic  165 us (15%)
  loops' own time  34.1 us (3%)
  between operations  14.3 us (1%)
  starting transfers between devices  13.8 us (1%)
    psum x1, waiting for transfers between devices, on_device(): w_sum, o_sum = lax.psum((w_grad, o_grad), ('row', 'col'))  126 us
    unnamed x61, local copies, waits for them, and re-layouts  55 us
    select_n x4, other arithmetic, per_block(): k_sel = jnp.take(key_all, chosen, axis=0)  51.6 us
    gather x4, local copies, waits for them, and re-layouts, per_block(): k_sel = jnp.take(key_all, chosen, axis=0)  42.8 us
    gather x4, local copies, waits for them, and re-layouts, per_block(): v_sel = jnp.take(value_all, chosen, axis=0)  42.6 us
    select_n x4, local copies, waits for them, and re-layouts, per_block(): v_sel = jnp.take(value_all, chosen, axis=0)  42.3 us
    dot_general x4, matrix products, per_block(): jnp.einsum('whiek,ekwhd->iwhd', probs_low, v_sel, preferred_element_type=...  39.2 us
    select_n x4, local copies, waits for them, and re-layouts, per_block(): k_sel = jnp.take(key_all, chosen, axis=0)  37.8 us
  transfers between devices with their start and end apart: 7, of which 3 were waited for; matrix products, arithmetic and copies ran while one was open for 19% of the time, Pallas kernels for 0%

commit v1 on v0

v1 whole, which is shorter than its diff:
```python
import functools

import jax
import jax.numpy as jnp
from jax import lax
from jax.experimental import pallas as pl
from jax.experimental.pallas import tpu as pltpu
from jax.sharding import PartitionSpec as P

F32 = jnp.float32
BF16 = jnp.bfloat16
CHUNKS = 4
VMEM_LIMIT = 56 * 1024 * 1024


def dot(a, b):
    return jnp.dot(a, b, preferred_element_type=F32)


def transposed_bias_kernel(bias_ref, out_ref):
    for kb in range(bias_ref.shape[0]):
        for h in range(bias_ref.shape[2]):
            out_ref[kb, 0, h] = bias_ref[kb, 0, h].astype(F32).T


def transposed_bias(blocks):
    key_blocks, query_blocks, heads, queries, keys = blocks.shape
    return pl.pallas_call(
        transposed_bias_kernel,
        grid=(query_blocks,),
        in_specs=[pl.BlockSpec((key_blocks, 1, heads, queries, keys), lambda b: (0, b, 0, 0, 0))],
        out_specs=pl.BlockSpec((key_blocks, 1, heads, keys, queries), lambda b: (0, b, 0, 0, 0)),
        out_shape=jax.ShapeDtypeStruct((key_blocks, query_blocks, heads, keys, queries), F32),
        compiler_params=pltpu.CompilerParams(vmem_limit_bytes=VMEM_LIMIT),
    )(blocks)


def attention_kernel(
    dims, first, tables_ref, lens_ref, owners_ref, *refs
):
    pieces, heads, head_dim, blocks, size, slots = dims
    refs = list(refs)
    acts_in = [refs.pop(0) for _ in range(pieces)]
    bias_ref, w_all_ref, w_all_t_ref, w_out_t_ref = [refs.pop(0) for _ in range(4)]
    carried = [] if first else [refs.pop(0) for _ in range(3)]
    d_pair_out = [refs.pop(0) for _ in range(pieces)]
    d_bias_ref, d_w_ref, d_wo_ref = [refs.pop(0) for _ in range(3)]
    (act_s, grad_s, kv_s, kv_t_s, joint_s, d_att_s, query_s, d_att_t_s, gate_s, d_gated_s,
     d_kv_s, att_t_s, d_query_t_s, d_pair_s) = refs
    proj = heads * head_dim
    tokens = blocks * size
    scale = head_dim ** (-0.5)
    tile_rows = acts_in[0].shape[2]

    @pl.when(pl.program_id(0) == 0)
    def _():
        joint_s[...] = jnp.zeros_like(joint_s)
        if first:
            for ref in (d_bias_ref, d_w_ref, d_wo_ref):
                ref[...] = jnp.zeros_like(ref)
        else:
            for ref, before in zip((d_bias_ref, d_w_ref, d_wo_ref), carried):
                ref[...] = before[...]

    for s in range(pieces):
        rows = pl.ds(pl.multiple_of(owners_ref[s] * tile_rows, tile_rows), tile_rows)
        act_s[rows, :] = acts_in[s][0, 0]
        grad_s[rows, :] = acts_in[s][1, 0]
    acts = act_s[...]
    grads = grad_s[...]
    projected = dot(acts, w_all_ref[...])
    queries = (projected[:, :proj] * scale).astype(BF16)
    keys = projected[:, proj : 2 * proj].astype(BF16)
    values = projected[:, 2 * proj : 3 * proj].astype(BF16)
    gate = 1.0 / (1.0 + jnp.exp(-projected[:, 3 * proj :]))
    d_gated = dot(grads, w_out_t_ref[...])
    d_att = (d_gated * gate).astype(BF16)
    gate_s[...] = gate
    d_gated_s[...] = d_gated
    lane_head = lax.broadcasted_iota(jnp.int32, (size, proj), 1) // head_dim
    for b in range(blocks):
        part = slice(b * size, (b + 1) * size)
        kv_s[b, :, :proj] = keys[part]
        kv_s[b, :, proj:] = values[part]
        kv_t_s[b, :proj, :] = keys[part].T
        kv_t_s[b, proj:, :] = values[part].T
        query_t = queries[part].T
        d_att_t = d_att[part].T
        d_att_t_s[b] = d_att_t.astype(F32)
        for h in range(heads):
            own = slice(h * head_dim, (h + 1) * head_dim)
            low = slice(proj + h * head_dim, proj + (h + 1) * head_dim)
            joint_s[b, h, own, :size] = query_t[own]
            joint_s[b, h, low, size:] = d_att_t[own]
            here = lane_head == h
            zero = jnp.zeros((size, proj), BF16)
            query_s[b, h * size : (h + 1) * size, :] = jnp.where(here, queries[part], zero)
            d_att_s[b, h * size : (h + 1) * size, :] = jnp.where(here, d_att[part], zero)
    d_kv_s[...] = jnp.zeros_like(d_kv_s)

    def query_block(b, live):
        chosen = [tables_ref[b, e] for e in range(live)]
        kv = jnp.concatenate([kv_s[c] for c in chosen], axis=0)
        kv_t = jnp.concatenate([kv_t_s[c] for c in chosen], axis=1)
        probs_all, ds_all = [], []
        for h in range(heads):
            own = slice(h * head_dim, (h + 1) * head_dim)
            low = slice(proj + h * head_dim, proj + (h + 1) * head_dim)
            joint = dot(kv, joint_s[b, h])
            bias = jnp.concatenate([bias_ref[c, b, h] for c in chosen], axis=0)
            scores = joint[:, :size] + bias
            peak = jnp.max(scores, axis=0, keepdims=True)
            weights = jnp.exp(scores - peak)
            probs = weights * (1.0 / jnp.sum(weights, axis=0, keepdims=True))
            probs_low = probs.astype(BF16)
            att_t = dot(kv_t[low], probs_low)
            delta = jnp.sum(d_att_t_s[b, own, :] * att_t, axis=0, keepdims=True)
            d_scores = probs * (joint[:, size:] - delta)
            for e in range(live):
                d_bias_ref[b, e, h] += d_scores[e * size : (e + 1) * size]
            ds_low = d_scores.astype(BF16)
            att_t_s[b, own, :] = att_t
            d_query_t_s[b, own, :] = dot(kv_t[own], ds_low)
            probs_all.append(probs_low)
            ds_all.append(ds_low)
        d_values = dot(jnp.concatenate(probs_all, axis=1), d_att_s[b])
        d_keys = dot(jnp.concatenate(ds_all, axis=1), query_s[b])
        for e in range(live):
            part = slice(e * size, (e + 1) * size)
            d_kv_s[chosen[e], :, :proj] += d_keys[part]
            d_kv_s[chosen[e], :, proj:] += d_values[part]

    @pl.loop(0, blocks)
    def _(b):
        for live in range(1, slots + 1):

            @pl.when(lens_ref[b] == live)
            def _():
                query_block(b, live)

    d_query, attended = [], []
    for b in range(blocks):
        d_query.append((d_query_t_s[b] * scale).T.astype(BF16))
        attended.append(att_t_s[b].T)
    d_query = jnp.concatenate(d_query, axis=0)
    attended = jnp.concatenate(attended, axis=0)
    gate = gate_s[...]
    gated = (gate * attended).astype(BF16)
    d_gpre = (d_gated_s[...] * attended * gate * (1.0 - gate)).astype(BF16)
    d_kv = d_kv_s[...].reshape(tokens, 2 * proj).astype(BF16)
    d_all = jnp.concatenate([d_query, d_kv, d_gpre], axis=1)
    d_pair_s[...] = dot(d_all, w_all_t_ref[...])
    for s in range(pieces):
        rows = pl.ds(pl.multiple_of(owners_ref[s] * tile_rows, tile_rows), tile_rows)
        d_pair_out[s][0] = d_pair_s[rows, :].astype(BF16)
    d_w_ref[...] += dot(act_s[...].T, d_all)
    d_wo_ref[...] += dot(gated.T, grad_s[...])


def attention(pieces, bias_t, w_all, w_out, key_blocks, list_len, owners, carried):
    count = len(pieces)
    _, columns, tile_rows, chan = pieces[0].shape
    blocks, slots = key_blocks.shape
    heads = bias_t.shape[2]
    proj = w_out.shape[0]
    size = tile_rows * count // blocks
    tokens = blocks * size
    dims = (count, heads, proj // heads, blocks, size, slots)
    first = carried is None
    whole = lambda shape: pl.BlockSpec(shape, lambda j, *_: (0,) * len(shape))
    sums = [
        jax.ShapeDtypeStruct((blocks, slots, heads, size, size), F32),
        jax.ShapeDtypeStruct((chan, 4 * proj), F32),
        jax.ShapeDtypeStruct((proj, chan), F32),
    ]
    fixed = [bias_t, w_all, w_all.T, w_out.T] + ([] if first else list(carried))
    pairs = count * tokens // count * size * slots * heads
    outs = pl.pallas_call(
        functools.partial(attention_kernel, dims, first),
        grid_spec=pltpu.PrefetchScalarGridSpec(
            num_scalar_prefetch=3,
            grid=(columns,),
            in_specs=[pl.BlockSpec((2, 1, tile_rows, chan), lambda j, *_: (0, j, 0, 0))] * count
            + [whole(x.shape) for x in fixed],
            out_specs=[pl.BlockSpec((1, tile_rows, chan), lambda j, *_: (j, 0, 0))] * count
            + [whole(x.shape) for x in sums],
            scratch_shapes=[
                pltpu.VMEM((tokens, chan), BF16),
                pltpu.VMEM((tokens, chan), BF16),
                pltpu.VMEM((blocks, size, 2 * proj), BF16),
                pltpu.VMEM((blocks, 2 * proj, size), BF16),
                pltpu.VMEM((blocks, heads, 2 * proj, 2 * size), BF16),
                pltpu.VMEM((blocks, heads * size, proj), BF16),
                pltpu.VMEM((blocks, heads * size, proj), BF16),
                pltpu.VMEM((blocks, proj, size), F32),
                pltpu.VMEM((tokens, proj), F32),
                pltpu.VMEM((tokens, proj), F32),
                pltpu.VMEM((blocks, size, 2 * proj), F32),
                pltpu.VMEM((blocks, proj, size), F32),
                pltpu.VMEM((blocks, proj, size), F32),
                pltpu.VMEM((tokens, chan), F32),
            ],
        ),
        out_shape=[jax.ShapeDtypeStruct((columns, tile_rows, chan), BF16)] * count + sums,
        compiler_params=pltpu.CompilerParams(vmem_limit_bytes=VMEM_LIMIT),
        cost_estimate=pl.CostEstimate(
            flops=columns * pairs * proj // heads * 12,
            bytes_accessed=columns * tokens * chan * 6 + 10 * 2**20,
            transcendentals=columns * pairs,
        ),
    )(key_blocks, list_len, owners, *pieces, *fixed)
    return outs[:count], outs[count:]


def partner_lists(count):
    paired = count & (count - 1) == 0
    if paired:
        return paired, [[(r, r ^ s) for r in range(count)] for s in range(count)]
    return paired, [[(r, (r + s) % count) for r in range(count)] for s in range(count)]


def on_device(
    pair_act, out_grad, tri_bias, w_query, w_key, w_value, w_gate, w_out, key_blocks, list_len
):
    row_count = lax.axis_size("row")
    col_count = lax.axis_size("col")
    tile_rows, tile_cols, chan = pair_act.shape
    heads = tri_bias.shape[0]
    query_tile = tri_bias.shape[2]
    proj = w_query.shape[1]
    blocks, slots = key_blocks.shape
    tokens = tile_rows * row_count
    size = tokens // blocks
    col_width = tile_cols // row_count
    chunks = CHUNKS if col_width % CHUNKS == 0 else 1
    width = col_width // chunks
    me = lax.axis_index("row")
    paired, partners = partner_lists(row_count)

    bias_all = lax.all_gather(jnp.transpose(tri_bias, (0, 2, 1)), ("row", "col"))
    bias_all = bias_all.reshape(row_count, col_count, heads, query_tile, tile_rows)
    bias_all = jnp.transpose(bias_all, (2, 1, 3, 0, 4)).reshape(heads, blocks, size, blocks, size)
    bias_t = transposed_bias(jnp.transpose(bias_all, (3, 1, 0, 2, 4)))

    both = jnp.stack([pair_act, out_grad]).reshape(
        2, tile_rows, row_count, chunks, width, chan
    )
    both = jnp.transpose(both, (2, 3, 0, 4, 1, 5))
    targets = [me ^ s if paired else (me + s) % row_count for s in range(row_count)]
    sources = [me ^ s if paired else (me - s) % row_count for s in range(row_count)]
    owners = jnp.stack(sources).astype(jnp.int32)
    w_all = jnp.concatenate([w_query, w_key, w_value, w_gate], axis=1)

    arrived = []
    for c in range(chunks):
        pieces = []
        for s in range(row_count):
            piece = lax.dynamic_index_in_dim(both, targets[s], 0, keepdims=False)[c]
            pieces.append(piece if s == 0 else lax.ppermute(piece, "row", partners[s]))
        arrived.append(pieces)
    carried = None
    returned = []
    for c in range(chunks):
        d_pieces, carried = attention(
            arrived[c], bias_t, w_all, w_out, key_blocks, list_len, owners, carried
        )
        back = []
        for s in range(row_count):
            home = [(t, f) for f, t in partners[s]]
            back.append(d_pieces[s] if s == 0 else lax.ppermute(d_pieces[s], "row", home))
        returned.append(jnp.stack(back))
    slot_bias, w_grad, o_grad = carried

    d_pair = jnp.stack(returned, axis=1)
    steps = jnp.arange(row_count)
    order = me ^ steps if paired else (steps - me) % row_count
    d_pair = jnp.take(d_pair, order, axis=0)
    d_pair = jnp.transpose(d_pair, (3, 0, 1, 2, 4)).reshape(tile_rows, tile_cols, chan)

    match = (key_blocks[:, :, None] == jnp.arange(blocks)[None, None, :]) & (
        jnp.arange(slots)[None, :, None] < list_len[:, None, None]
    )
    slot_form = jnp.transpose(slot_bias, (1, 2, 3, 0, 4)).reshape(slots, heads, size, tokens)
    slot_cols = lax.psum_scatter(
        slot_form.astype(BF16), "col", scatter_dimension=3, tiled=True
    ).astype(F32)
    query_ids = lax.axis_index("col") * query_tile + jnp.arange(query_tile, dtype=jnp.int32)
    hit = match[query_ids // size]
    expanded = jnp.sum(
        jnp.where(jnp.transpose(hit, (2, 1, 0))[:, :, None, None, :], slot_cols[None], 0.0), axis=1
    )
    expanded = jnp.transpose(expanded, (1, 0, 2, 3)).reshape(heads, tokens, query_tile)
    d_bias = lax.psum_scatter(
        expanded.astype(BF16), "row", scatter_dimension=1, tiled=True
    ).astype(F32)
    w_sum, o_sum = lax.psum((w_grad, o_grad), ("row", "col"))
    return (
        d_pair,
        d_bias,
        w_sum[:, :proj],
        w_sum[:, proj : 2 * proj],
        w_sum[:, 2 * proj : 3 * proj],
        w_sum[:, 3 * proj :],
        o_sum,
    )


def solution(mesh):
    in_specs = (
        P("row", "col", None),
        P("row", "col", None),
        P(None, "row", "col"),
        P(),
        P(),
        P(),
        P(),
        P(),
        P(),
        P(),
    )
    out_specs = (P("row", "col", None), P(None, "row", "col"), P(), P(), P(), P(), P())
    return jax.shard_map(
        on_device, mesh=mesh, in_specs=in_specs, out_specs=out_specs, check_vma=False
    )
```

time: 1070 us -> 450 us (0.42); the launches traced: 1060 us -> 455 us
  local copies, waits for them, and re-layouts: 460 us -> 32.4 us
  matrix products: 201 us -> 0 us
  Pallas kernels: 0 us -> 159 us
  other arithmetic: 165 us -> 10.2 us
  waiting for transfers between devices: 167 us -> 208 us
  loops' own time: 34.1 us -> 0 us
  starting transfers between devices: 13.8 us -> 32.2 us
    dot_general x31 -> x0, matrix products: 201 us -> none  [the longest x4 39.2 us: per_block(): jnp.einsum('whiek,ekwhd->iwhd', probs_low, v_sel, preferred_element_type=...]
    pallas_call x0 -> x5, Pallas kernels: none -> 159 us  [the longest x4 154 us: attention(): pl.pallas_call(functools.partial(attention_kernel, dims, first), grid_spe...]
    reshape x9 -> x0, local copies, waits for them, and re-layouts: 99.1 us -> none  [the longest x1 12.9 us: on_device(): gate_act.reshape(block_shape)]
    gather x12 -> x2, local copies, waits for them, and re-layouts: 87.9 us -> 3.21 us  [the longest x1 2.57 us: on_device(): d_pair = jnp.take(d_pair, order, axis=0)]
    select_n x8 -> x0, local copies, waits for them, and re-layouts: 80.1 us -> none  [the longest x4 42.3 us: per_block(): v_sel = jnp.take(value_all, chosen, axis=0)]
    scatter-add x8 -> x0, other arithmetic: 57.9 us -> none  [the longest x4 29 us: per_block(): dv_acc = dv_acc.at[chosen].add(dv_part)]
    select_n x9 -> x3, other arithmetic: 51.6 us -> 0.28 us  [the longest x2 0.27 us: on_device(): d_pair = jnp.take(d_pair, order, axis=0)]
    while x19 -> x0, local copies, waits for them, and re-layouts: 44.6 us -> none  [the longest x3 34 us: on_device(): lax.scan(per_block, start, scan_inputs)]
  transfers between devices with their start and end apart: 7 -> 28, of which waited for: 3 -> 13; matrix products, arithmetic and copies ran while one was open for 19% -> 7% of each run, Pallas kernels for 0% -> 26%
where the time goes in v1:
time: 450 us; the launch traced here: 455 us
  waiting for transfers between devices  208 us (46%)
  Pallas kernels  159 us (35%)
  local copies, waits for them, and re-layouts  32.4 us (7%)
  starting transfers between devices  32.2 us (7%)
  between operations  14.2 us (3%)
  other arithmetic  10.2 us (2%)
    pallas_call x4, Pallas kernels, attention(): pl.pallas_call(functools.partial(attention_kernel, dims, first), grid_spe...  154 us
    psum x1, waiting for transfers between devices, on_device(): w_sum, o_sum = lax.psum((w_grad, o_grad), ('row', 'col'))  125 us
    all_gather x1, waiting for transfers between devices, on_device(): lax.all_gather(jnp.transpose(tri_bias, (0, 2, 1)), ('row', 'col'))  36.2 us
    unnamed x5, waiting for transfers between devices  27 us
    unnamed x73, local copies, waits for them, and re-layouts  18.3 us
    ppermute x12, starting transfers between devices, on_device(): pieces.append(piece if s == 0 else lax.ppermute(piece, 'row', partners[s]))  16.5 us
    ppermute x12, starting transfers between devices, on_device(): lax.ppermute(d_pieces[s], 'row', home)  15.3 us
  transfers between devices with their start and end apart: 28, of which 13 were waited for; matrix products, arithmetic and copies ran while one was open for 7% of the time, Pallas kernels for 26%

profile of v1, /device:TPU:0, one launch (start us, length us, event | category | flops | bytes accessed | tf_op | source)
XLA Modules:
  0.0 455.4 jit_solution(11442106590780749455)
XLA Ops:
  8.0 3.1 copy.95
  11.1 2.7 copy.96
  13.7 1.9 fusion.1
  16.4 2.9 collective-permute-start.12
  20.2 1.5 collective-permute-start.13
  23.0 2.9 collective-permute-start.8
  28.9 1.5 fusion.11
  31.7 1.5 copy.103
  33.2 1.0 slice_bitcast_fusion.15
  34.2 36.2 %all-gather.3.cloned.1.call-done = bf16[128,64,128]{2,1,0:T(8,128)(2,1)} async-done(((bf16[4,64,128]{2,1,0:T(8,128)(2,1)}), bf16[128,64,128]{2,1,0:T(8,128)(2,1)}) %all-gather.3.cloned.1.call-update) | async-done | bytes 2097168 | tf_op jit(solution)/shard_map/all_gather | solution.py:240
  70.4 1.8 copy.97
  72.2 1.5 collective-permute-start.14
  73.8 1.4 collective-permute-start
  75.8 1.5 collective-permute-start.2
  77.3 1.6 copy_bitcast_fusion.bias_ref
  78.8 4.6 %shard_map.153.refs_4_ = f32[4,4,4,128,128]{4,3,2,1,0:T(8,128)} custom-call(bf16[4,4,4,128,128]{4,3,2,1,0:T(8,128)(2,1)} %copy_bitcast_fusion.bias_ref), custom_call_target="tpu_custom_call" | custom-call | tf_op jit(solution)/shard_map/pallas_call | solution.py:28
  83.4 4.6 %collective-permute-done.refs_1_ = bf16[2,4,128,128]{3,2,1,0:T(8,128)(2,1)S(1)} collective-permute-done((bf16[2,4,128,128]{3,2,1,0:T(8,128)(2,1)S(1)}, bf16[2,4,128,128]{3,2,1,0:T(8,128)(2,1)S(1)}, u32[]{:S(2)}, u32[]{:S(2)}) %collective-permute-start) | collective-permute-done | bytes 262176 | tf_op jit(solution)/shard_map/ppermute | solution.py:259
  88.6 1.4 collective-permute-start.19
  90.0 3.7 collective-permute-done.2.refs_3_
  93.6 1.5 collective-permute-start.20
  95.1 37.6 %shard_map.154 = (bf16[4,128,128]{2,1,0:T(8,128)(2,1)}, bf16[4,128,128]{2,1,0:T(8,128)(2,1)}, bf16[4,128,128]{2,1,0:T(8,128)(2,1)}, bf16[4,128,128]{2,1,0:T(8,12...) custom-call(s32[4,3]{1,0:T(4,128)} %tables_ref.7, s32[4]{0:T(128)} %lens_ref.7, ...), custom_call_target="tpu_custom_call" | custom-call | flops 1207959552 | bytes 12058624 | tf_op jit(solution)/shard_map/pallas_call | solution.py:178
  132.8 38.8 %shard_map.155 = (bf16[4,128,128]{2,1,0:T(8,128)(2,1)}, bf16[4,128,128]{2,1,0:T(8,128)(2,1)}, bf16[4,128,128]{2,1,0:T(8,128)(2,1)}, bf16[4,128,128]{2,1,0:T(8,12...) custom-call(s32[4,3]{1,0:T(4,128)} %tables_ref.7, s32[4]{0:T(128)} %lens_ref.7, ...), custom_call_target="tpu_custom_call" | custom-call | flops 1207959552 | bytes 12058624 | tf_op jit(solution)/shard_map/pallas_call | solution.py:178
  172.3 38.9 %shard_map.156 = (bf16[4,128,128]{2,1,0:T(8,128)(2,1)}, bf16[4,128,128]{2,1,0:T(8,128)(2,1)}, bf16[4,128,128]{2,1,0:T(8,128)(2,1)}, bf16[4,128,128]{2,1,0:T(8,12...) custom-call(s32[4,3]{1,0:T(4,128)} %tables_ref.7, s32[4]{0:T(128)} %lens_ref.7, ...), custom_call_target="tpu_custom_call" | custom-call | flops 1207959552 | bytes 12058624 | tf_op jit(solution)/shard_map/pallas_call | solution.py:178
  212.1 38.7 %shard_map.157 = (bf16[4,128,128]{2,1,0:T(8,128)(2,1)}, bf16[4,128,128]{2,1,0:T(8,128)(2,1)}, bf16[4,128,128]{2,1,0:T(8,128)(2,1)}, bf16[4,128,128]{2,1,0:T(8,12...) custom-call(s32[4,3]{1,0:T(4,128)} %tables_ref.7, s32[4]{0:T(128)} %lens_ref.7, ...), custom_call_target="tpu_custom_call" | custom-call | flops 1207959552 | bytes 12058624 | tf_op jit(solution)/shard_map/pallas_call | solution.py:178
  250.8 2.1 convert_bitcast_fusion
  253.1 1.6 copy.109
  255.0 1.5 collective-permute-start.23
  256.5 1.4 collective-permute-start.22
  258.6 1.5 collective-permute-start.17
  260.1 1.5 collective-permute-start.16
  262.3 1.5 collective-permute-start.15
  263.8 2.0 collective-permute-done.22
  265.8 1.4 collective-permute-start.11
  268.4 1.5 collective-permute-start.10
  271.4 1.4 collective-permute-start.5
  272.8 1.4 collective-permute-start.4
  275.2 1.8 collective-permute-done.10
  277.0 1.4 collective-permute-done.5
  278.4 1.0 collective-permute-done.4
  279.8 1.6 pad_maximum_fusion
  281.4 2.6 gather_fusion
  283.9 3.8 reduce-scatter.5.cloned.1.call-done
  289.2 1.0 reshape.195
  290.5 2.7 copy.111
  293.2 124.5 %all-reduce.3.cloned.1.call-done = (f32[128,512]{1,0:T(8,128)}, f32[128,128]{1,0:T(8,128)}) async-done(((f32[128,512]{1,0:T(8,128)}, f32[128,128]{1,0:T(8,128)}), (f32[128,512]{1,0:T(8,128)}, f32[128,128]{1,0:T(8,128)})) %all-reduce.3.cloned.1.call-update) | async-done | bytes 327696 | tf_op jit(solution)/shard_map/psum | solution.py:296
  417.7 1.6 fusion.12
  419.4 26.3 %reduce-scatter.7.cloned.1.call-done = bf16[128,256]{1,0:T(8,128)(2,1)} async-done(((bf16[512,256]{1,0:T(8,128)(2,1)}), bf16[128,256]{1,0:T(8,128)(2,1)}) %reduce-scatter.7.cloned.1.call-update) | async-done | bytes 65552
  447.4 1.5 copy.119
  (122 shorter events, 19.7 us)
Async XLA Ops:
  7.2 63.2 %all-gather.3.cloned.1.call-start = ((), (), s32[]{:S(2)}) async-start(), calls=%async_computation.3 | async-start | bytes 2162688 | tf_op jit(solution)/shard_map/all_gather | solution.py:240
  7.9 279.8 %reduce-scatter.5.cloned.1.call-start = ((), (), s32[]{:S(2)}) async-start(), calls=%async_computation.2 | async-start | bytes 1769472 | tf_op jit(solution)/shard_map/reduce_scatter | solution.py:284
  16.4 55.8 %collective-permute-start.12 = (bf16[2,4,128,128]{3,2,1,0:T(8,128)(2,1)}, bf16[2,4,128,128]{3,2,1,0:T(8,128)(2,1)}, u32[]{:S(2)}, u32[]{:S(2)}) collective-permute-start(bf16[2,4,128,128]{3,2,1,0:T(8,128)(2,1)} %get-tuple-element.121), channel_id=1, source_target_pairs={{0,8},{8,0},{16,24},{24,16},{1,9},{9,1},{17,25},{25,17},{2,10},{10... | collective-permute-start | bytes 786440 | tf_op jit(solution)/shard_map/ppermute | solution.py:259
  19.4 6.6 %copy-start.9 = (bf16[128,128]{1,0:T(8,128)(2,1)S(1)}, bf16[128,128]{1,0:T(8,128)(2,1)}, u32[]{:S(2)}) copy-start(bf16[128,128]{1,0:T(8,128)(2,1)} %param.16) | copy-start | bytes 98308
  19.4 7.3 %copy-start.10 = (bf16[128,128]{1,0:T(8,128)(2,1)S(1)}, bf16[128,128]{1,0:T(8,128)(2,1)}, u32[]{:S(2)}) copy-start(bf16[128,128]{1,0:T(8,128)(2,1)} %param.15) | copy-start | bytes 98308
  19.4 8.0 %copy-start.11 = (bf16[128,128]{1,0:T(8,128)(2,1)S(1)}, bf16[128,128]{1,0:T(8,128)(2,1)}, u32[]{:S(2)}) copy-start(bf16[128,128]{1,0:T(8,128)(2,1)} %param.14) | copy-start | bytes 98308
  19.4 8.8 %copy-start.12 = (bf16[128,128]{1,0:T(8,128)(2,1)S(1)}, bf16[128,128]{1,0:T(8,128)(2,1)}, u32[]{:S(2)}) copy-start(bf16[128,128]{1,0:T(8,128)(2,1)} %param.13) | copy-start | bytes 98308
  20.2 151.4 %collective-permute-start.13 = (bf16[2,4,128,128]{3,2,1,0:T(8,128)(2,1)S(1)}, bf16[2,4,128,128]{3,2,1,0:T(8,128)(2,1)}, u32[]{:S(2)}, u32[]{:S(2)}) collective-permute-start(bf16[2,4,128,128]{3,2,1,0:T(8,128)(2,1)S(1)} %get-tuple-element.117), channel_id=1, source_target_pairs={{0,16},{8,24},{16,0},{24,8},{1,17},{9,25},{17,1},{25,9},{2,18},{10... | collective-permute-start | bytes 786440 | tf_op jit(solution)/shard_map/ppermute | solution.py:259
  21.7 52.1 %collective-permute-start.6 = (bf16[2,4,128,128]{3,2,1,0:T(8,128)(2,1)S(1)}, bf16[2,4,128,128]{3,2,1,0:T(8,128)(2,1)}, u32[]{:S(2)}, u32[]{:S(2)}) collective-permute-start(bf16[2,4,128,128]{3,2,1,0:T(8,128)(2,1)S(1)} %get-tuple-element.122), channel_id=1, source_target_pairs={{0,8},{8,0},{16,24},{24,16},{1,9},{9,1},{17,25},{25,17},{2,10},{10... | collective-permute-start | bytes 786440 | tf_op jit(solution)/shard_map/ppermute | solution.py:259
  22.2 53.0 %collective-permute-start.7 = (bf16[2,4,128,128]{3,2,1,0:T(8,128)(2,1)}, bf16[2,4,128,128]{3,2,1,0:T(8,128)(2,1)}, u32[]{:S(2)}, u32[]{:S(2)}) collective-permute-start(bf16[2,4,128,128]{3,2,1,0:T(8,128)(2,1)} %get-tuple-element.118), channel_id=1, source_target_pairs={{0,16},{8,24},{16,0},{24,8},{1,17},{9,25},{17,1},{25,9},{2,18},{10... | collective-permute-start | bytes 786440 | tf_op jit(solution)/shard_map/ppermute | solution.py:259
  23.0 52.8 %collective-permute-start.8 = (bf16[2,4,128,128]{3,2,1,0:T(8,128)(2,1)}, bf16[2,4,128,128]{3,2,1,0:T(8,128)(2,1)}, u32[]{:S(2)}, u32[]{:S(2)}) collective-permute-start(bf16[2,4,128,128]{3,2,1,0:T(8,128)(2,1)} %get-tuple-element.114), channel_id=1, source_target_pairs={{0,24},{8,16},{16,8},{24,0},{1,25},{9,17},{17,9},{25,1},{2,26},{10... | collective-permute-start | bytes 786440 | tf_op jit(solution)/shard_map/ppermute | solution.py:259
  72.2 99.3 %collective-permute-start.14 = (bf16[2,4,128,128]{3,2,1,0:T(8,128)(2,1)S(1)}, bf16[2,4,128,128]{3,2,1,0:T(8,128)(2,1)S(1)}, u32[]{:S(2)}, u32[]{:S(2)}) collective-permute-start(bf16[2,4,128,128]{3,2,1,0:T(8,128)(2,1)S(1)} %get-tuple-element.113), channel_id=1, source_target_pairs={{0,24},{8,16},{16,8},{24,0},{1,25},{9,17},{17,9},{25,1},{2,26},{10... | collective-permute-start | bytes 786440 | tf_op jit(solution)/shard_map/ppermute | solution.py:259
  73.8 14.2 %collective-permute-start = (bf16[2,4,128,128]{3,2,1,0:T(8,128)(2,1)S(1)}, bf16[2,4,128,128]{3,2,1,0:T(8,128)(2,1)S(1)}, u32[]{:S(2)}, u32[]{:S(2)}) collective-permute-start(bf16[2,4,128,128]{3,2,1,0:T(8,128)(2,1)S(1)} %get-tuple-element.119), channel_id=1, source_target_pairs={{0,8},{8,0},{16,24},{24,16},{1,9},{9,1},{17,25},{25,17},{2,10},{10... | collective-permute-start | bytes 786440 | tf_op jit(solution)/shard_map/ppermute | solution.py:259
  75.2 13.3 %collective-permute-start.1 = (bf16[2,4,128,128]{3,2,1,0:T(8,128)(2,1)S(1)}, bf16[2,4,128,128]{3,2,1,0:T(8,128)(2,1)S(1)}, u32[]{:S(2)}, u32[]{:S(2)}) collective-permute-start(bf16[2,4,128,128]{3,2,1,0:T(8,128)(2,1)S(1)} %get-tuple-element.115), channel_id=1, source_target_pairs={{0,16},{8,24},{16,0},{24,8},{1,17},{9,25},{17,1},{25,9},{2,18},{10... | collective-permute-start | bytes 786440 | tf_op jit(solution)/shard_map/ppermute | solution.py:259
  75.8 17.9 %collective-permute-start.2 = (bf16[2,4,128,128]{3,2,1,0:T(8,128)(2,1)S(1)}, bf16[2,4,128,128]{3,2,1,0:T(8,128)(2,1)S(1)}, u32[]{:S(2)}, u32[]{:S(2)}) collective-permute-start(bf16[2,4,128,128]{3,2,1,0:T(8,128)(2,1)S(1)} %get-tuple-element.111), channel_id=1, source_target_pairs={{0,24},{8,16},{16,8},{24,0},{1,25},{9,17},{17,9},{25,1},{2,26},{10... | collective-permute-start | bytes 786440 | tf_op jit(solution)/shard_map/ppermute | solution.py:259
  88.0 7.1 %copy-start.15 = (bf16[2,4,128,128]{3,2,1,0:T(8,128)(2,1)}, bf16[2,4,128,128]{3,2,1,0:T(8,128)(2,1)S(1)}, u32[]{:S(2)}) copy-start(bf16[2,4,128,128]{3,2,1,0:T(8,128)(2,1)S(1)} %collective-permute-done.refs_1_) | copy-start | bytes 786436
  88.0 123.2 %collective-permute-start.18 = (bf16[2,4,128,128]{3,2,1,0:T(8,128)(2,1)S(1)}, bf16[2,4,128,128]{3,2,1,0:T(8,128)(2,1)S(1)}, u32[]{:S(2)}, u32[]{:S(2)}) collective-permute-start(bf16[2,4,128,128]{3,2,1,0:T(8,128)(2,1)S(1)} %get-tuple-element.120), channel_id=1, source_target_pairs={{0,8},{8,0},{16,24},{24,16},{1,9},{9,1},{17,25},{25,17},{2,10},{10... | collective-permute-start | bytes 786440 | tf_op jit(solution)/shard_map/ppermute | solution.py:259
  88.6 6.6 %copy-start.16 = (bf16[2,4,128,128]{3,2,1,0:T(8,128)(2,1)}, bf16[2,4,128,128]{3,2,1,0:T(8,128)(2,1)S(1)}, u32[]{:S(2)}) copy-start(bf16[2,4,128,128]{3,2,1,0:T(8,128)(2,1)S(1)} %collective-permute-done.1.refs_2_) | copy-start | bytes 786436
  88.6 122.7 %collective-permute-start.19 = (bf16[2,4,128,128]{3,2,1,0:T(8,128)(2,1)S(1)}, bf16[2,4,128,128]{3,2,1,0:T(8,128)(2,1)S(1)}, u32[]{:S(2)}, u32[]{:S(2)}) collective-permute-start(bf16[2,4,128,128]{3,2,1,0:T(8,128)(2,1)S(1)} %get-tuple-element.116), channel_id=1, source_target_pairs={{0,16},{8,24},{16,0},{24,8},{1,17},{9,25},{17,1},{25,9},{2,18},{10... | collective-permute-start | bytes 786440 | tf_op jit(solution)/shard_map/ppermute | solution.py:259
  93.6 117.6 %collective-permute-start.20 = (bf16[2,4,128,128]{3,2,1,0:T(8,128)(2,1)S(1)}, bf16[2,4,128,128]{3,2,1,0:T(8,128)(2,1)S(1)}, u32[]{:S(2)}, u32[]{:S(2)}) collective-permute-start(bf16[2,4,128,128]{3,2,1,0:T(8,128)(2,1)S(1)} %get-tuple-element.112), channel_id=1, source_target_pairs={{0,24},{8,16},{16,8},{24,0},{1,25},{9,17},{17,9},{25,1},{2,26},{10... | collective-permute-start | bytes 786440 | tf_op jit(solution)/shard_map/ppermute | solution.py:259
  253.0 5.0 %copy-start.27 = (bf16[4,128,128]{2,1,0:T(8,128)(2,1)S(1)}, bf16[4,128,128]{2,1,0:T(8,128)(2,1)}, u32[]{:S(2)}) copy-start(bf16[4,128,128]{2,1,0:T(8,128)(2,1)} %get-tuple-element.57) | copy-start | bytes 393220
  253.0 5.6 %copy-start.26 = (bf16[4,128,128]{2,1,0:T(8,128)(2,1)S(1)}, bf16[4,128,128]{2,1,0:T(8,128)(2,1)}, u32[]{:S(2)}) copy-start(bf16[4,128,128]{2,1,0:T(8,128)(2,1)} %get-tuple-element.52) | copy-start | bytes 393220
  253.0 7.1 %copy-start.25 = (bf16[4,128,128]{2,1,0:T(8,128)(2,1)S(1)}, bf16[4,128,128]{2,1,0:T(8,128)(2,1)}, u32[]{:S(2)}) copy-start(bf16[4,128,128]{2,1,0:T(8,128)(2,1)} %get-tuple-element.51) | copy-start | bytes 393220
  253.0 9.3 %copy-start.24 = (bf16[4,128,128]{2,1,0:T(8,128)(2,1)S(1)}, bf16[4,128,128]{2,1,0:T(8,128)(2,1)}, u32[]{:S(2)}) copy-start(bf16[4,128,128]{2,1,0:T(8,128)(2,1)} %get-tuple-element.50) | copy-start | bytes 393220
  253.0 12.8 %copy-start.23 = (bf16[4,128,128]{2,1,0:T(8,128)(2,1)S(1)}, bf16[4,128,128]{2,1,0:T(8,128)(2,1)}, u32[]{:S(2)}) copy-start(bf16[4,128,128]{2,1,0:T(8,128)(2,1)} %get-tuple-element.45) | copy-start | bytes 393220
  253.0 15.3 %copy-start.22 = (bf16[4,128,128]{2,1,0:T(8,128)(2,1)S(1)}, bf16[4,128,128]{2,1,0:T(8,128)(2,1)}, u32[]{:S(2)}) copy-start(bf16[4,128,128]{2,1,0:T(8,128)(2,1)} %get-tuple-element.44) | copy-start | bytes 393220
  253.0 16.8 %copy-start.21 = (bf16[4,128,128]{2,1,0:T(8,128)(2,1)S(1)}, bf16[4,128,128]{2,1,0:T(8,128)(2,1)}, u32[]{:S(2)}) copy-start(bf16[4,128,128]{2,1,0:T(8,128)(2,1)} %get-tuple-element.43) | copy-start | bytes 393220
  253.1 17.4 %copy-start.8 = (bf16[4,128,128]{2,1,0:T(8,128)(2,1)S(1)}, bf16[4,128,128]{2,1,0:T(8,128)(2,1)}, u32[]{:S(2)}) copy-start(bf16[4,128,128]{2,1,0:T(8,128)(2,1)} %get-tuple-element.56) | copy-start | bytes 393220
  254.7 16.7 %copy-start.20 = (bf16[4,128,128]{2,1,0:T(8,128)(2,1)S(1)}, bf16[4,128,128]{2,1,0:T(8,128)(2,1)}, u32[]{:S(2)}) copy-start(bf16[4,128,128]{2,1,0:T(8,128)(2,1)} %get-tuple-element.38) | copy-start | bytes 393220
  254.7 18.2 %copy-start.19 = (bf16[4,128,128]{2,1,0:T(8,128)(2,1)S(1)}, bf16[4,128,128]{2,1,0:T(8,128)(2,1)}, u32[]{:S(2)}) copy-start(bf16[4,128,128]{2,1,0:T(8,128)(2,1)} %get-tuple-element.37) | copy-start | bytes 393220
  254.7 19.6 %copy-start.18 = (bf16[4,128,128]{2,1,0:T(8,128)(2,1)S(1)}, bf16[4,128,128]{2,1,0:T(8,128)(2,1)}, u32[]{:S(2)}) copy-start(bf16[4,128,128]{2,1,0:T(8,128)(2,1)} %get-tuple-element.36) | copy-start | bytes 393220
  254.7 20.5 %copy-start.7 = (bf16[4,128,128]{2,1,0:T(8,128)(2,1)S(1)}, bf16[4,128,128]{2,1,0:T(8,128)(2,1)}, u32[]{:S(2)}) copy-start(bf16[4,128,128]{2,1,0:T(8,128)(2,1)} %get-tuple-element.49) | copy-start | bytes 393220
  254.7 22.3 %copy-start.6 = (bf16[4,128,128]{2,1,0:T(8,128)(2,1)S(1)}, bf16[4,128,128]{2,1,0:T(8,128)(2,1)}, u32[]{:S(2)}) copy-start(bf16[4,128,128]{2,1,0:T(8,128)(2,1)} %get-tuple-element.42) | copy-start | bytes 393220
  254.7 25.0 %copy-start.5 = (bf16[4,128,128]{2,1,0:T(8,128)(2,1)S(1)}, bf16[4,128,128]{2,1,0:T(8,128)(2,1)}, u32[]{:S(2)}) copy-start(bf16[4,128,128]{2,1,0:T(8,128)(2,1)} %get-tuple-element.35) | copy-start | bytes 393220
  254.7 163.0 %all-reduce.3.cloned.1.call-start = ((), (), s32[]{:S(2)}) async-start(), calls=%async_computation.5 | async-start | bytes 655360 | tf_op jit(solution)/shard_map/psum | solution.py:296
  255.0 7.4 %collective-permute-start.23 = (bf16[4,128,128]{2,1,0:T(8,128)(2,1)S(1)}, bf16[4,128,128]{2,1,0:T(8,128)(2,1)S(1)}, u32[]{:S(2)}, u32[]{:S(2)}) collective-permute-start(bf16[4,128,128]{2,1,0:T(8,128)(2,1)S(1)} %copy-done.29), channel_id=1, source_target_pairs={{24,0},{16,8},{8,16},{0,24},{25,1},{17,9},{9,17},{1,25},{26,2},{18... | collective-permute-start | bytes 393224 | tf_op jit(solution)/shard_map/ppermute | solution.py:270
  256.5 9.3 %collective-permute-start.22 = (bf16[4,128,128]{2,1,0:T(8,128)(2,1)S(1)}, bf16[4,128,128]{2,1,0:T(8,128)(2,1)S(1)}, u32[]{:S(2)}, u32[]{:S(2)}) collective-permute-start(bf16[4,128,128]{2,1,0:T(8,128)(2,1)S(1)} %copy-done.28), channel_id=1, source_target_pairs={{16,0},{24,8},{0,16},{8,24},{17,1},{25,9},{1,17},{9,25},{18,2},{26... | collective-permute-start | bytes 393224 | tf_op jit(solution)/shard_map/ppermute | solution.py:270
  258.0 10.4 %collective-permute-start.21 = (bf16[4,128,128]{2,1,0:T(8,128)(2,1)S(1)}, bf16[4,128,128]{2,1,0:T(8,128)(2,1)S(1)}, u32[]{:S(2)}, u32[]{:S(2)}) collective-permute-start(bf16[4,128,128]{2,1,0:T(8,128)(2,1)S(1)} %copy-done.27), channel_id=1, source_target_pairs={{8,0},{0,8},{24,16},{16,24},{9,1},{1,9},{25,17},{17,25},{10,2},{2,... | collective-permute-start | bytes 393224 | tf_op jit(solution)/shard_map/ppermute | solution.py:270
  258.6 11.3 %collective-permute-start.17 = (bf16[4,128,128]{2,1,0:T(8,128)(2,1)S(1)}, bf16[4,128,128]{2,1,0:T(8,128)(2,1)S(1)}, u32[]{:S(2)}, u32[]{:S(2)}) collective-permute-start(bf16[4,128,128]{2,1,0:T(8,128)(2,1)S(1)} %copy-done.26), channel_id=1, source_target_pairs={{24,0},{16,8},{8,16},{0,24},{25,1},{17,9},{9,17},{1,25},{26,2},{18... | collective-permute-start | bytes 393224 | tf_op jit(solution)/shard_map/ppermute | solution.py:270
  260.1 11.3 %collective-permute-start.16 = (bf16[4,128,128]{2,1,0:T(8,128)(2,1)S(1)}, bf16[4,128,128]{2,1,0:T(8,128)(2,1)S(1)}, u32[]{:S(2)}, u32[]{:S(2)}) collective-permute-start(bf16[4,128,128]{2,1,0:T(8,128)(2,1)S(1)} %copy-done.25), channel_id=1, source_target_pairs={{16,0},{24,8},{0,16},{8,24},{17,1},{25,9},{1,17},{9,25},{18,2},{26... | collective-permute-start | bytes 393224 | tf_op jit(solution)/shard_map/ppermute | solution.py:270
  262.3 10.5 %collective-permute-start.15 = (bf16[4,128,128]{2,1,0:T(8,128)(2,1)S(1)}, bf16[4,128,128]{2,1,0:T(8,128)(2,1)S(1)}, u32[]{:S(2)}, u32[]{:S(2)}) collective-permute-start(bf16[4,128,128]{2,1,0:T(8,128)(2,1)S(1)} %copy-done.24), channel_id=1, source_target_pairs={{8,0},{0,8},{24,16},{16,24},{9,1},{1,9},{25,17},{17,25},{10,2},{2,... | collective-permute-start | bytes 393224 | tf_op jit(solution)/shard_map/ppermute | solution.py:270
  265.8 8.4 %collective-permute-start.11 = (bf16[4,128,128]{2,1,0:T(8,128)(2,1)S(1)}, bf16[4,128,128]{2,1,0:T(8,128)(2,1)S(1)}, u32[]{:S(2)}, u32[]{:S(2)}) collective-permute-start(bf16[4,128,128]{2,1,0:T(8,128)(2,1)S(1)} %copy-done.23), channel_id=1, source_target_pairs={{24,0},{16,8},{8,16},{0,24},{25,1},{17,9},{9,17},{1,25},{26,2},{18... | collective-permute-start | bytes 393224 | tf_op jit(solution)/shard_map/ppermute | solution.py:270
  268.1 177.6 %reduce-scatter.7.cloned.1.call-start = ((), (), s32[]{:S(2)}) async-start(), calls=%async_computation.4 | async-start | bytes 327680
  268.4 8.6 %collective-permute-start.10 = (bf16[4,128,128]{2,1,0:T(8,128)(2,1)S(1)}, bf16[4,128,128]{2,1,0:T(8,128)(2,1)S(1)}, u32[]{:S(2)}, u32[]{:S(2)}) collective-permute-start(bf16[4,128,128]{2,1,0:T(8,128)(2,1)S(1)} %copy-done.22), channel_id=1, source_target_pairs={{16,0},{24,8},{0,16},{8,24},{17,1},{25,9},{1,17},{9,25},{18,2},{26... | collective-permute-start | bytes 393224 | tf_op jit(solution)/shard_map/ppermute | solution.py:270
  269.9 7.1 %collective-permute-start.9 = (bf16[4,128,128]{2,1,0:T(8,128)(2,1)S(1)}, bf16[4,128,128]{2,1,0:T(8,128)(2,1)S(1)}, u32[]{:S(2)}, u32[]{:S(2)}) collective-permute-start(bf16[4,128,128]{2,1,0:T(8,128)(2,1)S(1)} %copy-done.21), channel_id=1, source_target_pairs={{8,0},{0,8},{24,16},{16,24},{9,1},{1,9},{25,17},{17,25},{10,2},{2,... | collective-permute-start | bytes 393224 | tf_op jit(solution)/shard_map/ppermute | solution.py:270
  271.4 7.1 %collective-permute-start.5 = (bf16[4,128,128]{2,1,0:T(8,128)(2,1)S(1)}, bf16[4,128,128]{2,1,0:T(8,128)(2,1)S(1)}, u32[]{:S(2)}, u32[]{:S(2)}) collective-permute-start(bf16[4,128,128]{2,1,0:T(8,128)(2,1)S(1)} %copy-done.20), channel_id=1, source_target_pairs={{24,0},{16,8},{8,16},{0,24},{25,1},{17,9},{9,17},{1,25},{26,2},{18... | collective-permute-start | bytes 393224 | tf_op jit(solution)/shard_map/ppermute | solution.py:270
  272.8 6.7 %collective-permute-start.4 = (bf16[4,128,128]{2,1,0:T(8,128)(2,1)S(1)}, bf16[4,128,128]{2,1,0:T(8,128)(2,1)S(1)}, u32[]{:S(2)}, u32[]{:S(2)}) collective-permute-start(bf16[4,128,128]{2,1,0:T(8,128)(2,1)S(1)} %copy-done.19), channel_id=1, source_target_pairs={{16,0},{24,8},{0,16},{8,24},{17,1},{25,9},{1,17},{9,25},{18,2},{26... | collective-permute-start | bytes 393224 | tf_op jit(solution)/shard_map/ppermute | solution.py:270
  274.3 5.5 %collective-permute-start.3 = (bf16[4,128,128]{2,1,0:T(8,128)(2,1)S(1)}, bf16[4,128,128]{2,1,0:T(8,128)(2,1)S(1)}, u32[]{:S(2)}, u32[]{:S(2)}) collective-permute-start(bf16[4,128,128]{2,1,0:T(8,128)(2,1)S(1)} %copy-done.18), channel_id=1, source_target_pairs={{8,0},{0,8},{24,16},{16,24},{9,1},{1,9},{25,17},{17,25},{10,2},{2,... | collective-permute-start | bytes 393224 | tf_op jit(solution)/shard_map/ppermute | solution.py:270
  (10 other events, 16.9 us)
Sparse Core Ops, SparseCore 0:
  11.0 59.3 all-gather.2
  254.8 32.8 reduce-scatter.4
  293.7 124.0 all-reduce.2
  420.6 25.0 reduce-scatter.6

commit v2 on v0

v2 whole, which is shorter than its diff:
```python
import functools
import math

import jax
import jax.numpy as jnp
from jax import lax
from jax.experimental import pallas as pl
from jax.experimental.pallas import tpu as pltpu
from jax.sharding import PartitionSpec as P

F32 = jnp.float32
BF16 = jnp.bfloat16
CHUNKS = 2
TOGETHER = 2
STRIP = 32
LOG2E = math.log2(math.e)
SAFE_SCORE = 30.0
VMEM_LIMIT = 56 * 1024 * 1024


def dot(a, b):
    return jnp.dot(a, b, preferred_element_type=F32)


def bias_kernel(tables_ref, lens_ref, col_pos_ref, row_pos_ref, *refs):
    *parts, out_ref = refs
    b = pl.program_id(0)
    blocks, _, heads, size, _ = out_ref.shape
    slots = tables_ref.shape[1]
    rows, _, _, tile = parts[0].shape[1:]
    per_block = size // tile
    for h in range(heads):
        for r in range(rows):
            piece = jnp.concatenate([p[0, row_pos_ref[r], h] for p in parts], axis=0)
            at = (r % per_block) * tile
            out_ref[r // per_block, 0, h, at : at + tile, :] = piece.astype(F32).T
    for h in range(heads):
        peak = jnp.max(out_ref[tables_ref[b, 0], 0, h], axis=0, keepdims=True)
        for e in range(1, slots):
            other = jnp.max(out_ref[tables_ref[b, e], 0, h], axis=0, keepdims=True)
            peak = jnp.where(e < lens_ref[b], jnp.maximum(peak, other), peak)
        for kb in range(blocks):
            out_ref[kb, 0, h] = (out_ref[kb, 0, h] - peak) * LOG2E


def shifted_bias(gathered, key_blocks, list_len, col_pos, row_pos):
    cols, rows, heads, query_tile, key_tile = gathered.shape
    blocks = key_blocks.shape[0]
    size = cols * query_tile // blocks
    per_block = size // query_tile

    def part(sub):
        return pl.BlockSpec(
            (1, rows, heads, query_tile, key_tile),
            lambda b, tables, lens, col_at, row_at: (col_at[b * per_block + sub], 0, 0, 0, 0),
        )

    return pl.pallas_call(
        bias_kernel,
        grid_spec=pltpu.PrefetchScalarGridSpec(
            num_scalar_prefetch=4,
            grid=(blocks,),
            in_specs=[part(sub) for sub in range(per_block)],
            out_specs=pl.BlockSpec((blocks, 1, heads, size, size), lambda b, *_: (0, b, 0, 0, 0)),
        ),
        out_shape=jax.ShapeDtypeStruct((blocks, blocks, heads, size, size), F32),
        compiler_params=pltpu.CompilerParams(vmem_limit_bytes=VMEM_LIMIT),
    )(key_blocks, list_len, col_pos, row_pos, *([gathered] * per_block))


def attention_kernel(dims, first, last, tables_ref, lens_ref, owners_ref, *refs):
    pieces, heads, head_dim, blocks, size, slots, together = dims
    refs = list(refs)
    take = lambda n: [refs.pop(0) for _ in range(n)]
    inputs = take(pieces)
    bias_ref, w_all_ref, w_all_t_ref, w_out_ref = take(4)
    carried = [] if first else take(4)
    d_pair_out = take(pieces)
    if last:
        d_bias_out, d_w_out = take(2)
    else:
        sums_out = take(4)
    d_bias_s, dw_qg_s, dw_kv_s, dwo_s = sums = take(4) if last else sums_out
    (act_s, grad_s, act_t_s, kv_s, kv_t_s, joint_s, d_att_s, query_s, gate_t_s, d_gated_t_s,
     score_s, probs_s, ds_s, d_kv_s, att_t_s, d_query_t_s, d_pair_s) = refs
    proj = heads * head_dim
    scale = head_dim ** (-0.5)
    tile_rows = inputs[0].shape[2]
    span = [slice(b * size, (b + 1) * size) for b in range(blocks)]
    own = [slice(h * head_dim, (h + 1) * head_dim) for h in range(heads)]
    low = [slice(proj + h * head_dim, proj + (h + 1) * head_dim) for h in range(heads)]

    @pl.when(pl.program_id(0) == 0)
    def _():
        joint_s[...] = jnp.zeros_like(joint_s)
        for n, ref in enumerate(sums):
            ref[...] = jnp.zeros_like(ref) if first else carried[n][...]

    lane_head = lax.broadcasted_iota(jnp.int32, (size, proj), 1) // head_dim
    bound = jnp.float32(0.0)
    for c in range(together):
        for s in range(pieces):
            rows = pl.ds(pl.multiple_of(owners_ref[s] * tile_rows, tile_rows), tile_rows)
            act_s[c, rows, :] = inputs[s][0, c]
            grad_s[c, rows, :] = inputs[s][1, c]
        acts = act_s[c]
        acts_t = acts.T
        act_t_s[c] = acts_t
        natural = dot(acts, w_all_ref[:, : 3 * proj])
        across = dot(w_all_t_ref[...], acts_t)
        queries_t = (across[:proj] * scale).astype(BF16)
        kv_t = across[proj : 3 * proj].astype(BF16)
        gate_t = 1.0 / (1.0 + jnp.exp(-across[3 * proj :]))
        d_gated_t = dot(w_out_ref[...], grad_s[c].T)
        d_att_t = (d_gated_t * gate_t).astype(BF16)
        gate_t_s[c] = gate_t
        d_gated_t_s[c] = d_gated_t
        squares = lambda x: jnp.max(
            jnp.sum(jnp.square(x.astype(F32)).reshape(heads, head_dim, -1), axis=1)
        )
        bound = jnp.maximum(bound, squares(queries_t) * squares(kv_t[:proj]))
        queries = (natural[:, :proj] * scale).astype(BF16)
        kv = natural[:, proj:].astype(BF16)
        zero = jnp.zeros((size, proj), BF16)
        for b in range(blocks):
            kv_s[c, b] = kv[span[b]]
            kv_t_s[c, b] = kv_t[:, span[b]]
            d_att = d_att_t[:, span[b]].T
            for h in range(heads):
                joint_s[c, b, h, own[h], :size] = queries_t[own[h], span[b]]
                joint_s[c, b, h, low[h], size:] = d_att_t[own[h], span[b]]
                here = lane_head == h
                query_s[c, b, h * size : (h + 1) * size, :] = jnp.where(here, queries[span[b]], zero)
                d_att_s[c, b, h * size : (h + 1) * size, :] = jnp.where(here, d_att, zero)
    d_kv_s[...] = jnp.zeros_like(d_kv_s)

    def query_block(b, live, shift):
        chosen = [tables_ref[b, e] for e in range(live)]
        strips = [
            (e, e * size + at, at) for e in range(live) for at in range(0, size, STRIP)
        ]
        rows_of = lambda x: jnp.sum(x.reshape(-1, 8, size), axis=0)
        for c in range(together):
            kv = jnp.concatenate([kv_s[c, k] for k in chosen], axis=0)
            for h in range(heads):
                score_s[c, h, : live * size, :] = dot(kv, joint_s[c, b, h])
        for h in range(heads):
            stats = []
            for c in range(together):
                def scores(e, row, at):
                    return (
                        score_s[c, h, row : row + STRIP, :size] * LOG2E
                        + bias_ref[chosen[e], b, h, at : at + STRIP, :]
                    )

                if shift:
                    peak = jnp.full((8, size), -jnp.inf, F32)
                    for strip in strips:
                        peak = jnp.maximum(
                            peak, jnp.max(scores(*strip).reshape(-1, 8, size), axis=0)
                        )
                    peak = jnp.max(peak, axis=0, keepdims=True)
                total = jnp.zeros((8, size), F32)
                mixed = jnp.zeros((8, size), F32)
                for e, row, at in strips:
                    value = scores(e, row, at)
                    weight = jnp.exp2(value - peak if shift else value)
                    total += rows_of(weight)
                    mixed += rows_of(weight * score_s[c, h, row : row + STRIP, size:])
                    score_s[c, h, row : row + STRIP, :size] = weight
                norm = 1.0 / jnp.sum(total, axis=0, keepdims=True)
                stats.append((norm, jnp.sum(mixed, axis=0, keepdims=True) * norm))
            lanes = slice(h * size, (h + 1) * size)
            for e, row, at in strips:
                part = slice(row, row + STRIP)
                gathered = d_bias_s[b, e, h, at : at + STRIP, :]
                for c, (norm, delta) in enumerate(stats):
                    probs = score_s[c, h, part, :size] * norm
                    d_scores = probs * (score_s[c, h, part, size:] - delta)
                    probs_s[c, part, lanes] = probs.astype(BF16)
                    ds_s[c, part, lanes] = d_scores.astype(BF16)
                    gathered += d_scores
                d_bias_s[b, e, h, at : at + STRIP, :] = gathered
        for c in range(together):
            probs = probs_s[c, : live * size, :]
            ds = ds_s[c, : live * size, :]
            kv_t = jnp.concatenate([kv_t_s[c, k] for k in chosen], axis=1)
            for h in range(heads):
                lanes = slice(h * size, (h + 1) * size)
                att_t_s[c, b, own[h], :] = dot(kv_t[low[h]], probs[:, lanes])
                d_query_t_s[c, b, own[h], :] = dot(kv_t[own[h]], ds[:, lanes])
            d_values = dot(probs, d_att_s[c, b])
            d_keys = dot(ds, query_s[c, b])
            for e in range(live):
                part = slice(e * size, (e + 1) * size)
                d_kv_s[c, chosen[e], :, :proj] += d_keys[part]
                d_kv_s[c, chosen[e], :, proj:] += d_values[part]

    def all_blocks(shift):
        @pl.loop(0, blocks)
        def _(b):
            for live in range(1, slots + 1):

                @pl.when(lens_ref[b] == live)
                def _():
                    query_block(b, live, shift)

    small = bound <= SAFE_SCORE * SAFE_SCORE

    @pl.when(small)
    def _():
        all_blocks(False)

    @pl.when(jnp.logical_not(small))
    def _():
        all_blocks(True)

    for c in range(together):
        att_t = jnp.concatenate([att_t_s[c, b] for b in range(blocks)], axis=1)
        d_query_t = jnp.concatenate([d_query_t_s[c, b] for b in range(blocks)], axis=1)
        gate_t = gate_t_s[c]
        gated_t = (gate_t * att_t).astype(BF16)
        d_gpre_t = (d_gated_t_s[c] * att_t * gate_t * (1.0 - gate_t)).astype(BF16)
        d_qg_t = jnp.concatenate([(d_query_t * scale).astype(BF16), d_gpre_t], axis=0)
        d_kv = d_kv_s[c].reshape(blocks * size, 2 * proj).astype(BF16)
        w_qg = jnp.concatenate([w_all_ref[:, :proj], w_all_ref[:, 3 * proj :]], axis=1)
        d_pair_s[...] = dot(d_kv, w_all_t_ref[proj : 3 * proj, :]) + dot(w_qg, d_qg_t).T
        for s in range(pieces):
            rows = pl.ds(pl.multiple_of(owners_ref[s] * tile_rows, tile_rows), tile_rows)
            d_pair_out[s][c] = d_pair_s[rows, :].astype(BF16)
        dw_qg_s[...] += dot(d_qg_t, act_s[c])
        dw_kv_s[...] += dot(act_t_s[c], d_kv)
        dwo_s[...] += dot(gated_t, grad_s[c])

    if last:

        @pl.when(pl.program_id(0) == pl.num_programs(0) - 1)
        def _():
            tile = d_bias_out.shape[3]
            for b in range(blocks):
                for e in range(slots):
                    for h in range(heads):
                        turned = d_bias_s[b, e, h].T.astype(BF16)
                        for sub in range(size // tile):
                            d_bias_out[b * (size // tile) + sub, e, h] = turned[
                                sub * tile : (sub + 1) * tile
                            ]
            d_w_out[0] = dw_qg_s[:proj, :].T
            d_w_out[1] = dw_kv_s[:, :proj]
            d_w_out[2] = dw_kv_s[:, proj:]
            d_w_out[3] = dw_qg_s[proj:, :].T
            d_w_out[4] = dwo_s[...]


def attention(pieces, bias, w_all, w_out, tables, lens, owners, carried, last, query_tile):
    count = len(pieces)
    _, columns, tile_rows, chan = pieces[0].shape
    blocks, slots = tables.shape
    heads = bias.shape[2]
    proj = w_out.shape[0]
    size = tile_rows * count // blocks
    tokens = blocks * size
    together = math.gcd(TOGETHER, columns)
    dims = (count, heads, proj // heads, blocks, size, slots, together)
    first = carried is None

    def whole(x):
        return pl.BlockSpec(x.shape, lambda j, *_: (0,) * len(x.shape))

    sums = [
        ((blocks, slots, heads, size, size), F32),
        ((2 * proj, chan), F32),
        ((chan, 2 * proj), F32),
        ((proj, chan), F32),
    ]
    if last:
        results = [
            ((tokens // query_tile, slots, heads, query_tile, size), BF16),
            ((5, chan, proj), F32),
        ]
    else:
        results = sums
    results = [jax.ShapeDtypeStruct(*x) for x in results]
    scratch = [
        ((together, tokens, chan), BF16),
        ((together, tokens, chan), BF16),
        ((together, chan, tokens), BF16),
        ((together, blocks, size, 2 * proj), BF16),
        ((together, blocks, 2 * proj, size), BF16),
        ((together, blocks, heads, 2 * proj, 2 * size), BF16),
        ((together, blocks, heads * size, proj), BF16),
        ((together, blocks, heads * size, proj), BF16),
        ((together, proj, tokens), F32),
        ((together, proj, tokens), F32),
        ((together, heads, slots * size, 2 * size), F32),
        ((together, slots * size, heads * size), BF16),
        ((together, slots * size, heads * size), BF16),
        ((together, blocks, size, 2 * proj), F32),
        ((together, blocks, proj, size), F32),
        ((together, blocks, proj, size), F32),
        ((tokens, chan), F32),
    ]
    scratch = [pltpu.VMEM(*x) for x in (sums if last else []) + scratch]
    fixed = [bias, w_all, w_all.T, w_out] + ([] if first else list(carried))
    pairs = tokens * size * slots * heads
    outs = pl.pallas_call(
        functools.partial(attention_kernel, dims, first, last),
        grid_spec=pltpu.PrefetchScalarGridSpec(
            num_scalar_prefetch=3,
            grid=(columns // together,),
            in_specs=[
                pl.BlockSpec((2, together, tile_rows, chan), lambda j, *_: (0, j, 0, 0))
            ] * count
            + [whole(x) for x in fixed],
            out_specs=[pl.BlockSpec((together, tile_rows, chan), lambda j, *_: (j, 0, 0))] * count
            + [whole(x) for x in results],
            scratch_shapes=scratch,
        ),
        out_shape=[jax.ShapeDtypeStruct((columns, tile_rows, chan), BF16)] * count + results,
        compiler_params=pltpu.CompilerParams(vmem_limit_bytes=VMEM_LIMIT),
        cost_estimate=pl.CostEstimate(
            flops=columns * pairs * 1200,
            bytes_accessed=columns * tokens * chan * 6 + 10 * 2**20,
            transcendentals=columns * pairs,
        ),
    )(tables, lens, owners, *pieces, *fixed)
    return outs[:count], outs[count:]


class Peers:
    def __init__(self, axis, stride, count):
        self.axis, self.count = axis, count
        self.paired = count & (count - 1) == 0
        place = lax.axis_index(axis)
        self.digit = place // stride % count
        everyone = range(lax.axis_size(axis))
        self.routes = []
        for s in range(count):
            route = []
            for p in everyone:
                d = p // stride % count
                route.append((p, p + (self.step(d, s) - d) * stride))
            self.routes.append(route)

    def step(self, digit, s):
        return digit ^ s if self.paired else (digit + s) % self.count

    def target(self, s):
        return self.step(self.digit, s)

    def source(self, s):
        return self.target(s) if self.paired else (self.digit - s) % self.count

    def send(self, x, s, home=False):
        route = self.routes[s]
        if home:
            route = [(t, f) for f, t in route]
        return x if s == 0 else lax.ppermute(x, self.axis, route)

    def positions(self):
        digits = jnp.arange(self.count)
        return self.digit ^ digits if self.paired else (self.digit - digits) % self.count

    def gather(self, x):
        return jnp.stack([self.send(x, s) for s in range(self.count)])

    def scatter_sum(self, parts):
        total = None
        for s in range(self.count):
            mine = [lax.dynamic_index_in_dim(p, self.target(s), 0, keepdims=False) for p in parts]
            total = self.add(total, mine, s)
        return total

    def add(self, total, parts, s):
        width = parts[0].shape[-1]
        if s and all(p.shape[-1] == width for p in parts):
            joined = jnp.concatenate([p.reshape(-1, width).astype(BF16) for p in parts])
            joined = self.send(joined, s)
            came, at = [], 0
            for p in parts:
                rows = p.size // width
                came.append(joined[at : at + rows].reshape(p.shape))
                at += rows
        else:
            came = [self.send(p.astype(BF16), s) if s else p for p in parts]
        came = [x.astype(F32) for x in came]
        return came if total is None else [t + x for t, x in zip(total, came)]


def on_device(
    pair_act, out_grad, tri_bias, w_query, w_key, w_value, w_gate, w_out, key_blocks, list_len
):
    row_count = lax.axis_size("row")
    col_count = lax.axis_size("col")
    tile_rows, tile_cols, chan = pair_act.shape
    heads = tri_bias.shape[0]
    query_tile = tri_bias.shape[2]
    proj = w_query.shape[1]
    blocks, slots = key_blocks.shape
    tokens = tile_rows * row_count
    size = tokens // blocks
    col_width = tile_cols // row_count
    chunks = math.gcd(CHUNKS, col_width)
    width = col_width // chunks
    inner = math.gcd(2, col_count)
    rows = Peers("row", 1, row_count)
    near = Peers("col", 1, inner)
    far = Peers("col", inner, col_count // inner)

    gathered = far.gather(rows.gather(jnp.transpose(tri_bias, (0, 2, 1))))
    gathered = near.gather(gathered).reshape((col_count,) + (row_count, heads, query_tile, tile_rows))
    columns = jnp.arange(col_count)
    col_pos = near.positions()[columns % inner] * far.count + far.positions()[columns // inner]
    bias = shifted_bias(
        gathered,
        key_blocks,
        list_len,
        col_pos.astype(jnp.int32),
        rows.positions().astype(jnp.int32),
    )

    both = jnp.stack([pair_act, out_grad]).reshape(2, tile_rows, row_count, chunks, width, chan)
    both = jnp.transpose(both, (2, 3, 0, 4, 1, 5))
    owners = jnp.stack([rows.source(s) for s in range(row_count)]).astype(jnp.int32)
    w_all = jnp.concatenate([w_query, w_key, w_value, w_gate], axis=1)
    outgoing = [
        lax.dynamic_index_in_dim(both, rows.target(s), 0, keepdims=False) for s in range(row_count)
    ]
    carried = None
    returned = []
    for c in range(chunks):
        pieces = [rows.send(outgoing[s][c], s) for s in range(row_count)]
        d_pieces, carried = attention(
            pieces, bias, w_all, w_out, key_blocks, list_len, owners, carried,
            c == chunks - 1, query_tile,
        )
        returned.append(jnp.stack([rows.send(d_pieces[s], s, home=True) for s in range(row_count)]))

    d_pair = jnp.stack(returned, axis=1)
    steps = jnp.arange(row_count)
    order = rows.digit ^ steps if rows.paired else (steps - rows.digit) % row_count
    d_pair = jnp.take(d_pair, order, axis=0)
    d_pair = jnp.transpose(d_pair, (3, 0, 1, 2, 4)).reshape(tile_rows, tile_cols, chan)

    slot_bias, w_part = carried
    weights = w_part.shape[0]
    w_part = w_part.reshape(col_count // inner, inner, -1, proj)
    slot_bias = slot_bias.reshape((col_count // inner, inner) + slot_bias.shape[1:])
    parts = near.scatter_sum([jnp.moveaxis(slot_bias, 1, 0), jnp.moveaxis(w_part, 1, 0)])
    slot_bias, w_part = far.scatter_sum(parts)
    block = lax.axis_index("col") * query_tile // size
    chosen = lax.dynamic_index_in_dim(key_blocks, block, 0, keepdims=False)
    live = jnp.arange(slots) < lax.dynamic_index_in_dim(list_len, block, 0, keepdims=False)
    per_block = size // tile_rows
    slot_bias = slot_bias.reshape(slots, heads, query_tile, per_block, tile_rows)

    total = None
    for s in range(row_count):
        owner = rows.target(s)
        piece = lax.dynamic_index_in_dim(slot_bias, owner % per_block, 3, keepdims=False)
        hit = (chosen == owner // per_block) & live
        piece = jnp.sum(jnp.where(hit[:, None, None, None], piece, 0.0), axis=0)
        total = rows.add(total, [piece, w_part], s)
    d_bias, w_part = total
    w_sum = near.gather(far.gather(w_part.astype(BF16)))
    w_sum = jnp.take(jnp.take(w_sum, near.positions(), axis=0), far.positions(), axis=1)
    w_sum = jnp.moveaxis(w_sum, 0, 1).reshape(weights, chan, proj).astype(F32)
    return (d_pair, jnp.transpose(d_bias, (0, 2, 1))) + tuple(w_sum[n] for n in range(weights))


def solution(mesh):
    in_specs = (
        P("row", "col", None),
        P("row", "col", None),
        P(None, "row", "col"),
        P(),
        P(),
        P(),
        P(),
        P(),
        P(),
        P(),
    )
    out_specs = (P("row", "col", None), P(None, "row", "col"), P(), P(), P(), P(), P())
    return jax.shard_map(
        on_device, mesh=mesh, in_specs=in_specs, out_specs=out_specs, check_vma=False
    )
```

time: 1070 us -> 208 us (0.19); the launches traced: 1060 us -> 212 us
  local copies, waits for them, and re-layouts: 460 us -> 24 us
  matrix products: 201 us -> 0 us
  other arithmetic: 165 us -> 14.6 us
  waiting for transfers between devices: 167 us -> 41 us
  Pallas kernels: 0 us -> 91.9 us
  loops' own time: 34.1 us -> 0 us
  starting transfers between devices: 13.8 us -> 38.7 us
  between operations: 14.3 us -> 1.34 us
    dot_general x31 -> x0, matrix products: 201 us -> none  [the longest x4 39.2 us: per_block(): jnp.einsum('whiek,ekwhd->iwhd', probs_low, v_sel, preferred_element_type=...]
    psum x1 -> x0, waiting for transfers between devices: 126 us -> none  [on_device(): w_sum, o_sum = lax.psum((w_grad, o_grad), ('row', 'col'))]
    reshape x9 -> x0, local copies, waits for them, and re-layouts: 99.1 us -> none  [the longest x1 12.9 us: on_device(): gate_act.reshape(block_shape)]
    pallas_call x0 -> x3, Pallas kernels: none -> 91.9 us  [the longest x2 86 us: attention(): pl.pallas_call(functools.partial(attention_kernel, dims, first, last), gr...]
    gather x12 -> x5, local copies, waits for them, and re-layouts: 87.9 us -> 4.99 us  [the longest x1 2.54 us: on_device(): d_pair = jnp.take(d_pair, order, axis=0)]
    select_n x8 -> x0, local copies, waits for them, and re-layouts: 80.1 us -> none  [the longest x4 42.3 us: per_block(): v_sel = jnp.take(value_all, chosen, axis=0)]
    scatter-add x8 -> x0, other arithmetic: 57.9 us -> none  [the longest x4 29 us: per_block(): dv_acc = dv_acc.at[chosen].add(dv_part)]
    select_n x9 -> x7, other arithmetic: 51.6 us -> 0.46 us  [the longest x2 0.27 us: on_device(): d_pair = jnp.take(d_pair, order, axis=0)]
  transfers between devices with their start and end apart: 7 -> 30, of which waited for: 3 -> 9; matrix products, arithmetic and copies ran while one was open for 19% -> 15% of each run, Pallas kernels for 0% -> 23%
where the time goes in v2:
time: 208 us; the launch traced here: 212 us
  Pallas kernels  91.9 us (44%)
  waiting for transfers between devices  41 us (20%)
  starting transfers between devices  38.7 us (19%)
  local copies, waits for them, and re-layouts  24 us (12%)
  other arithmetic  14.6 us (7%)
    pallas_call x2, Pallas kernels, attention(): pl.pallas_call(functools.partial(attention_kernel, dims, first, last), gr...  86 us
    ppermute x30, waiting for transfers between devices, send(): return x if s == 0 else lax.ppermute(x, self.axis, route)  41 us
    ppermute x30, starting transfers between devices, send(): return x if s == 0 else lax.ppermute(x, self.axis, route)  38.7 us
    unnamed x51, local copies, waits for them, and re-layouts  10 us
    pallas_call x1, Pallas kernels, shifted_bias(): pl.pallas_call(bias_kernel, grid_spec=pltpu.PrefetchScalarGridSpec(num_sc...  5.86 us
    squeeze x4, local copies, waits for them, and re-layouts, on_device(): pieces = [rows.send(outgoing[s][c], s) for s in range(row_count)]  4.33 us
  transfers between devices with their start and end apart: 30, of which 9 were waited for; matrix products, arithmetic and copies ran while one was open for 15% of the time, Pallas kernels for 23%

profile of v2, /device:TPU:0, one launch (start us, length us, event | category | flops | bytes accessed | tf_op | source)
XLA Modules:
  0.0 211.5 jit_solution(16852116501228633323)
XLA Ops:
  0.6 3.0 %collective-permute-start.3 = (bf16[4,64,128]{2,1,0:T(8,128)(2,1)}, bf16[4,64,128]{2,1,0:T(8,128)(2,1)S(1)}, u32[]{:S(2)}, u32[]{:S(2)}) collective-permute-start(bf16[4,64,128]{2,1,0:T(8,128)(2,1)} %bitcast.190), channel_id=1, source_target_pairs={{0,8},{8,0},{16,24},{24,16},{1,9},{9,1},{17,25},{25,17},{2,10},{10... | collective-permute-start | bytes 196616 | tf_op jit(solution)/shard_map/ppermute | solution.py:358
  3.6 1.5 collective-permute-start.4
  5.2 3.1 %copy.26 = bf16[128,64,128]{2,0,1:T(8,128)(2,1)S(1)} copy(bf16[128,64,128]{2,1,0:T(8,128)(2,1)} %param.10) | data formatting | bytes 4194304 | tf_op args[0]
  8.3 2.7 %copy.27 = bf16[128,64,128]{2,0,1:T(8,128)(2,1)} copy(bf16[128,64,128]{2,1,0:T(8,128)(2,1)S(1)} %copy-done.1) | data formatting | bytes 4194304 | tf_op args[1]
  11.0 2.9 %fusion.1 = (bf16[1,2,2,8,128,128]{5,4,3,2,1,0:T(8,128)(2,1)}, bf16[1,2,2,8,128,128]{5,4,3,2,1,0:T(8,128)(2,1)S(1)}, bf16[1,2,2,8,128,128]{5,4,3,2,1,0:T(8,128)(2,1)S(1)}, bf16[1,2,2,8,128,128]{5,4,3,2,1,0:T(8,128)(2,1)S(1)}) fusion(s32[]{:T(128)S(6)} %select_n.216, bf16[1,128,4,2,8,128]{5,1,4,0,3,2:T(8,128)(2,1)S(1)} %bitcast.153, ...), kind=kLoop, calls=%fused_computation.18 | loop fusion | flops 2097152 | bytes 8388624 | tf_op jit(solution)/shard_map/jit(dynamic_index_in_dim)/dynamic_slice | solution.py:427
  13.9 1.1 slice_bitcast_fusion.6
  15.0 1.9 collective-permute-start
  17.0 1.1 slice_bitcast_fusion.5
  18.1 1.5 collective-permute-start.1
  20.2 0.7 fusion.21
  20.9 0.8 copy.32.refs_5_
  22.3 0.6 gather_fusion
  23.6 1.6 collective-permute-start.6
  25.3 2.6 %collective-permute-start.7 = (bf16[4,4,64,128]{3,2,1,0:T(8,128)(2,1)S(1)}, bf16[4,4,64,128]{3,2,1,0:T(8,128)(2,1)S(1)}, u32[]{:S(2)}, u32[]{:S(2)}) collective-permute-start(bf16[4,4,64,128]{3,2,1,0:T(8,128)(2,1)S(1)} %get-tuple-element.78), channel_id=1, source_target_pairs={{0,4},{1,5},{2,6},{3,7},{4,0},{5,1},{6,2},{7,3},{8,12},{9,13},{10,... | collective-permute-start | bytes 786440 | tf_op jit(solution)/shard_map/ppermute | solution.py:358
  28.1 1.1 slice_bitcast_fusion.4
  29.2 5.1 %collective-permute-done.6 = bf16[4,4,64,128]{3,2,1,0:T(8,128)(2,1)S(1)} collective-permute-done((bf16[4,4,64,128]{3,2,1,0:T(8,128)(2,1)S(1)}, bf16[4,4,64,128]{3,2,1,0:T(8,128)(2,1)S(1)}, u32[]{:S(2)}, u32[]{:S(2)}) %collective-permute-start.6) | collective-permute-done | bytes 262176 | tf_op jit(solution)/shard_map/ppermute | solution.py:358
  34.5 12.1 %collective-permute-done.7 = bf16[4,4,64,128]{3,2,1,0:T(8,128)(2,1)S(1)} collective-permute-done((bf16[4,4,64,128]{3,2,1,0:T(8,128)(2,1)S(1)}, bf16[4,4,64,128]{3,2,1,0:T(8,128)(2,1)S(1)}, u32[]{:S(2)}, u32[]{:S(2)}) %collective-permute-start.7) | collective-permute-done | bytes 262176 | tf_op jit(solution)/shard_map/ppermute | solution.py:358
  48.6 0.7 pad_add_fusion.owners_ref
  49.3 1.0 slice_bitcast_fusion.7
  50.9 2.7 %pad_maximum_fusion = bf16[2,4,4,4,64,128]{5,4,3,2,1,0:T(8,128)(2,1)} fusion(bf16[1,4,4,4,64,128]{5,4,3,2,1,0:T(8,128)(2,1)} %bitcast.26, bf16[1,4,4,4,64,128]{5,4,3,2,1,0:T(8,128)(2,1)S(1)} %get-tuple-element.70), kind=kLoop, calls=%fused_computation.13 | loop fusion | flops 1048576 | bytes 4194304 | tf_op jit(solution)/shard_map/stack | solution.py:365
  53.6 5.9 %shard_map.153.refs_4_ = f32[4,4,4,128,128]{4,3,2,1,0:T(8,128)} custom-call(s32[4,3]{1,0:T(4,128)} %tables_ref.5, s32[4]{0:T(128)} %lens_ref.5, s32[8]{0:T(128)} %multiply_add_fusion.col_pos_ref, s32[4]{0:T(128)} %iota_xor_fusion.2.row_pos_ref, bf16[8,4,4,64,128]{4,3,2,1,0:T(8,128)(2,1)} %bitcast.151, bf16[8,4,4,64,128]{4,3,2,1,0:T(8,128)(2,1)} %bitcast.152), custom_call_target="tpu_custom_call" | custom-call | tf_op jit(solution)/shard_map/pallas_call | solution.py:58
  59.5 2.5 %collective-permute-start.15 = (bf16[2,8,128,128]{3,2,1,0:T(8,128)(2,1)S(1)}, bf16[2,8,128,128]{3,2,1,0:T(8,128)(2,1)S(1)}, u32[]{:S(2)}, u32[]{:S(2)}) collective-permute-start(bf16[2,8,128,128]{3,2,1,0:T(8,128)(2,1)S(1)} %copy-done.4), channel_id=1, source_target_pairs={{0,24},{8,16},{16,8},{24,0},{1,25},{9,17},{17,9},{25,1},{2,26},{10... | collective-permute-start | bytes 1572872 | tf_op jit(solution)/shard_map/ppermute | solution.py:358
  62.0 42.2 %shard_map.154 = (bf16[8,128,128]{2,1,0:T(8,128)(2,1)}, bf16[8,128,128]{2,1,0:T(8,128)(2,1)}, bf16[8,128,128]{2,1,0:T(8,128)(2,1)}, bf16[8,128,128]{2,1,0:T(8,12...) custom-call(s32[4,3]{1,0:T(4,128)} %tables_ref.5, ...), custom_call_target="tpu_custom_call" | custom-call | flops 7549747200 | bytes 13631488 | tf_op jit(solution)/shard_map/pallas_call | solution.py:306
  104.2 0.8 copy-done.14
  105.2 43.8 %shard_map.155 = (bf16[8,128,128]{2,1,0:T(8,128)(2,1)}, bf16[8,128,128]{2,1,0:T(8,128)(2,1)}, bf16[8,128,128]{2,1,0:T(8,128)(2,1)}, bf16[8,128,128]{2,1,0:T(8,12...) custom-call(s32[4,3]{1,0:T(4,128)} %tables_ref.5, s32[4]{0:T(128)} %lens_ref.5, ...), custom_call_target="tpu_custom_call" | custom-call | flops 7549747200 | bytes 13631488 | tf_op jit(solution)/shard_map/pallas_call | solution.py:306
  149.1 1.3 constant_dynamic-slice_fusion
  150.4 1.1 dynamic-slice_convert_fusion.3
  151.6 1.3 bitcast_and_fusion.3
  154.7 2.4 %collective-permute-start.12 = (bf16[8,128,128]{2,1,0:T(8,128)(2,1)S(1)}, bf16[8,128,128]{2,1,0:T(8,128)(2,1)S(1)}, u32[]{:S(2)}, u32[]{:S(2)}) collective-permute-start(bf16[8,128,128]{2,1,0:T(8,128)(2,1)S(1)} %copy-done.17), channel_id=1, source_target_pairs={{24,0},{16,8},{8,16},{0,24},{25,1},{17,9},{9,17},{1,25},{26,2},{18... | collective-permute-start | bytes 786440 | tf_op jit(solution)/shard_map/ppermute | solution.py:358
  158.9 3.9 %collective-permute-done.10 = bf16[8,128,128]{2,1,0:T(8,128)(2,1)S(1)} collective-permute-done((bf16[8,128,128]{2,1,0:T(8,128)(2,1)S(1)}, bf16[8,128,128]{2,1,0:T(8,128)(2,1)S(1)}, u32[]{:S(2)}, u32[]{:S(2)}) %collective-permute-start.10) | collective-permute-done | bytes 262176 | tf_op jit(solution)/shard_map/ppermute | solution.py:358
  163.3 5.7 %collective-permute-done.11 = bf16[8,128,128]{2,1,0:T(8,128)(2,1)S(1)} collective-permute-done((bf16[8,128,128]{2,1,0:T(8,128)(2,1)S(1)}, bf16[8,128,128]{2,1,0:T(8,128)(2,1)S(1)}, u32[]{:S(2)}, u32[]{:S(2)}) %collective-permute-start.11) | collective-permute-done | bytes 262176 | tf_op jit(solution)/shard_map/ppermute | solution.py:358
  169.0 3.8 %collective-permute-start.21 = (bf16[848,128]{1,0:T(8,128)(2,1)S(1)}, bf16[848,128]{1,0:T(8,128)(2,1)S(1)}, u32[]{:S(2)}, u32[]{:S(2)}) collective-permute-start(bf16[848,128]{1,0:T(8,128)(2,1)S(1)} %pad_maximum_fusion.6), channel_id=1, source_target_pairs={{0,4},{1,5},{2,6},{3,7},{4,0},{5,1},{6,2},{7,3},{8,12},{9,13},{10,... | collective-permute-start | bytes 651272 | tf_op jit(solution)/shard_map/ppermute | solution.py:358
  172.9 1.2 collective-permute-done.16
  174.1 1.9 collective-permute-start.22
  176.2 3.4 %collective-permute-done.17 = bf16[8,128,128]{2,1,0:T(8,128)(2,1)S(1)} collective-permute-done((bf16[8,128,128]{2,1,0:T(8,128)(2,1)S(1)}, bf16[8,128,128]{2,1,0:T(8,128)(2,1)S(1)}, u32[]{:S(2)}, u32[]{:S(2)}) %collective-permute-start.17) | collective-permute-done | bytes 262176 | tf_op jit(solution)/shard_map/ppermute | solution.py:358
  179.7 7.8 %collective-permute-done.22 = bf16[848,128]{1,0:T(8,128)(2,1)S(1)} collective-permute-done((bf16[848,128]{1,0:T(8,128)(2,1)S(1)}, bf16[848,128]{1,0:T(8,128)(2,1)S(1)}, u32[]{:S(2)}, u32[]{:S(2)}) %collective-permute-start.22) | collective-permute-done | bytes 217120 | tf_op jit(solution)/shard_map/ppermute | solution.py:358
  187.8 0.7 pad_maximum_fusion.11
  188.5 0.9 collective-permute-start.23
  189.9 2.1 collective-permute-start.25
  192.0 1.5 pad_maximum_fusion.1
  193.5 2.5 %gather_fusion.2 = bf16[4,2,8,128,128]{4,3,2,1,0:T(8,128)(2,1)S(1)} fusion(bf16[4,2,8,128,128]{4,3,2,0,1:T(8,128)(2,1)} %pad_maximum_fusion.1, s32[1024]{0:T(1024)S(1)} %pad_clamp_fusion.2), kind=kCustom, calls=%fused_computation.2 | custom fusion | bytes 4194320 | tf_op jit(solution)/shard_map/jit(_take)/gather | solution.py:442
  196.1 4.4 %collective-permute-start.26 = (bf16[80,128]{1,0:T(8,128)(2,1)S(1)}, bf16[80,128]{1,0:T(8,128)(2,1)S(1)}, u32[]{:S(2)}, u32[]{:S(2)}) collective-permute-start(bf16[80,128]{1,0:T(8,128)(2,1)S(1)} %add_convert_fusion), channel_id=1, source_target_pairs={{0,2},{1,3},{2,0},{3,1},{4,6},{5,7},{6,4},{7,5},{8,10},{9,11},{10,... | collective-permute-start | bytes 61448 | tf_op jit(solution)/shard_map/ppermute | solution.py:358
  200.5 2.0 collective-permute-start.27
  202.5 1.4 collective-permute-start.28
  204.1 2.7 %copy.34 = bf16[128,64,128]{2,1,0:T(8,128)(2,1)} copy(bf16[128,64,128]{2,0,1:T(8,128)(2,1)S(1)} %bitcast.155) | data formatting | bytes 4194304
  206.8 1.2 collective-permute-done.28
  208.1 0.7 fusion.8
  210.8 0.7 slice_bitcast_fusion.8
  (134 shorter events, 12.5 us)
Async XLA Ops:
  0.6 22.9 %collective-permute-start.3 = (bf16[4,64,128]{2,1,0:T(8,128)(2,1)}, bf16[4,64,128]{2,1,0:T(8,128)(2,1)S(1)}, u32[]{:S(2)}, u32[]{:S(2)}) collective-permute-start(bf16[4,64,128]{2,1,0:T(8,128)(2,1)} %bitcast.190), channel_id=1, source_target_pairs={{0,8},{8,0},{16,24},{24,16},{1,9},{9,1},{17,25},{25,17},{2,10},{10... | collective-permute-start | bytes 196616 | tf_op jit(solution)/shard_map/ppermute | solution.py:358
  3.6 19.9 %collective-permute-start.4 = (bf16[4,64,128]{2,1,0:T(8,128)(2,1)}, bf16[4,64,128]{2,1,0:T(8,128)(2,1)S(1)}, u32[]{:S(2)}, u32[]{:S(2)}) collective-permute-start(bf16[4,64,128]{2,1,0:T(8,128)(2,1)} %bitcast.191), channel_id=1, source_target_pairs={{0,16},{8,24},{16,0},{24,8},{1,17},{9,25},{17,1},{25,9},{2,18},{10... | collective-permute-start | bytes 196616 | tf_op jit(solution)/shard_map/ppermute | solution.py:358
  5.2 18.4 %collective-permute-start.5 = (bf16[4,64,128]{2,1,0:T(8,128)(2,1)}, bf16[4,64,128]{2,1,0:T(8,128)(2,1)S(1)}, u32[]{:S(2)}, u32[]{:S(2)}) collective-permute-start(bf16[4,64,128]{2,1,0:T(8,128)(2,1)} %bitcast.192), channel_id=1, source_target_pairs={{0,24},{8,16},{16,8},{24,0},{1,25},{9,17},{17,9},{25,1},{2,26},{10... | collective-permute-start | bytes 196616 | tf_op jit(solution)/shard_map/ppermute | solution.py:358
  5.2 3.1 %copy-start.1 = (bf16[128,64,128]{2,1,0:T(8,128)(2,1)S(1)}, bf16[128,64,128]{2,1,0:T(8,128)(2,1)}, u32[]{:S(2)}) copy-start(bf16[128,64,128]{2,1,0:T(8,128)(2,1)} %param.11) | copy-start | bytes 6291460
  13.9 5.8 %copy-start.9 = (bf16[128,128]{1,0:T(8,128)(2,1)S(1)}, bf16[128,128]{1,0:T(8,128)(2,1)}, u32[]{:S(2)}) copy-start(bf16[128,128]{1,0:T(8,128)(2,1)} %param.13) | copy-start | bytes 98308
  13.9 5.9 %copy-start.10 = (bf16[128,128]{1,0:T(8,128)(2,1)S(1)}, bf16[128,128]{1,0:T(8,128)(2,1)}, u32[]{:S(2)}) copy-start(bf16[128,128]{1,0:T(8,128)(2,1)} %param.14) | copy-start | bytes 98308
  13.9 6.1 %copy-start.11 = (bf16[128,128]{1,0:T(8,128)(2,1)S(1)}, bf16[128,128]{1,0:T(8,128)(2,1)}, u32[]{:S(2)}) copy-start(bf16[128,128]{1,0:T(8,128)(2,1)} %param.15) | copy-start | bytes 98308
  13.9 6.2 %copy-start.12 = (bf16[128,128]{1,0:T(8,128)(2,1)S(1)}, bf16[128,128]{1,0:T(8,128)(2,1)}, u32[]{:S(2)}) copy-start(bf16[128,128]{1,0:T(8,128)(2,1)} %param.16) | copy-start | bytes 98308
  15.0 44.4 %collective-permute-start = (bf16[2,8,128,128]{3,2,1,0:T(8,128)(2,1)}, bf16[2,8,128,128]{3,2,1,0:T(8,128)(2,1)}, u32[]{:S(2)}, u32[]{:S(2)}) collective-permute-start(bf16[2,8,128,128]{3,2,1,0:T(8,128)(2,1)} %get-tuple-element.66), channel_id=1, source_target_pairs={{0,8},{8,0},{16,24},{24,16},{1,9},{9,1},{17,25},{25,17},{2,10},{10... | collective-permute-start | bytes 1572872 | tf_op jit(solution)/shard_map/ppermute | solution.py:358
  17.0 6.6 %copy-start.8 = (bf16[4,128,64]{1,2,0:T(8,128)(2,1)S(1)}, bf16[4,128,64]{1,2,0:T(8,128)(2,1)}, u32[]{:S(2)}) copy-start(bf16[4,128,64]{1,2,0:T(8,128)(2,1)} %param.12) | copy-start | bytes 196612
  17.0 11.1 %copy-start = (bf16[1,2,2,8,128,128]{5,4,3,2,1,0:T(8,128)(2,1)S(1)}, bf16[1,2,2,8,128,128]{5,4,3,2,1,0:T(8,128)(2,1)}, u32[]{:S(2)}) copy-start(bf16[1,2,2,8,128,128]{5,4,3,2,1,0:T(8,128)(2,1)} %get-tuple-element.55) | copy-start | bytes 3145732
  18.1 43.9 %collective-permute-start.1 = (bf16[2,8,128,128]{3,2,1,0:T(8,128)(2,1)}, bf16[2,8,128,128]{3,2,1,0:T(8,128)(2,1)}, u32[]{:S(2)}, u32[]{:S(2)}) collective-permute-start(bf16[2,8,128,128]{3,2,1,0:T(8,128)(2,1)} %get-tuple-element.64), channel_id=1, source_target_pairs={{0,16},{8,24},{16,0},{24,8},{1,17},{9,25},{17,1},{25,9},{2,18},{10... | collective-permute-start | bytes 1572872 | tf_op jit(solution)/shard_map/ppermute | solution.py:358
  23.6 10.6 %collective-permute-start.6 = (bf16[4,4,64,128]{3,2,1,0:T(8,128)(2,1)S(1)}, bf16[4,4,64,128]{3,2,1,0:T(8,128)(2,1)S(1)}, u32[]{:S(2)}, u32[]{:S(2)}) collective-permute-start(bf16[4,4,64,128]{3,2,1,0:T(8,128)(2,1)S(1)} %get-tuple-element.78), channel_id=1, source_target_pairs={{0,2},{1,3},{2,0},{3,1},{4,6},{5,7},{6,4},{7,5},{8,10},{9,11},{10,... | collective-permute-start | bytes 786440 | tf_op jit(solution)/shard_map/ppermute | solution.py:358
  25.3 21.4 %collective-permute-start.7 = (bf16[4,4,64,128]{3,2,1,0:T(8,128)(2,1)S(1)}, bf16[4,4,64,128]{3,2,1,0:T(8,128)(2,1)S(1)}, u32[]{:S(2)}, u32[]{:S(2)}) collective-permute-start(bf16[4,4,64,128]{3,2,1,0:T(8,128)(2,1)S(1)} %get-tuple-element.78), channel_id=1, source_target_pairs={{0,4},{1,5},{2,6},{3,7},{4,0},{5,1},{6,2},{7,3},{8,12},{9,13},{10,... | collective-permute-start | bytes 786440 | tf_op jit(solution)/shard_map/ppermute | solution.py:358
  27.9 19.3 %collective-permute-start.8 = (bf16[4,4,64,128]{3,2,1,0:T(8,128)(2,1)S(1)}, bf16[4,4,64,128]{3,2,1,0:T(8,128)(2,1)S(1)}, u32[]{:S(2)}, u32[]{:S(2)}) collective-permute-start(bf16[4,4,64,128]{3,2,1,0:T(8,128)(2,1)S(1)} %get-tuple-element.78), channel_id=1, source_target_pairs={{0,6},{1,7},{2,4},{3,5},{4,2},{5,3},{6,0},{7,1},{8,14},{9,15},{10,... | collective-permute-start | bytes 786440 | tf_op jit(solution)/shard_map/ppermute | solution.py:358
  29.1 18.3 %copy-start.13 = (s32[4]{0:T(128)S(1)}, s32[4]{0:T(128)}, u32[]{:S(2)}) copy-start(s32[4]{0:T(128)} %lens_ref.5) | copy-start | bytes 52
  34.3 27.7 %collective-permute-start.2 = (bf16[2,8,128,128]{3,2,1,0:T(8,128)(2,1)}, bf16[2,8,128,128]{3,2,1,0:T(8,128)(2,1)}, u32[]{:S(2)}, u32[]{:S(2)}) collective-permute-start(bf16[2,8,128,128]{3,2,1,0:T(8,128)(2,1)} %get-tuple-element.62), channel_id=1, source_target_pairs={{0,24},{8,16},{16,8},{24,0},{1,25},{9,17},{17,9},{25,1},{2,26},{10... | collective-permute-start | bytes 1572872 | tf_op jit(solution)/shard_map/ppermute | solution.py:358
  46.6 57.5 %collective-permute-start.13 = (bf16[2,8,128,128]{3,2,1,0:T(8,128)(2,1)}, bf16[2,8,128,128]{3,2,1,0:T(8,128)(2,1)}, u32[]{:S(2)}, u32[]{:S(2)}) collective-permute-start(bf16[2,8,128,128]{3,2,1,0:T(8,128)(2,1)} %get-tuple-element.67), channel_id=1, source_target_pairs={{0,8},{8,0},{16,24},{24,16},{1,9},{9,1},{17,25},{25,17},{2,10},{10... | collective-permute-start | bytes 1572872 | tf_op jit(solution)/shard_map/ppermute | solution.py:358
  47.3 3.0 %collective-permute-start.9 = (bf16[4,4,4,64,128]{4,3,2,1,0:T(8,128)(2,1)S(1)}, bf16[4,4,4,64,128]{4,3,2,1,0:T(8,128)(2,1)}, u32[]{:S(2)}, u32[]{:S(2)}) collective-permute-start(bf16[4,4,4,64,128]{4,3,2,1,0:T(8,128)(2,1)S(1)} %get-tuple-element.71), channel_id=1, source_target_pairs={{0,1},{1,0},{2,3},{3,2},{4,5},{5,4},{6,7},{7,6},{8,9},{9,8},{10,11... | collective-permute-start | bytes 3145736 | tf_op jit(solution)/shard_map/ppermute | solution.py:358
  50.3 53.8 %collective-permute-start.14 = (bf16[2,8,128,128]{3,2,1,0:T(8,128)(2,1)S(1)}, bf16[2,8,128,128]{3,2,1,0:T(8,128)(2,1)S(1)}, u32[]{:S(2)}, u32[]{:S(2)}) collective-permute-start(bf16[2,8,128,128]{3,2,1,0:T(8,128)(2,1)S(1)} %copy-done.3), channel_id=1, source_target_pairs={{0,16},{8,24},{16,0},{24,8},{1,17},{9,25},{17,1},{25,9},{2,18},{10... | collective-permute-start | bytes 1572872 | tf_op jit(solution)/shard_map/ppermute | solution.py:358
  53.6 5.9 %copy-start.4 = (bf16[2,8,128,128]{3,2,1,0:T(8,128)(2,1)S(1)}, bf16[2,8,128,128]{3,2,1,0:T(8,128)(2,1)}, u32[]{:S(2)}) copy-start(bf16[2,8,128,128]{3,2,1,0:T(8,128)(2,1)} %get-tuple-element.63) | copy-start | bytes 1572868
  59.5 44.7 %collective-permute-start.15 = (bf16[2,8,128,128]{3,2,1,0:T(8,128)(2,1)S(1)}, bf16[2,8,128,128]{3,2,1,0:T(8,128)(2,1)S(1)}, u32[]{:S(2)}, u32[]{:S(2)}) collective-permute-start(bf16[2,8,128,128]{3,2,1,0:T(8,128)(2,1)S(1)} %copy-done.4), channel_id=1, source_target_pairs={{0,24},{8,16},{16,8},{24,0},{1,25},{9,17},{17,9},{25,1},{2,26},{10... | collective-permute-start | bytes 1572872 | tf_op jit(solution)/shard_map/ppermute | solution.py:358
  149.0 4.6 %copy-start.21 = (bf16[8,128,128]{2,1,0:T(8,128)(2,1)S(1)}, bf16[8,128,128]{2,1,0:T(8,128)(2,1)}, u32[]{:S(2)}) copy-start(bf16[8,128,128]{2,1,0:T(8,128)(2,1)} %get-tuple-element.22) | copy-start | bytes 786436
  149.1 5.2 %copy-start.19 = (bf16[8,128,128]{2,1,0:T(8,128)(2,1)S(1)}, bf16[8,128,128]{2,1,0:T(8,128)(2,1)}, u32[]{:S(2)}) copy-start(bf16[8,128,128]{2,1,0:T(8,128)(2,1)} %get-tuple-element.23) | copy-start | bytes 786436
  149.1 5.7 %copy-start.17 = (bf16[8,128,128]{2,1,0:T(8,128)(2,1)S(1)}, bf16[8,128,128]{2,1,0:T(8,128)(2,1)}, u32[]{:S(2)}) copy-start(bf16[8,128,128]{2,1,0:T(8,128)(2,1)} %get-tuple-element.24) | copy-start | bytes 786436
  149.1 8.1 %copy-start.20 = (bf16[8,128,128]{2,1,0:T(8,128)(2,1)S(1)}, bf16[8,128,128]{2,1,0:T(8,128)(2,1)}, u32[]{:S(2)}) copy-start(bf16[8,128,128]{2,1,0:T(8,128)(2,1)} %get-tuple-element.30) | copy-start | bytes 786436
  149.1 8.7 %copy-start.18 = (bf16[8,128,128]{2,1,0:T(8,128)(2,1)S(1)}, bf16[8,128,128]{2,1,0:T(8,128)(2,1)}, u32[]{:S(2)}) copy-start(bf16[8,128,128]{2,1,0:T(8,128)(2,1)} %get-tuple-element.31) | copy-start | bytes 786436
  150.4 8.0 %copy-start.2 = (bf16[8,3,4,64,128]{4,3,2,1,0:T(8,128)(2,1)S(1)}, bf16[8,3,4,64,128]{4,3,2,1,0:T(8,128)(2,1)}, u32[]{:S(2)}) copy-start(bf16[8,3,4,64,128]{4,3,2,1,0:T(8,128)(2,1)} %get-tuple-element.33) | copy-start | bytes 4718596
  151.5 6.2 %collective-permute-start.19 = (bf16[3392,128]{1,0:T(8,128)(2,1)S(1)}, bf16[3392,128]{1,0:T(8,128)(2,1)S(1)}, u32[]{:S(2)}, u32[]{:S(2)}) collective-permute-start(bf16[3392,128]{1,0:T(8,128)(2,1)S(1)} %pad_maximum_fusion.3), channel_id=1, source_target_pairs={{0,1},{1,0},{2,3},{3,2},{4,5},{5,4},{6,7},{7,6},{8,9},{9,8},{10,11... | collective-permute-start | bytes 2605064 | tf_op jit(solution)/shard_map/ppermute | solution.py:358
  153.6 9.2 %collective-permute-start.10 = (bf16[8,128,128]{2,1,0:T(8,128)(2,1)S(1)}, bf16[8,128,128]{2,1,0:T(8,128)(2,1)S(1)}, u32[]{:S(2)}, u32[]{:S(2)}) collective-permute-start(bf16[8,128,128]{2,1,0:T(8,128)(2,1)S(1)} %copy-done.21), channel_id=1, source_target_pairs={{8,0},{0,8},{24,16},{16,24},{9,1},{1,9},{25,17},{17,25},{10,2},{2,... | collective-permute-start | bytes 786440 | tf_op jit(solution)/shard_map/ppermute | solution.py:358
  154.3 14.8 %collective-permute-start.11 = (bf16[8,128,128]{2,1,0:T(8,128)(2,1)S(1)}, bf16[8,128,128]{2,1,0:T(8,128)(2,1)S(1)}, u32[]{:S(2)}, u32[]{:S(2)}) collective-permute-start(bf16[8,128,128]{2,1,0:T(8,128)(2,1)S(1)} %copy-done.19), channel_id=1, source_target_pairs={{16,0},{24,8},{0,16},{8,24},{17,1},{25,9},{1,17},{9,25},{18,2},{26... | collective-permute-start | bytes 786440 | tf_op jit(solution)/shard_map/ppermute | solution.py:358
  154.7 14.3 %collective-permute-start.12 = (bf16[8,128,128]{2,1,0:T(8,128)(2,1)S(1)}, bf16[8,128,128]{2,1,0:T(8,128)(2,1)S(1)}, u32[]{:S(2)}, u32[]{:S(2)}) collective-permute-start(bf16[8,128,128]{2,1,0:T(8,128)(2,1)S(1)} %copy-done.17), channel_id=1, source_target_pairs={{24,0},{16,8},{8,16},{0,24},{25,1},{17,9},{9,17},{1,25},{26,2},{18... | collective-permute-start | bytes 786440 | tf_op jit(solution)/shard_map/ppermute | solution.py:358
  157.2 16.9 %collective-permute-start.16 = (bf16[8,128,128]{2,1,0:T(8,128)(2,1)S(1)}, bf16[8,128,128]{2,1,0:T(8,128)(2,1)S(1)}, u32[]{:S(2)}, u32[]{:S(2)}) collective-permute-start(bf16[8,128,128]{2,1,0:T(8,128)(2,1)S(1)} %copy-done.20), channel_id=1, source_target_pairs={{8,0},{0,8},{24,16},{16,24},{9,1},{1,9},{25,17},{17,25},{10,2},{2,... | collective-permute-start | bytes 786440 | tf_op jit(solution)/shard_map/ppermute | solution.py:358
  157.8 21.8 %collective-permute-start.17 = (bf16[8,128,128]{2,1,0:T(8,128)(2,1)S(1)}, bf16[8,128,128]{2,1,0:T(8,128)(2,1)S(1)}, u32[]{:S(2)}, u32[]{:S(2)}) collective-permute-start(bf16[8,128,128]{2,1,0:T(8,128)(2,1)S(1)} %copy-done.18), channel_id=1, source_target_pairs={{16,0},{24,8},{0,16},{8,24},{17,1},{25,9},{1,17},{9,25},{18,2},{26... | collective-permute-start | bytes 786440 | tf_op jit(solution)/shard_map/ppermute | solution.py:358
  158.4 4.4 %copy-start.16 = (bf16[8,128,128]{2,1,0:T(8,128)(2,1)S(1)}, bf16[8,128,128]{2,1,0:T(8,128)(2,1)}, u32[]{:S(2)}) copy-start(bf16[8,128,128]{2,1,0:T(8,128)(2,1)} %get-tuple-element.32) | copy-start | bytes 786436
  158.7 17.4 %copy-start.5 = (bf16[8,128,128]{2,1,0:T(8,128)(2,1)S(1)}, bf16[8,128,128]{2,1,0:T(8,128)(2,1)}, u32[]{:S(2)}) copy-start(bf16[8,128,128]{2,1,0:T(8,128)(2,1)} %get-tuple-element.21) | copy-start | bytes 786436
  158.8 20.7 %copy-start.6 = (bf16[8,128,128]{2,1,0:T(8,128)(2,1)S(1)}, bf16[8,128,128]{2,1,0:T(8,128)(2,1)}, u32[]{:S(2)}) copy-start(bf16[8,128,128]{2,1,0:T(8,128)(2,1)} %get-tuple-element.29) | copy-start | bytes 786436
  162.8 16.7 %collective-permute-start.18 = (bf16[8,128,128]{2,1,0:T(8,128)(2,1)S(1)}, bf16[8,128,128]{2,1,0:T(8,128)(2,1)S(1)}, u32[]{:S(2)}, u32[]{:S(2)}) collective-permute-start(bf16[8,128,128]{2,1,0:T(8,128)(2,1)S(1)} %copy-done.16), channel_id=1, source_target_pairs={{24,0},{16,8},{8,16},{0,24},{25,1},{17,9},{9,17},{1,25},{26,2},{18... | collective-permute-start | bytes 786440 | tf_op jit(solution)/shard_map/ppermute | solution.py:358
  169.0 10.7 %collective-permute-start.20 = (bf16[848,128]{1,0:T(8,128)(2,1)S(1)}, bf16[848,128]{1,0:T(8,128)(2,1)S(1)}, u32[]{:S(2)}, u32[]{:S(2)}) collective-permute-start(bf16[848,128]{1,0:T(8,128)(2,1)S(1)} %pad_maximum_fusion.5), channel_id=1, source_target_pairs={{0,2},{1,3},{2,0},{3,1},{4,6},{5,7},{6,4},{7,5},{8,10},{9,11},{10,... | collective-permute-start | bytes 651272 | tf_op jit(solution)/shard_map/ppermute | solution.py:358
  169.0 10.7 %collective-permute-start.21 = (bf16[848,128]{1,0:T(8,128)(2,1)S(1)}, bf16[848,128]{1,0:T(8,128)(2,1)S(1)}, u32[]{:S(2)}, u32[]{:S(2)}) collective-permute-start(bf16[848,128]{1,0:T(8,128)(2,1)S(1)} %pad_maximum_fusion.6), channel_id=1, source_target_pairs={{0,4},{1,5},{2,6},{3,7},{4,0},{5,1},{6,2},{7,3},{8,12},{9,13},{10,... | collective-permute-start | bytes 651272 | tf_op jit(solution)/shard_map/ppermute | solution.py:358
  174.1 13.5 %collective-permute-start.22 = (bf16[848,128]{1,0:T(8,128)(2,1)S(1)}, bf16[848,128]{1,0:T(8,128)(2,1)S(1)}, u32[]{:S(2)}, u32[]{:S(2)}) collective-permute-start(bf16[848,128]{1,0:T(8,128)(2,1)S(1)} %pad_maximum_fusion.7), channel_id=1, source_target_pairs={{0,6},{1,7},{2,4},{3,5},{4,2},{5,3},{6,0},{7,1},{8,14},{9,15},{10,... | collective-permute-start | bytes 651272 | tf_op jit(solution)/shard_map/ppermute | solution.py:358
  188.5 7.5 %collective-permute-start.23 = (bf16[336,128]{1,0:T(8,128)(2,1)}, bf16[336,128]{1,0:T(8,128)(2,1)S(1)}, u32[]{:S(2)}, u32[]{:S(2)}) collective-permute-start(bf16[336,128]{1,0:T(8,128)(2,1)} %get-tuple-element.86), channel_id=1, source_target_pairs={{0,8},{8,0},{16,24},{24,16},{1,9},{9,1},{17,25},{25,17},{2,10},{10... | collective-permute-start | bytes 258056 | tf_op jit(solution)/shard_map/ppermute | solution.py:358
  189.4 6.6 %collective-permute-start.24 = (bf16[336,128]{1,0:T(8,128)(2,1)S(1)}, bf16[336,128]{1,0:T(8,128)(2,1)S(1)}, u32[]{:S(2)}, u32[]{:S(2)}) collective-permute-start(bf16[336,128]{1,0:T(8,128)(2,1)S(1)} %get-tuple-element.87), channel_id=1, source_target_pairs={{0,16},{8,24},{16,0},{24,8},{1,17},{9,25},{17,1},{25,9},{2,18},{10... | collective-permute-start | bytes 258056 | tf_op jit(solution)/shard_map/ppermute | solution.py:358
  189.9 6.2 %collective-permute-start.25 = (bf16[336,128]{1,0:T(8,128)(2,1)S(1)}, bf16[336,128]{1,0:T(8,128)(2,1)S(1)}, u32[]{:S(2)}, u32[]{:S(2)}) collective-permute-start(bf16[336,128]{1,0:T(8,128)(2,1)S(1)} %get-tuple-element.88), channel_id=1, source_target_pairs={{0,24},{8,16},{16,8},{24,0},{1,25},{9,17},{17,9},{25,1},{2,26},{10... | collective-permute-start | bytes 258056 | tf_op jit(solution)/shard_map/ppermute | solution.py:358
  196.1 10.7 %collective-permute-start.26 = (bf16[80,128]{1,0:T(8,128)(2,1)S(1)}, bf16[80,128]{1,0:T(8,128)(2,1)S(1)}, u32[]{:S(2)}, u32[]{:S(2)}) collective-permute-start(bf16[80,128]{1,0:T(8,128)(2,1)S(1)} %add_convert_fusion), channel_id=1, source_target_pairs={{0,2},{1,3},{2,0},{3,1},{4,6},{5,7},{6,4},{7,5},{8,10},{9,11},{10,... | collective-permute-start | bytes 61448 | tf_op jit(solution)/shard_map/ppermute | solution.py:358
  200.5 6.4 %collective-permute-start.27 = (bf16[80,128]{1,0:T(8,128)(2,1)S(1)}, bf16[80,128]{1,0:T(8,128)(2,1)S(1)}, u32[]{:S(2)}, u32[]{:S(2)}) collective-permute-start(bf16[80,128]{1,0:T(8,128)(2,1)S(1)} %add_convert_fusion), channel_id=1, source_target_pairs={{0,4},{1,5},{2,6},{3,7},{4,0},{5,1},{6,2},{7,3},{8,12},{9,13},{10,... | collective-permute-start | bytes 61448 | tf_op jit(solution)/shard_map/ppermute | solution.py:358
  202.5 5.6 %collective-permute-start.28 = (bf16[80,128]{1,0:T(8,128)(2,1)S(1)}, bf16[80,128]{1,0:T(8,128)(2,1)S(1)}, u32[]{:S(2)}, u32[]{:S(2)}) collective-permute-start(bf16[80,128]{1,0:T(8,128)(2,1)S(1)} %add_convert_fusion), channel_id=1, source_target_pairs={{0,6},{1,7},{2,4},{3,5},{4,2},{5,3},{6,0},{7,1},{8,14},{9,15},{10,... | collective-permute-start | bytes 61448 | tf_op jit(solution)/shard_map/ppermute | solution.py:358
  208.1 1.3 collective-permute-start.29
  (4 other events, 5.7 us)

commit v3 on v2

--- a/solution.py
+++ b/solution.py
@@ -68,42 +68,63 @@
     )(key_blocks, list_len, col_pos, row_pos, *([gathered] * per_block))
 
 
-def attention_kernel(dims, first, last, tables_ref, lens_ref, owners_ref, *refs):
-    pieces, heads, head_dim, blocks, size, slots, together = dims
+def attention_kernel(
+    dims, first, last, tables_ref, lens_ref, owners_ref, parity_ref, *refs
+):
+    pieces, heads, head_dim, blocks, size, slots, together, inner = dims
     refs = list(refs)
     take = lambda n: [refs.pop(0) for _ in range(n)]
     inputs = take(pieces)
     bias_ref, w_all_ref, w_all_t_ref, w_out_ref = take(4)
-    carried = [] if first else take(4)
-    d_pair_out = take(pieces)
+    carried = [] if first else take(5)
     if last:
-        d_bias_out, d_w_out = take(2)
+        d_pair_out = take(pieces)
+        keep_out, message_out, d_w_out = take(3)
+        d_pair_s, *sums = take(5)
     else:
-        sums_out = take(4)
-    d_bias_s, dw_qg_s, dw_kv_s, dwo_s = sums = take(4) if last else sums_out
-    (act_s, grad_s, act_t_s, kv_s, kv_t_s, joint_s, d_att_s, query_s, gate_t_s, d_gated_t_s,
-     score_s, probs_s, ds_s, d_kv_s, att_t_s, d_query_t_s, d_pair_s) = refs
+        d_pair_s, *sums = take(5)
+    d_bias_s, dw_qg_s, dw_kv_s, dwo_s = sums
+    (x_s, act_s, grad_s, act_t_s, kv_s, kv_t_s, joint_s, d_att_s, query_s, gate_t_s, d_gated_t_s,
+     score_s, probs_s, ds_s, d_kv_s, att_t_s, d_query_t_s) = refs
     proj = heads * head_dim
     scale = head_dim ** (-0.5)
-    tile_rows = inputs[0].shape[2]
+    _, tile_rows, width, chan = inputs[0].shape
+    tokens = blocks * size
+    all_width = d_pair_s.shape[0] // tokens
+    step = pl.program_id(0)
     span = [slice(b * size, (b + 1) * size) for b in range(blocks)]
     own = [slice(h * head_dim, (h + 1) * head_dim) for h in range(heads)]
     low = [slice(proj + h * head_dim, proj + (h + 1) * head_dim) for h in range(heads)]
 
-    @pl.when(pl.program_id(0) == 0)
+    def rows_at(s, columns):
+        count = tile_rows * columns
+        return pl.ds(pl.multiple_of(owners_ref[s] * count, count), count)
+
+    @pl.when(step == 0)
     def _():
         joint_s[...] = jnp.zeros_like(joint_s)
         for n, ref in enumerate(sums):
-            ref[...] = jnp.zeros_like(ref) if first else carried[n][...]
+            ref[...] = jnp.zeros_like(ref) if first else carried[n + 1][...]
+        if not first:
+            before = all_width - width
+            for j in range(before):
+                d_pair_s[pl.ds(j, tokens, stride=all_width), :] = carried[0][
+                    pl.ds(j, tokens, stride=before), :
+                ]
+        for s in range(pieces):
+            for n in range(2):
+                x_s[n, rows_at(s, width), :] = (
+                    inputs[s][n].astype(F32).reshape(tile_rows * width, chan)
+                )
 
     lane_head = lax.broadcasted_iota(jnp.int32, (size, proj), 1) // head_dim
     bound = jnp.float32(0.0)
     for c in range(together):
-        for s in range(pieces):
-            rows = pl.ds(pl.multiple_of(owners_ref[s] * tile_rows, tile_rows), tile_rows)
-            act_s[c, rows, :] = inputs[s][0, c]
-            grad_s[c, rows, :] = inputs[s][1, c]
-        acts = act_s[c]
+        column = pl.ds(step * together + c, tokens, stride=width)
+        acts = x_s[0, column, :].astype(BF16)
+        grads = x_s[1, column, :].astype(BF16)
+        act_s[c] = acts
+        grad_s[c] = grads
         acts_t = acts.T
         act_t_s[c] = acts_t
         natural = dot(acts, w_all_ref[:, : 3 * proj])
@@ -111,7 +132,7 @@
         queries_t = (across[:proj] * scale).astype(BF16)
         kv_t = across[proj : 3 * proj].astype(BF16)
         gate_t = 1.0 / (1.0 + jnp.exp(-across[3 * proj :]))
-        d_gated_t = dot(w_out_ref[...], grad_s[c].T)
+        d_gated_t = dot(w_out_ref[...], grads.T)
         d_att_t = (d_gated_t * gate_t).astype(BF16)
         gate_t_s[c] = gate_t
         d_gated_t_s[c] = d_gated_t
@@ -140,16 +161,16 @@
             (e, e * size + at, at) for e in range(live) for at in range(0, size, STRIP)
         ]
         rows_of = lambda x: jnp.sum(x.reshape(-1, 8, size), axis=0)
-        for c in range(together):
-            kv = jnp.concatenate([kv_s[c, k] for k in chosen], axis=0)
-            for h in range(heads):
-                score_s[c, h, : live * size, :] = dot(kv, joint_s[c, b, h])
+        kv = [jnp.concatenate([kv_s[c, k] for k in chosen], axis=0) for c in range(together)]
+        kv_t = [jnp.concatenate([kv_t_s[c, k] for k in chosen], axis=1) for c in range(together)]
         for h in range(heads):
             stats = []
             for c in range(together):
+                joint = dot(kv[c], joint_s[c, b, h])
+
                 def scores(e, row, at):
                     return (
-                        score_s[c, h, row : row + STRIP, :size] * LOG2E
+                        joint[row : row + STRIP, :size] * LOG2E
                         + bias_ref[chosen[e], b, h, at : at + STRIP, :]
                     )
 
@@ -165,9 +186,11 @@
                 for e, row, at in strips:
                     value = scores(e, row, at)
                     weight = jnp.exp2(value - peak if shift else value)
+                    d_probs = joint[row : row + STRIP, size:]
                     total += rows_of(weight)
-                    mixed += rows_of(weight * score_s[c, h, row : row + STRIP, size:])
+                    mixed += rows_of(weight * d_probs)
                     score_s[c, h, row : row + STRIP, :size] = weight
+                    score_s[c, h, row : row + STRIP, size:] = d_probs
                 norm = 1.0 / jnp.sum(total, axis=0, keepdims=True)
                 stats.append((norm, jnp.sum(mixed, axis=0, keepdims=True) * norm))
             lanes = slice(h * size, (h + 1) * size)
@@ -181,16 +204,12 @@
                     ds_s[c, part, lanes] = d_scores.astype(BF16)
                     gathered += d_scores
                 d_bias_s[b, e, h, at : at + STRIP, :] = gathered
+            for c in range(together):
+                att_t_s[c, b, own[h], :] = dot(kv_t[c][low[h]], probs_s[c, : live * size, lanes])
+                d_query_t_s[c, b, own[h], :] = dot(kv_t[c][own[h]], ds_s[c, : live * size, lanes])
         for c in range(together):
-            probs = probs_s[c, : live * size, :]
-            ds = ds_s[c, : live * size, :]
-            kv_t = jnp.concatenate([kv_t_s[c, k] for k in chosen], axis=1)
-            for h in range(heads):
-                lanes = slice(h * size, (h + 1) * size)
-                att_t_s[c, b, own[h], :] = dot(kv_t[low[h]], probs[:, lanes])
-                d_query_t_s[c, b, own[h], :] = dot(kv_t[own[h]], ds[:, lanes])
-            d_values = dot(probs, d_att_s[c, b])
-            d_keys = dot(ds, query_s[c, b])
+            d_values = dot(probs_s[c, : live * size, :], d_att_s[c, b])
+            d_keys = dot(ds_s[c, : live * size, :], query_s[c, b])
             for e in range(live):
                 part = slice(e * size, (e + 1) * size)
                 d_kv_s[c, chosen[e], :, :proj] += d_keys[part]
@@ -215,6 +234,7 @@
     def _():
         all_blocks(True)
 
+    w_qg = jnp.concatenate([w_all_ref[:, :proj], w_all_ref[:, 3 * proj :]], axis=1)
     for c in range(together):
         att_t = jnp.concatenate([att_t_s[c, b] for b in range(blocks)], axis=1)
         d_query_t = jnp.concatenate([d_query_t_s[c, b] for b in range(blocks)], axis=1)
@@ -222,66 +242,87 @@
         gated_t = (gate_t * att_t).astype(BF16)
         d_gpre_t = (d_gated_t_s[c] * att_t * gate_t * (1.0 - gate_t)).astype(BF16)
         d_qg_t = jnp.concatenate([(d_query_t * scale).astype(BF16), d_gpre_t], axis=0)
-        d_kv = d_kv_s[c].reshape(blocks * size, 2 * proj).astype(BF16)
-        w_qg = jnp.concatenate([w_all_ref[:, :proj], w_all_ref[:, 3 * proj :]], axis=1)
-        d_pair_s[...] = dot(d_kv, w_all_t_ref[proj : 3 * proj, :]) + dot(w_qg, d_qg_t).T
-        for s in range(pieces):
-            rows = pl.ds(pl.multiple_of(owners_ref[s] * tile_rows, tile_rows), tile_rows)
-            d_pair_out[s][c] = d_pair_s[rows, :].astype(BF16)
+        d_kv = d_kv_s[c].reshape(tokens, 2 * proj).astype(BF16)
+        column = pl.ds(all_width - width + step * together + c, tokens, stride=all_width)
+        d_pair_s[column, :] = (
+            dot(d_kv, w_all_t_ref[proj : 3 * proj, :]) + dot(w_qg, d_qg_t).T
+        )
         dw_qg_s[...] += dot(d_qg_t, act_s[c])
         dw_kv_s[...] += dot(act_t_s[c], d_kv)
         dwo_s[...] += dot(gated_t, grad_s[c])
 
-    if last:
-
-        @pl.when(pl.program_id(0) == pl.num_programs(0) - 1)
-        def _():
-            tile = d_bias_out.shape[3]
-            for b in range(blocks):
-                for e in range(slots):
-                    for h in range(heads):
-                        turned = d_bias_s[b, e, h].T.astype(BF16)
-                        for sub in range(size // tile):
-                            d_bias_out[b * (size // tile) + sub, e, h] = turned[
-                                sub * tile : (sub + 1) * tile
-                            ]
-            d_w_out[0] = dw_qg_s[:proj, :].T
-            d_w_out[1] = dw_kv_s[:, :proj]
-            d_w_out[2] = dw_kv_s[:, proj:]
-            d_w_out[3] = dw_qg_s[proj:, :].T
-            d_w_out[4] = dwo_s[...]
-
-
-def attention(pieces, bias, w_all, w_out, tables, lens, owners, carried, last, query_tile):
+    if not last:
+        return
+
+    @pl.when(step == pl.num_programs(0) - 1)
+    def _():
+        for s in range(pieces):
+            piece = d_pair_s[rows_at(s, all_width), :].reshape(tile_rows, all_width, chan)
+            d_pair_out[s][...] = piece.astype(BF16)
+        weights = [dw_qg_s[:proj, :].T, dw_kv_s[:, :proj], dw_kv_s[:, proj:], dw_qg_s[proj:, :].T]
+        weights.append(dwo_s[...])
+        far, each = keep_out.shape[0], keep_out.shape[1]
+        tile = each // (slots * heads)
+        for n, w in enumerate(weights):
+            d_w_out[n * chan : (n + 1) * chan, :] = w
+            message_out[far * each + n * chan : far * each + (n + 1) * chan, :] = w.astype(BF16)
+        for mine in range(inner):
+
+            @pl.when(parity_ref[0] == mine)
+            def _():
+                for b in range(blocks):
+                    for e in range(slots):
+                        for h in range(heads):
+                            turned = d_bias_s[b, e, h].T.astype(BF16)
+                            at = (e * heads + h) * tile
+                            for sub in range(size // tile):
+                                col = b * (size // tile) + sub
+                                piece = turned[sub * tile : (sub + 1) * tile]
+                                if col % inner == mine:
+                                    keep_out[col // inner, at : at + tile, :] = piece
+                                else:
+                                    start = (col // inner) * each + at
+                                    message_out[start : start + tile, :] = piece
+
+
+def attention(
+    pieces, bias, w_all, w_out, tables, lens, owners, parity, carried, last, query_tile, inner
+):
     count = len(pieces)
-    _, columns, tile_rows, chan = pieces[0].shape
+    _, tile_rows, columns, chan = pieces[0].shape
     blocks, slots = tables.shape
     heads = bias.shape[2]
     proj = w_out.shape[0]
     size = tile_rows * count // blocks
     tokens = blocks * size
     together = math.gcd(TOGETHER, columns)
-    dims = (count, heads, proj // heads, blocks, size, slots, together)
+    dims = (count, heads, proj // heads, blocks, size, slots, together, inner)
     first = carried is None
+    all_width = columns + (0 if first else carried[0].shape[0] // tokens)
+    far = tokens // query_tile // inner
 
     def whole(x):
         return pl.BlockSpec(x.shape, lambda j, *_: (0,) * len(x.shape))
 
     sums = [
+        ((tokens * all_width, chan), F32),
         ((blocks, slots, heads, size, size), F32),
         ((2 * proj, chan), F32),
         ((chan, 2 * proj), F32),
         ((proj, chan), F32),
     ]
     if last:
-        results = [
-            ((tokens // query_tile, slots, heads, query_tile, size), BF16),
-            ((5, chan, proj), F32),
+        each = slots * heads * query_tile
+        results = [((tile_rows, all_width, chan), BF16)] * count + [
+            ((far, each, size), BF16),
+            ((far * each + 5 * chan, size), BF16),
+            ((5 * chan, proj), F32),
         ]
     else:
         results = sums
     results = [jax.ShapeDtypeStruct(*x) for x in results]
     scratch = [
+        ((2, tokens * columns, chan), F32),
         ((together, tokens, chan), BF16),
         ((together, tokens, chan), BF16),
         ((together, chan, tokens), BF16),
@@ -298,33 +339,154 @@
         ((together, blocks, size, 2 * proj), F32),
         ((together, blocks, proj, size), F32),
         ((together, blocks, proj, size), F32),
-        ((tokens, chan), F32),
     ]
     scratch = [pltpu.VMEM(*x) for x in (sums if last else []) + scratch]
     fixed = [bias, w_all, w_all.T, w_out] + ([] if first else list(carried))
     pairs = tokens * size * slots * heads
-    outs = pl.pallas_call(
+    operands = list(pieces) + fixed
+    return pl.pallas_call(
         functools.partial(attention_kernel, dims, first, last),
         grid_spec=pltpu.PrefetchScalarGridSpec(
-            num_scalar_prefetch=3,
+            num_scalar_prefetch=4,
             grid=(columns // together,),
-            in_specs=[
-                pl.BlockSpec((2, together, tile_rows, chan), lambda j, *_: (0, j, 0, 0))
-            ] * count
-            + [whole(x) for x in fixed],
-            out_specs=[pl.BlockSpec((together, tile_rows, chan), lambda j, *_: (j, 0, 0))] * count
-            + [whole(x) for x in results],
+            in_specs=[whole(x) for x in operands],
+            out_specs=[whole(x) for x in results],
             scratch_shapes=scratch,
         ),
-        out_shape=[jax.ShapeDtypeStruct((columns, tile_rows, chan), BF16)] * count + results,
+        out_shape=results,
         compiler_params=pltpu.CompilerParams(vmem_limit_bytes=VMEM_LIMIT),
         cost_estimate=pl.CostEstimate(
             flops=columns * pairs * 1200,
             bytes_accessed=columns * tokens * chan * 6 + 10 * 2**20,
             transcendentals=columns * pairs,
         ),
-    )(tables, lens, owners, *pieces, *fixed)
-    return outs[:count], outs[count:]
+    )(tables, lens, owners, parity, *operands)
+
+
+def small_call(body, scalars, arrays, results):
+    return pl.pallas_call(
+        body,
+        grid_spec=pltpu.PrefetchScalarGridSpec(
+            num_scalar_prefetch=len(scalars),
+            grid=(1,),
+            in_specs=[pl.BlockSpec(x.shape, lambda j, *_, n=x.ndim: (0,) * n) for x in arrays],
+            out_specs=[
+                pl.BlockSpec(x[0], lambda j, *_, n=len(x[0]): (0,) * n) for x in results
+            ],
+        ),
+        out_shape=[jax.ShapeDtypeStruct(*x) for x in results],
+        compiler_params=pltpu.CompilerParams(vmem_limit_bytes=VMEM_LIMIT),
+    )(*scalars, *arrays)
+
+
+def aligned(index, count):
+    return pl.ds(pl.multiple_of(index * count, count), count)
+
+
+def split_by_far(targets, keep, came, weights):
+    far, each, lanes = keep.shape
+    share = weights.shape[0] // far
+
+    def body(targets_ref, keep_ref, came_ref, weights_ref, own_ref, *message_refs):
+        for s in range(far):
+            t = targets_ref[s]
+            out = message_refs[s - 1] if s else own_ref
+            bias = keep_ref[t].astype(F32)
+            weight = weights_ref[aligned(t, share), :].astype(BF16).astype(F32)
+            if came_ref is not None:
+                bias += came_ref[aligned(t, each), :].astype(F32)
+                rest = came_ref[far * each :, :].astype(F32)
+                half = jnp.zeros_like(weight)
+                for u in range(far):
+                    half = jnp.where(t == u, rest[u * share : (u + 1) * share], half)
+                weight += half
+            out[:each, :] = bias.astype(out.dtype)
+            out[each:, :] = weight.astype(out.dtype)
+
+    results = [((each + share, lanes), F32 if s == 0 else BF16) for s in range(far)]
+    return small_call(body, [targets], [keep, came, weights], results)
+
+
+def split_by_row(owners, chosen, live, own, came, dims):
+    rows, slots, per_block, each = dims
+    lanes = own.shape[1]
+    part = each // slots
+    share = own.shape[0] - each
+
+    def body(owners_ref, chosen_ref, live_ref, own_ref, *refs):
+        came_refs, outs = refs[: len(came)], refs[len(came) :]
+        weight = own_ref[each:, :]
+        for ref in came_refs:
+            weight += ref[each:, :].astype(F32)
+        for s in range(rows):
+            outs[s][part:, :] = weight.astype(BF16).astype(outs[s].dtype)
+            outs[s][:part, :] = jnp.zeros((part, lanes), outs[s].dtype)
+        for e in range(slots):
+            at = slice(e * part, (e + 1) * part)
+            bias = own_ref[at, :]
+            for ref in came_refs:
+                bias += ref[at, :].astype(F32)
+            for s in range(rows):
+                hit = (chosen_ref[e] == owners_ref[s] // per_block) & (e < live_ref[0])
+
+                @pl.when(hit)
+                def _():
+                    outs[s][:part, :] = bias.astype(outs[s].dtype)
+
+    results = [((part + share, lanes), F32 if s == 0 else BF16) for s in range(rows)]
+    return small_call(body, [owners, chosen, live], [own, *came], results)
+
+
+def add_rows(own, came, part):
+    share, lanes = own.shape[0] - part, own.shape[1]
+
+    def body(own_ref, *refs):
+        came_refs, (bias_ref, weight_ref) = refs[: len(came)], refs[len(came) :]
+        terms = [own_ref[...]] + [ref[...].astype(F32) for ref in came_refs]
+        while len(terms) > 1:
+            terms = [sum(terms[n : n + 2]) for n in range(0, len(terms), 2)]
+        total = terms[0]
+        bias_ref[...] = total[:part]
+        weight_ref[...] = total[part:].astype(BF16)
+
+    results = [((part, lanes), F32), ((share, lanes), BF16)]
+    return small_call(body, [], [own, *came], results)
+
+
+def place_weights(sources, parts, count):
+    share, lanes = parts[0].shape
+
+    def body(sources_ref, *refs):
+        part_refs, out_refs, scratch = refs[: len(parts)], refs[len(parts) : -1], refs[-1]
+        for s, ref in enumerate(part_refs):
+            scratch[aligned(sources_ref[s], share), :] = ref[...].astype(F32)
+        for n, ref in enumerate(out_refs):
+            ref[...] = scratch[n * lanes : (n + 1) * lanes, :]
+
+    rows = share * len(parts)
+    shape = (rows // count, lanes)
+    return pl.pallas_call(
+        body,
+        grid_spec=pltpu.PrefetchScalarGridSpec(
+            num_scalar_prefetch=1,
+            grid=(1,),
+            in_specs=[pl.BlockSpec(x.shape, lambda j, *_: (0, 0)) for x in parts],
+            out_specs=[pl.BlockSpec(shape, lambda j, *_: (0, 0))] * count,
+            scratch_shapes=[pltpu.VMEM((rows, lanes), F32)],
+        ),
+        out_shape=[jax.ShapeDtypeStruct(shape, F32)] * count,
+    )(sources, *parts)
+
+
+def place_pair(groups, pieces):
+    tile_rows, width, chan = pieces[0].shape
+
+    def body(groups_ref, *refs):
+        for s, ref in enumerate(refs[:-1]):
+            refs[-1][:, groups_ref[s]] = ref[...]
+
+    out = small_call(body, [groups], pieces, [((tile_rows, len(pieces), width, chan), BF16)])[0]
+    return out.reshape(tile_rows, len(pieces) * width, chan)
 
 
 class Peers:
@@ -364,27 +526,14 @@
     def gather(self, x):
         return jnp.stack([self.send(x, s) for s in range(self.count)])
 
-    def scatter_sum(self, parts):
-        total = None
-        for s in range(self.count):
-            mine = [lax.dynamic_index_in_dim(p, self.target(s), 0, keepdims=False) for p in parts]
-            total = self.add(total, mine, s)
-        return total
-
-    def add(self, total, parts, s):
-        width = parts[0].shape[-1]
-        if s and all(p.shape[-1] == width for p in parts):
-            joined = jnp.concatenate([p.reshape(-1, width).astype(BF16) for p in parts])
-            joined = self.send(joined, s)
-            came, at = [], 0
-            for p in parts:
-                rows = p.size // width
-                came.append(joined[at : at + rows].reshape(p.shape))
-                at += rows
-        else:
-            came = [self.send(p.astype(BF16), s) if s else p for p in parts]
-        came = [x.astype(F32) for x in came]
-        return came if total is None else [t + x for t, x in zip(total, came)]
+    def targets(self):
+        return jnp.stack([self.target(s) for s in range(self.count)]).astype(jnp.int32)
+
+    def sources(self):
+        return jnp.stack([self.source(s) for s in range(self.count)]).astype(jnp.int32)
+
+    def swap(self, messages):
+        return [self.send(x, s + 1) for s, x in enumerate(messages)]
 
 
 def on_device(
@@ -419,53 +568,43 @@
         rows.positions().astype(jnp.int32),
     )
 
-    both = jnp.stack([pair_act, out_grad]).reshape(2, tile_rows, row_count, chunks, width, chan)
-    both = jnp.transpose(both, (2, 3, 0, 4, 1, 5))
-    owners = jnp.stack([rows.source(s) for s in range(row_count)]).astype(jnp.int32)
+    owners = rows.sources()
+    parity = near.targets()[:1]
     w_all = jnp.concatenate([w_query, w_key, w_value, w_gate], axis=1)
-    outgoing = [
-        lax.dynamic_index_in_dim(both, rows.target(s), 0, keepdims=False) for s in range(row_count)
-    ]
+
+    def piece(s, c):
+        at = rows.target(s) * col_width + c * width
+        cut = lambda x: lax.dynamic_slice_in_dim(x, at, width, 1)
+        return rows.send(jnp.stack([cut(pair_act), cut(out_grad)]), s)
+
     carried = None
-    returned = []
     for c in range(chunks):
-        pieces = [rows.send(outgoing[s][c], s) for s in range(row_count)]
-        d_pieces, carried = attention(
-            pieces, bias, w_all, w_out, key_blocks, list_len, owners, carried,
-            c == chunks - 1, query_tile,
+        pieces = [piece(s, c) for s in range(row_count)]
+        carried = attention(
+            pieces, bias, w_all, w_out, key_blocks, list_len, owners, parity, carried,
+            c == chunks - 1, query_tile, inner,
         )
-        returned.append(jnp.stack([rows.send(d_pieces[s], s, home=True) for s in range(row_count)]))
-
-    d_pair = jnp.stack(returned, axis=1)
-    steps = jnp.arange(row_count)
-    order = rows.digit ^ steps if rows.paired else (steps - rows.digit) % row_count
-    d_pair = jnp.take(d_pair, order, axis=0)
-    d_pair = jnp.transpose(d_pair, (3, 0, 1, 2, 4)).reshape(tile_rows, tile_cols, chan)
-
-    slot_bias, w_part = carried
-    weights = w_part.shape[0]
-    w_part = w_part.reshape(col_count // inner, inner, -1, proj)
-    slot_bias = slot_bias.reshape((col_count // inner, inner) + slot_bias.shape[1:])
-    parts = near.scatter_sum([jnp.moveaxis(slot_bias, 1, 0), jnp.moveaxis(w_part, 1, 0)])
-    slot_bias, w_part = far.scatter_sum(parts)
+    *d_pieces, keep, message, w_part = carried
+    far_targets, row_targets = far.targets(), rows.targets()
+
+    each = keep.shape[1]
+    own, *messages = split_by_far(far_targets, keep, near.send(message, inner - 1), w_part)
+    came = far.swap(messages)
     block = lax.axis_index("col") * query_tile // size
     chosen = lax.dynamic_index_in_dim(key_blocks, block, 0, keepdims=False)
-    live = jnp.arange(slots) < lax.dynamic_index_in_dim(list_len, block, 0, keepdims=False)
+    live = lax.dynamic_slice_in_dim(list_len, block, 1)
     per_block = size // tile_rows
-    slot_bias = slot_bias.reshape(slots, heads, query_tile, per_block, tile_rows)
-
-    total = None
-    for s in range(row_count):
-        owner = rows.target(s)
-        piece = lax.dynamic_index_in_dim(slot_bias, owner % per_block, 3, keepdims=False)
-        hit = (chosen == owner // per_block) & live
-        piece = jnp.sum(jnp.where(hit[:, None, None, None], piece, 0.0), axis=0)
-        total = rows.add(total, [piece, w_part], s)
-    d_bias, w_part = total
-    w_sum = near.gather(far.gather(w_part.astype(BF16)))
-    w_sum = jnp.take(jnp.take(w_sum, near.positions(), axis=0), far.positions(), axis=1)
-    w_sum = jnp.moveaxis(w_sum, 0, 1).reshape(weights, chan, proj).astype(F32)
-    return (d_pair, jnp.transpose(d_bias, (0, 2, 1))) + tuple(w_sum[n] for n in range(weights))
+    own, *messages = split_by_row(
+        row_targets, chosen, live, own, came, (row_count, slots, per_block, each)
+    )
+    d_bias, w_part = add_rows(own, rows.swap(messages), each // slots)
+    weights = place_weights(far.sources(), [far.send(w_part, s) for s in range(far.count)], 5)
+    d_bias = d_bias.reshape(heads, query_tile, per_block, tile_rows)
+    d_bias = lax.dynamic_index_in_dim(d_bias, rows.digit % per_block, 2, keepdims=False)
+
+    d_pieces = [rows.send(x, s, home=True) for s, x in enumerate(d_pieces)]
+    d_pair = place_pair(row_targets, d_pieces)
+    return (d_pair, jnp.transpose(d_bias, (0, 2, 1)), *weights)
 
 
 def solution(mesh):

time: 208 us -> 225 us (1.082)
  Pallas kernels: 91.9 us -> 126 us
  local copies, waits for them, and re-layouts: 24 us -> 16.5 us
  starting transfers between devices: 38.7 us -> 34 us
  waiting for transfers between devices: 41 us -> 37.5 us
    pallas_call x2, Pallas kernels: 86 us -> 106 us  [attention(): pl.pallas_call(functools.partial(attention_kernel, dims, first, last), gr...]
    pallas_call x0 -> x5, Pallas kernels: none -> 14.8 us  [the longest x4 12.5 us: small_call(): pl.pallas_call(body, grid_spec=pltpu.PrefetchScalarGridSpec(num_scalar_pr...]
    another operation x4 -> x10, other arithmetic: 2.42 us -> 8.94 us  [the longest x8 7.71 us: piece(): return rows.send(jnp.stack([cut(pair_act), cut(out_grad)]), s)]
    ppermute x30 -> x26, starting transfers between devices: 38.7 us -> 34 us  [send(): return x if s == 0 else lax.ppermute(x, self.axis, route)]
    squeeze x5 -> x1, local copies, waits for them, and re-layouts: 5.06 us -> 1.2 us  [on_device(): chosen = lax.dynamic_index_in_dim(key_blocks, block, 0, keepdims=False)]
    gather x3 -> x0, local copies, waits for them, and re-layouts: 3.7 us -> none  [the longest x1 2.54 us: on_device(): d_pair = jnp.take(d_pair, order, axis=0)]
    ppermute x30 -> x26, waiting for transfers between devices: 41 us -> 37.5 us  [send(): return x if s == 0 else lax.ppermute(x, self.axis, route)]
    dynamic_slice x1 -> x0, other arithmetic: 2.9 us -> none  [on_device(): lax.dynamic_index_in_dim(both, rows.target(s), 0, keepdims=False)]
  transfers between devices with their start and end apart: 30 -> 26, of which waited for: 9 -> 7; matrix products, arithmetic and copies ran while one was open for 15% -> 10% of each run, Pallas kernels for 23% -> 29%
where the time goes in v3:
time: 225 us; the launch traced here: 229 us
  Pallas kernels  126 us (56%)
  waiting for transfers between devices  37.5 us (17%)
  starting transfers between devices  34 us (15%)
  local copies, waits for them, and re-layouts  16.5 us (7%)
  other arithmetic  13.5 us (6%)
    pallas_call x2, Pallas kernels, attention(): pl.pallas_call(functools.partial(attention_kernel, dims, first, last), gr...  106 us
    ppermute x26, waiting for transfers between devices, send(): return x if s == 0 else lax.ppermute(x, self.axis, route)  37.5 us
    ppermute x26, starting transfers between devices, send(): return x if s == 0 else lax.ppermute(x, self.axis, route)  34 us
    pallas_call x4, Pallas kernels, small_call(): pl.pallas_call(body, grid_spec=pltpu.PrefetchScalarGridSpec(num_scalar_pr...  12.5 us
    unnamed x70, local copies, waits for them, and re-layouts  9.11 us
    another operation x8, other arithmetic, piece(): return rows.send(jnp.stack([cut(pair_act), cut(out_grad)]), s)  7.71 us
    pallas_call x1, Pallas kernels, shifted_bias(): pl.pallas_call(bias_kernel, grid_spec=pltpu.PrefetchScalarGridSpec(num_sc...  5.87 us
  transfers between devices with their start and end apart: 26, of which 7 were waited for; matrix products, arithmetic and copies ran while one was open for 10% of the time, Pallas kernels for 29%

profile of v3, /device:TPU:0, one launch (start us, length us, event | category | flops | bytes accessed | tf_op | source)
XLA Modules:
  0.0 228.5 jit_solution(7541412702310420739)
XLA Ops:
  0.6 3.0 %collective-permute-start.3 = (bf16[4,64,128]{2,1,0:T(8,128)(2,1)}, bf16[4,64,128]{2,1,0:T(8,128)(2,1)S(1)}, u32[]{:S(2)}, u32[]{:S(2)}) collective-permute-start(bf16[4,64,128]{2,1,0:T(8,128)(2,1)} %bitcast.75), channel_id=1, source_target_pairs={{0,8},{8,0},{16,24},{24,16},{1,9},{9,1},{17,25},{25,17},{2,10},{10... | collective-permute-start | bytes 196616 | tf_op jit(solution)/shard_map/ppermute | solution.py:520
  3.6 1.5 collective-permute-start.4
  5.2 3.5 %dynamic-slice_bitcast_fusion = (bf16[1,128,8,128]{3,2,1,0:T(8,128)(2,1)S(1)}, bf16[1,128,8,128]{3,2,1,0:T(8,128)(2,1)S(1)}, bf16[1,128,8,128]{3,2,1,0:T(8,128)(...) fusion(bf16[128,64,128]{2,1,0:T(8,128)(2,1)} %param.11, ...), kind=kLoop, calls=%fused_computation.13 | loop fusion | bytes 8388640 | tf_op jit(solution)/shard_map/stack | solution.py:578
  8.8 0.8 pad_maximum_fusion.7
  9.6 1.9 collective-permute-start.10
  11.5 0.8 pad_maximum_fusion.8
  12.4 1.5 collective-permute-start.11
  14.6 1.6 collective-permute-start.6
  16.2 2.6 %collective-permute-start.7 = (bf16[4,4,64,128]{3,2,1,0:T(8,128)(2,1)S(1)}, bf16[4,4,64,128]{3,2,1,0:T(8,128)(2,1)S(1)}, u32[]{:S(2)}, u32[]{:S(2)}) collective-permute-start(bf16[4,4,64,128]{3,2,1,0:T(8,128)(2,1)S(1)} %get-tuple-element.80), channel_id=1, source_target_pairs={{0,4},{1,5},{2,6},{3,7},{4,0},{5,1},{6,2},{7,3},{8,12},{9,13},{10,... | collective-permute-start | bytes 786440 | tf_op jit(solution)/shard_map/ppermute | solution.py:520
  22.0 0.9 pad_maximum_fusion.9
  22.9 0.8 pad_maximum_fusion.5
  23.7 1.5 collective-permute-done.6
  25.5 12.1 %collective-permute-done.7 = bf16[4,4,64,128]{3,2,1,0:T(8,128)(2,1)S(1)} collective-permute-done((bf16[4,4,64,128]{3,2,1,0:T(8,128)(2,1)S(1)}, bf16[4,4,64,128]{3,2,1,0:T(8,128)(2,1)S(1)}, u32[]{:S(2)}, u32[]{:S(2)}) %collective-permute-start.7) | collective-permute-done | bytes 262176 | tf_op jit(solution)/shard_map/ppermute | solution.py:520
  38.8 1.2 fusion.5
  40.8 0.8 pad_maximum_fusion.6.refs_0_
  41.7 0.9 pad_maximum_fusion.4
  42.5 0.8 pad_maximum_fusion.3
  44.0 0.8 copy.28.refs_5_
  46.0 1.8 pad_maximum_fusion.2.refs_0_
  48.4 1.5 collective-permute-start.1
  49.9 1.5 pad_maximum_fusion
  51.4 5.9 %shard_map.153.refs_4_ = f32[4,4,4,128,128]{4,3,2,1,0:T(8,128)} custom-call(s32[4,3]{1,0:T(4,128)} %tables_ref.5, s32[4]{0:T(128)} %lens_ref.5, s32[8]{0:T(128)} %multiply_add_fusion.col_pos_ref, s32[4]{0:T(128)} %iota_xor_fusion.row_pos_ref, bf16[8,4,4,64,128]{4,3,2,1,0:T(8,128)(2,1)} %bitcast.68, bf16[8,4,4,64,128]{4,3,2,1,0:T(8,128)(2,1)} %bitcast.69), custom_call_target="tpu_custom_call" | custom-call | tf_op jit(solution)/shard_map/pallas_call | solution.py:58
  57.3 1.6 collective-permute-start
  58.8 50.4 %shard_map.154 = (f32[4096,128]{1,0:T(8,128)}, f32[4,3,4,128,128]{4,3,2,1,0:T(8,128)}, f32[256,128]{1,0:T(8,128)}, f32[128,256]{1,0:T(8,128)}, f32[128,128]{1,0:T(8,128)}) custom-call(s32[4,3]{1,0:T(4,128)} %tables_ref.5, s32[4]{0:T(128)} %lens_ref.5, s32[4]{0:T(128)} %pad_add_fusion.owners_ref.groups_ref, s32[1]{0:T(128)} %bitcast.4.parity_ref, ...), custom_call_target="tpu_custom_call" | custom-call | flops 7549747200 | bytes 13631488 | tf_op jit(solution)/shard_map/pallas_call | solution.py:347
  109.2 0.8 copy-done.31
  110.2 55.2 %shard_map.155 = (bf16[128,16,128]{2,1,0:T(8,128)(2,1)}, bf16[128,16,128]{2,1,0:T(8,128)(2,1)}, bf16[128,16,128]{2,1,0:T(8,128)(2,1)}, bf16[128,16,128]{2,1,0:T(...) custom-call(s32[4,3]{1,0:T(4,128)} %tables_ref.5, s32[4]{0:T(128)} %lens_ref.5, ...), custom_call_target="tpu_custom_call" | custom-call | flops 7549747200 | bytes 13631488 | tf_op jit(solution)/shard_map/pallas_call | solution.py:347
  166.1 2.1 collective-permute-done.16.came_ref
  168.2 0.9 copy-done.6
  169.1 3.4 %shard_map.157 = (f32[928,128]{1,0:T(8,128)}, bf16[928,128]{1,0:T(8,128)(2,1)}, bf16[928,128]{1,0:T(8,128)(2,1)}, bf16[928,128]{1,0:T(8,128)(2,1)}) custom-call(s32[4]{0:T(128)} %pad_add_fusion.1.targets_ref.sources_ref, bf16[4,768,128]{2,1,0:T(8,128)(2,1)} %get-tuple-element.43.keep_ref, bf16[3712,128]{1,0:T(8,128)(2,1)} %copy-done.6, ...), custom_call_target="tpu_custom_call" | custom-call | tf_op jit(solution)/shard_map/pallas_call | solution.py:367
  172.9 1.5 collective-permute-start.13
  174.4 1.5 collective-permute-start.14
  176.4 2.0 collective-permute-start.18
  178.5 4.3 %collective-permute-done.17.refs_0_ = bf16[928,128]{1,0:T(8,128)(2,1)S(1)} collective-permute-done((bf16[928,128]{1,0:T(8,128)(2,1)}, bf16[928,128]{1,0:T(8,128)(2,1)S(1)}, u32[]{:S(2)}, u32[]{:S(2)}) %collective-permute-start.17) | collective-permute-done | bytes 237600 | tf_op jit(solution)/shard_map/ppermute | solution.py:520
  182.8 0.9 collective-permute-start.19
  184.3 1.2 fusion.2.chosen_ref
  185.5 11.0 %collective-permute-done.18.refs_1_ = bf16[928,128]{1,0:T(8,128)(2,1)S(1)} collective-permute-done((bf16[928,128]{1,0:T(8,128)(2,1)}, bf16[928,128]{1,0:T(8,128)(2,1)S(1)}, u32[]{:S(2)}, u32[]{:S(2)}) %collective-permute-start.18) | collective-permute-done | bytes 237600 | tf_op jit(solution)/shard_map/ppermute | solution.py:520
  197.2 3.6 %shard_map.158 = (f32[416,128]{1,0:T(8,128)}, bf16[416,128]{1,0:T(8,128)(2,1)}, bf16[416,128]{1,0:T(8,128)(2,1)}, bf16[416,128]{1,0:T(8,128)(2,1)}) custom-call(s32[4]{0:T(128)} %pad_add_fusion.owners_ref.groups_ref, s32[3]{0:T(128)} %fusion.2.chosen_ref, s32[1]{0:T(128)} %dynamic_slice.74.live_ref, f32[928,128]{1,0:T(8,128)} %get-tuple-element.46.own_ref, ...), custom_call_target="tpu_custom_call" | custom-call | tf_op jit(solution)/shard_map/pallas_call | solution.py:367
  200.8 1.5 collective-permute-start.20
  202.3 1.5 collective-permute-start.21
  203.8 2.7 %collective-permute-done.20.refs_0_ = bf16[416,128]{1,0:T(8,128)(2,1)S(1)} collective-permute-done((bf16[416,128]{1,0:T(8,128)(2,1)}, bf16[416,128]{1,0:T(8,128)(2,1)S(1)}, u32[]{:S(2)}, u32[]{:S(2)}) %collective-permute-start.20) | collective-permute-done | bytes 106528 | tf_op jit(solution)/shard_map/ppermute | solution.py:520
  206.5 2.2 collective-permute-start.22
  208.7 3.7 %collective-permute-done.22.refs_2_ = bf16[416,128]{1,0:T(8,128)(2,1)S(1)} collective-permute-done((bf16[416,128]{1,0:T(8,128)(2,1)}, bf16[416,128]{1,0:T(8,128)(2,1)S(1)}, u32[]{:S(2)}, u32[]{:S(2)}) %collective-permute-start.22) | collective-permute-done | bytes 106528 | tf_op jit(solution)/shard_map/ppermute | solution.py:520
  213.0 1.8 shard_map.159
  214.8 3.0 %collective-permute-start.23 = (bf16[160,128]{1,0:T(8,128)(2,1)}, bf16[160,128]{1,0:T(8,128)(2,1)S(1)}, u32[]{:S(2)}, u32[]{:S(2)}) collective-permute-start(bf16[160,128]{1,0:T(8,128)(2,1)} %get-tuple-element.55.refs_0_), channel_id=1, source_target_pairs={{0,2},{1,3},{2,0},{3,1},{4,6},{5,7},{6,4},{7,5},{8,10},{9,11},{10,... | collective-permute-start | bytes 122888 | tf_op jit(solution)/shard_map/ppermute | solution.py:520
  217.8 1.0 collective-permute-start.24
  218.8 1.5 collective-permute-start.25
  221.3 3.8 %shard_map.156 = bf16[128,4,16,128]{3,2,1,0:T(8,128)(2,1)} custom-call(s32[4]{0:T(128)} %pad_add_fusion.owners_ref.groups_ref, bf16[128,16,128]{2,1,0:T(8,128)(2,1)} %get-tuple-element.39.refs_0_, bf16[128,16,128]{2,1,0:T(8,128)(2,1)} %copy-done.7, bf16[128,16,128]{2,1,0:T(8,128)(2,1)} %copy-done.8, bf16[128,16,128]{2,1,0:T(8,128)(2,1)} %copy-done.9), custom_call_target="tpu_custom_call" | custom-call | tf_op jit(solution)/shard_map/pallas_call | solution.py:367
  226.3 2.2 shard_map.160
  (109 shorter events, 14.5 us)
Async XLA Ops:
  0.6 13.9 %collective-permute-start.3 = (bf16[4,64,128]{2,1,0:T(8,128)(2,1)}, bf16[4,64,128]{2,1,0:T(8,128)(2,1)S(1)}, u32[]{:S(2)}, u32[]{:S(2)}) collective-permute-start(bf16[4,64,128]{2,1,0:T(8,128)(2,1)} %bitcast.75), channel_id=1, source_target_pairs={{0,8},{8,0},{16,24},{24,16},{1,9},{9,1},{17,25},{25,17},{2,10},{10... | collective-permute-start | bytes 196616 | tf_op jit(solution)/shard_map/ppermute | solution.py:520
  3.6 10.9 %collective-permute-start.4 = (bf16[4,64,128]{2,1,0:T(8,128)(2,1)}, bf16[4,64,128]{2,1,0:T(8,128)(2,1)S(1)}, u32[]{:S(2)}, u32[]{:S(2)}) collective-permute-start(bf16[4,64,128]{2,1,0:T(8,128)(2,1)} %bitcast.76), channel_id=1, source_target_pairs={{0,16},{8,24},{16,0},{24,8},{1,17},{9,25},{17,1},{25,9},{2,18},{10... | collective-permute-start | bytes 196616 | tf_op jit(solution)/shard_map/ppermute | solution.py:520
  5.2 9.4 %collective-permute-start.5 = (bf16[4,64,128]{2,1,0:T(8,128)(2,1)}, bf16[4,64,128]{2,1,0:T(8,128)(2,1)S(1)}, u32[]{:S(2)}, u32[]{:S(2)}) collective-permute-start(bf16[4,64,128]{2,1,0:T(8,128)(2,1)} %bitcast.77), channel_id=1, source_target_pairs={{0,24},{8,16},{16,8},{24,0},{1,25},{9,17},{17,9},{25,1},{2,26},{10... | collective-permute-start | bytes 196616 | tf_op jit(solution)/shard_map/ppermute | solution.py:520
  8.7 5.8 %copy-start.22 = (bf16[4,128,64]{1,2,0:T(8,128)(2,1)S(1)}, bf16[4,128,64]{1,2,0:T(8,128)(2,1)}, u32[]{:S(2)}) copy-start(bf16[4,128,64]{1,2,0:T(8,128)(2,1)} %param.12) | copy-start | bytes 196612
  8.7 10.4 %copy-start.26 = (bf16[128,128]{1,0:T(8,128)(2,1)S(1)}, bf16[128,128]{1,0:T(8,128)(2,1)}, u32[]{:S(2)}) copy-start(bf16[128,128]{1,0:T(8,128)(2,1)} %param.13) | copy-start | bytes 98308
  8.7 11.1 %copy-start.27 = (bf16[128,128]{1,0:T(8,128)(2,1)S(1)}, bf16[128,128]{1,0:T(8,128)(2,1)}, u32[]{:S(2)}) copy-start(bf16[128,128]{1,0:T(8,128)(2,1)} %param.14) | copy-start | bytes 98308
  8.7 11.8 %copy-start.28 = (bf16[128,128]{1,0:T(8,128)(2,1)S(1)}, bf16[128,128]{1,0:T(8,128)(2,1)}, u32[]{:S(2)}) copy-start(bf16[128,128]{1,0:T(8,128)(2,1)} %param.15) | copy-start | bytes 98308
  8.7 12.5 %copy-start.29 = (bf16[128,128]{1,0:T(8,128)(2,1)S(1)}, bf16[128,128]{1,0:T(8,128)(2,1)}, u32[]{:S(2)}) copy-start(bf16[128,128]{1,0:T(8,128)(2,1)} %param.16) | copy-start | bytes 98308
  9.6 47.7 %collective-permute-start.10 = (bf16[2,128,8,128]{3,2,1,0:T(8,128)(2,1)}, bf16[2,128,8,128]{3,2,1,0:T(8,128)(2,1)}, u32[]{:S(2)}, u32[]{:S(2)}) collective-permute-start(bf16[2,128,8,128]{3,2,1,0:T(8,128)(2,1)} %pad_maximum_fusion.7), channel_id=1, source_target_pairs={{0,8},{8,0},{16,24},{24,16},{1,9},{9,1},{17,25},{25,17},{2,10},{10... | collective-permute-start | bytes 1572872 | tf_op jit(solution)/shard_map/ppermute | solution.py:520
  12.4 46.5 %collective-permute-start.11 = (bf16[2,128,8,128]{3,2,1,0:T(8,128)(2,1)}, bf16[2,128,8,128]{3,2,1,0:T(8,128)(2,1)}, u32[]{:S(2)}, u32[]{:S(2)}) collective-permute-start(bf16[2,128,8,128]{3,2,1,0:T(8,128)(2,1)} %pad_maximum_fusion.8), channel_id=1, source_target_pairs={{0,16},{8,24},{16,0},{24,8},{1,17},{9,25},{17,1},{25,9},{2,18},{10... | collective-permute-start | bytes 1572872 | tf_op jit(solution)/shard_map/ppermute | solution.py:520
  14.6 10.6 %collective-permute-start.6 = (bf16[4,4,64,128]{3,2,1,0:T(8,128)(2,1)S(1)}, bf16[4,4,64,128]{3,2,1,0:T(8,128)(2,1)S(1)}, u32[]{:S(2)}, u32[]{:S(2)}) collective-permute-start(bf16[4,4,64,128]{3,2,1,0:T(8,128)(2,1)S(1)} %get-tuple-element.80), channel_id=1, source_target_pairs={{0,2},{1,3},{2,0},{3,1},{4,6},{5,7},{6,4},{7,5},{8,10},{9,11},{10,... | collective-permute-start | bytes 786440 | tf_op jit(solution)/shard_map/ppermute | solution.py:520
  16.2 21.4 %collective-permute-start.7 = (bf16[4,4,64,128]{3,2,1,0:T(8,128)(2,1)S(1)}, bf16[4,4,64,128]{3,2,1,0:T(8,128)(2,1)S(1)}, u32[]{:S(2)}, u32[]{:S(2)}) collective-permute-start(bf16[4,4,64,128]{3,2,1,0:T(8,128)(2,1)S(1)} %get-tuple-element.80), channel_id=1, source_target_pairs={{0,4},{1,5},{2,6},{3,7},{4,0},{5,1},{6,2},{7,3},{8,12},{9,13},{10,... | collective-permute-start | bytes 786440 | tf_op jit(solution)/shard_map/ppermute | solution.py:520
  18.8 19.2 %collective-permute-start.8 = (bf16[4,4,64,128]{3,2,1,0:T(8,128)(2,1)S(1)}, bf16[4,4,64,128]{3,2,1,0:T(8,128)(2,1)S(1)}, u32[]{:S(2)}, u32[]{:S(2)}) collective-permute-start(bf16[4,4,64,128]{3,2,1,0:T(8,128)(2,1)S(1)} %get-tuple-element.80), channel_id=1, source_target_pairs={{0,6},{1,7},{2,4},{3,5},{4,2},{5,3},{6,0},{7,1},{8,14},{9,15},{10,... | collective-permute-start | bytes 786440 | tf_op jit(solution)/shard_map/ppermute | solution.py:520
  22.8 17.3 %copy-start.15 = (bf16[128,128]{0,1:T(8,128)(2,1)S(1)}, bf16[128,128]{0,1:T(8,128)(2,1)}, u32[]{:S(2)}) copy-start(bf16[128,128]{0,1:T(8,128)(2,1)} %copy.23) | copy-start | bytes 98308
  22.8 17.3 %copy-start.16 = (bf16[128,128]{0,1:T(8,128)(2,1)S(1)}, bf16[128,128]{0,1:T(8,128)(2,1)}, u32[]{:S(2)}) copy-start(bf16[128,128]{0,1:T(8,128)(2,1)} %copy.24) | copy-start | bytes 98308
  22.8 17.3 %copy-start.17 = (bf16[128,128]{0,1:T(8,128)(2,1)S(1)}, bf16[128,128]{0,1:T(8,128)(2,1)}, u32[]{:S(2)}) copy-start(bf16[128,128]{0,1:T(8,128)(2,1)} %copy.25) | copy-start | bytes 98308
  22.8 17.3 %copy-start.18 = (bf16[128,128]{0,1:T(8,128)(2,1)S(1)}, bf16[128,128]{0,1:T(8,128)(2,1)}, u32[]{:S(2)}) copy-start(bf16[128,128]{0,1:T(8,128)(2,1)} %copy.26) | copy-start | bytes 98308
  22.8 18.0 %copy-start.4 = (bf16[1,128,8,128]{3,2,1,0:T(8,128)(2,1)S(1)}, bf16[1,128,8,128]{3,2,1,0:T(8,128)(2,1)}, u32[]{:S(2)}) copy-start(bf16[1,128,8,128]{3,2,1,0:T(8,128)(2,1)} %get-tuple-element.71) | copy-start | bytes 786436
  22.8 18.0 %copy-start.5 = (bf16[1,128,8,128]{3,2,1,0:T(8,128)(2,1)S(1)}, bf16[1,128,8,128]{3,2,1,0:T(8,128)(2,1)}, u32[]{:S(2)}) copy-start(bf16[1,128,8,128]{3,2,1,0:T(8,128)(2,1)} %get-tuple-element.90) | copy-start | bytes 786436
  25.2 33.6 %collective-permute-start.12 = (bf16[2,128,8,128]{3,2,1,0:T(8,128)(2,1)}, bf16[2,128,8,128]{3,2,1,0:T(8,128)(2,1)}, u32[]{:S(2)}, u32[]{:S(2)}) collective-permute-start(bf16[2,128,8,128]{3,2,1,0:T(8,128)(2,1)} %pad_maximum_fusion.9), channel_id=1, source_target_pairs={{0,24},{8,16},{16,8},{24,0},{1,25},{9,17},{17,9},{25,1},{2,26},{10... | collective-permute-start | bytes 1572872 | tf_op jit(solution)/shard_map/ppermute | solution.py:520
  37.6 71.6 %collective-permute-start.2 = (bf16[2,128,8,128]{3,2,1,0:T(8,128)(2,1)}, bf16[2,128,8,128]{3,2,1,0:T(8,128)(2,1)}, u32[]{:S(2)}, u32[]{:S(2)}) collective-permute-start(bf16[2,128,8,128]{3,2,1,0:T(8,128)(2,1)} %pad_maximum_fusion.5), channel_id=1, source_target_pairs={{0,24},{8,16},{16,8},{24,0},{1,25},{9,17},{17,9},{25,1},{2,26},{10... | collective-permute-start | bytes 1572872 | tf_op jit(solution)/shard_map/ppermute | solution.py:520
  38.8 2.9 %copy-start.2 = (bf16[1,128,8,128]{3,2,1,0:T(8,128)(2,1)S(1)}, bf16[1,128,8,128]{3,2,1,0:T(8,128)(2,1)}, u32[]{:S(2)}) copy-start(bf16[1,128,8,128]{3,2,1,0:T(8,128)(2,1)} %get-tuple-element.73) | copy-start | bytes 786436
  38.8 2.9 %copy-start.3 = (bf16[1,128,8,128]{3,2,1,0:T(8,128)(2,1)S(1)}, bf16[1,128,8,128]{3,2,1,0:T(8,128)(2,1)}, u32[]{:S(2)}) copy-start(bf16[1,128,8,128]{3,2,1,0:T(8,128)(2,1)} %get-tuple-element.88) | copy-start | bytes 786436
  38.8 3.7 %copy-start = (bf16[1,128,8,128]{3,2,1,0:T(8,128)(2,1)S(1)}, bf16[1,128,8,128]{3,2,1,0:T(8,128)(2,1)}, u32[]{:S(2)}) copy-start(bf16[1,128,8,128]{3,2,1,0:T(8,128)(2,1)} %get-tuple-element.74) | copy-start | bytes 786436
  38.8 3.7 %copy-start.1 = (bf16[1,128,8,128]{3,2,1,0:T(8,128)(2,1)S(1)}, bf16[1,128,8,128]{3,2,1,0:T(8,128)(2,1)}, u32[]{:S(2)}) copy-start(bf16[1,128,8,128]{3,2,1,0:T(8,128)(2,1)} %get-tuple-element.87) | copy-start | bytes 786436
  40.0 8.4 %collective-permute-start.9 = (bf16[4,4,4,64,128]{4,3,2,1,0:T(8,128)(2,1)S(1)}, bf16[4,4,4,64,128]{4,3,2,1,0:T(8,128)(2,1)S(1)}, u32[]{:S(2)}, u32[]{:S(2)}) collective-permute-start(bf16[4,4,4,64,128]{4,3,2,1,0:T(8,128)(2,1)S(1)} %get-tuple-element.78), channel_id=1, source_target_pairs={{0,1},{1,0},{2,3},{3,2},{4,5},{5,4},{6,7},{7,6},{8,9},{9,8},{10,11... | collective-permute-start | bytes 3145736 | tf_op jit(solution)/shard_map/ppermute | solution.py:520
  48.4 60.8 %collective-permute-start.1 = (bf16[2,128,8,128]{3,2,1,0:T(8,128)(2,1)}, bf16[2,128,8,128]{3,2,1,0:T(8,128)(2,1)S(1)}, u32[]{:S(2)}, u32[]{:S(2)}) collective-permute-start(bf16[2,128,8,128]{3,2,1,0:T(8,128)(2,1)} %pad_maximum_fusion.4), channel_id=1, source_target_pairs={{0,16},{8,24},{16,0},{24,8},{1,17},{9,25},{17,1},{25,9},{2,18},{10... | collective-permute-start | bytes 1572872 | tf_op jit(solution)/shard_map/ppermute | solution.py:520
  51.4 5.9 %copy-start.10 = (bf16[2,128,8,128]{3,2,1,0:T(8,128)(2,1)S(1)}, bf16[2,128,8,128]{3,2,1,0:T(8,128)(2,1)}, u32[]{:S(2)}) copy-start(bf16[2,128,8,128]{3,2,1,0:T(8,128)(2,1)} %pad_maximum_fusion.3) | copy-start | bytes 1572868
  57.3 51.9 %collective-permute-start = (bf16[2,128,8,128]{3,2,1,0:T(8,128)(2,1)S(1)}, bf16[2,128,8,128]{3,2,1,0:T(8,128)(2,1)S(1)}, u32[]{:S(2)}, u32[]{:S(2)}) collective-permute-start(bf16[2,128,8,128]{3,2,1,0:T(8,128)(2,1)S(1)} %copy-done.10), channel_id=1, source_target_pairs={{0,8},{8,0},{16,24},{24,16},{1,9},{9,1},{17,25},{25,17},{2,10},{10... | collective-permute-start | bytes 1572872 | tf_op jit(solution)/shard_map/ppermute | solution.py:520
  165.4 18.3 %copy-start.30 = (s32[4]{0:T(128)S(1)}, s32[4]{0:T(128)}, u32[]{:S(2)}) copy-start(s32[4]{0:T(128)} %lens_ref.5) | copy-start | bytes 52
  165.4 2.8 %collective-permute-start.16 = (bf16[3712,128]{1,0:T(8,128)(2,1)}, bf16[3712,128]{1,0:T(8,128)(2,1)S(1)}, u32[]{:S(2)}, u32[]{:S(2)}) collective-permute-start(bf16[3712,128]{1,0:T(8,128)(2,1)} %get-tuple-element.44), channel_id=1, source_target_pairs={{0,1},{1,0},{2,3},{3,2},{4,5},{5,4},{6,7},{7,6},{8,9},{9,8},{10,11... | collective-permute-start | bytes 2850824 | tf_op jit(solution)/shard_map/ppermute | solution.py:520
  172.5 10.4 %collective-permute-start.17 = (bf16[928,128]{1,0:T(8,128)(2,1)}, bf16[928,128]{1,0:T(8,128)(2,1)S(1)}, u32[]{:S(2)}, u32[]{:S(2)}) collective-permute-start(bf16[928,128]{1,0:T(8,128)(2,1)} %get-tuple-element.47), channel_id=1, source_target_pairs={{0,2},{1,3},{2,0},{3,1},{4,6},{5,7},{6,4},{7,5},{8,10},{9,11},{10,... | collective-permute-start | bytes 712712 | tf_op jit(solution)/shard_map/ppermute | solution.py:520
  172.9 45.8 %collective-permute-start.13 = (bf16[128,16,128]{2,1,0:T(8,128)(2,1)}, bf16[128,16,128]{2,1,0:T(8,128)(2,1)S(1)}, u32[]{:S(2)}, u32[]{:S(2)}) collective-permute-start(bf16[128,16,128]{2,1,0:T(8,128)(2,1)} %get-tuple-element.40), channel_id=1, source_target_pairs={{8,0},{0,8},{24,16},{16,24},{9,1},{1,9},{25,17},{17,25},{10,2},{2,... | collective-permute-start | bytes 1572872 | tf_op jit(solution)/shard_map/ppermute | solution.py:520
  174.4 45.9 %collective-permute-start.14 = (bf16[128,16,128]{2,1,0:T(8,128)(2,1)}, bf16[128,16,128]{2,1,0:T(8,128)(2,1)S(1)}, u32[]{:S(2)}, u32[]{:S(2)}) collective-permute-start(bf16[128,16,128]{2,1,0:T(8,128)(2,1)} %get-tuple-element.41), channel_id=1, source_target_pairs={{16,0},{24,8},{0,16},{8,24},{17,1},{25,9},{1,17},{9,25},{18,2},{26... | collective-permute-start | bytes 1572872 | tf_op jit(solution)/shard_map/ppermute | solution.py:520
  176.0 44.3 %collective-permute-start.15 = (bf16[128,16,128]{2,1,0:T(8,128)(2,1)}, bf16[128,16,128]{2,1,0:T(8,128)(2,1)S(1)}, u32[]{:S(2)}, u32[]{:S(2)}) collective-permute-start(bf16[128,16,128]{2,1,0:T(8,128)(2,1)} %get-tuple-element.42), channel_id=1, source_target_pairs={{24,0},{16,8},{8,16},{0,24},{25,1},{17,9},{9,17},{1,25},{26,2},{18... | collective-permute-start | bytes 1572872 | tf_op jit(solution)/shard_map/ppermute | solution.py:520
  176.4 20.0 %collective-permute-start.18 = (bf16[928,128]{1,0:T(8,128)(2,1)}, bf16[928,128]{1,0:T(8,128)(2,1)S(1)}, u32[]{:S(2)}, u32[]{:S(2)}) collective-permute-start(bf16[928,128]{1,0:T(8,128)(2,1)} %get-tuple-element.48), channel_id=1, source_target_pairs={{0,4},{1,5},{2,6},{3,7},{4,0},{5,1},{6,2},{7,3},{8,12},{9,13},{10,... | collective-permute-start | bytes 712712 | tf_op jit(solution)/shard_map/ppermute | solution.py:520
  182.8 13.6 %copy-start.12 = (bf16[928,128]{1,0:T(8,128)(2,1)}, bf16[928,128]{1,0:T(8,128)(2,1)S(1)}, u32[]{:S(2)}) copy-start(bf16[928,128]{1,0:T(8,128)(2,1)S(1)} %collective-permute-done.17.refs_0_) | copy-start | bytes 712708
  182.8 13.6 %collective-permute-start.19 = (bf16[928,128]{1,0:T(8,128)(2,1)}, bf16[928,128]{1,0:T(8,128)(2,1)S(1)}, u32[]{:S(2)}, u32[]{:S(2)}) collective-permute-start(bf16[928,128]{1,0:T(8,128)(2,1)} %get-tuple-element.49), channel_id=1, source_target_pairs={{0,6},{1,7},{2,4},{3,5},{4,2},{5,3},{6,0},{7,1},{8,14},{9,15},{10,... | collective-permute-start | bytes 712712 | tf_op jit(solution)/shard_map/ppermute | solution.py:520
  200.8 5.7 %collective-permute-start.20 = (bf16[416,128]{1,0:T(8,128)(2,1)}, bf16[416,128]{1,0:T(8,128)(2,1)S(1)}, u32[]{:S(2)}, u32[]{:S(2)}) collective-permute-start(bf16[416,128]{1,0:T(8,128)(2,1)} %get-tuple-element.51), channel_id=1, source_target_pairs={{0,8},{8,0},{16,24},{24,16},{1,9},{9,1},{17,25},{25,17},{2,10},{10... | collective-permute-start | bytes 319496 | tf_op jit(solution)/shard_map/ppermute | solution.py:520
  202.3 6.4 %collective-permute-start.21 = (bf16[416,128]{1,0:T(8,128)(2,1)}, bf16[416,128]{1,0:T(8,128)(2,1)S(1)}, u32[]{:S(2)}, u32[]{:S(2)}) collective-permute-start(bf16[416,128]{1,0:T(8,128)(2,1)} %get-tuple-element.52), channel_id=1, source_target_pairs={{0,16},{8,24},{16,0},{24,8},{1,17},{9,25},{17,1},{25,9},{2,18},{10... | collective-permute-start | bytes 319496 | tf_op jit(solution)/shard_map/ppermute | solution.py:520
  206.5 5.8 %copy-start.19 = (bf16[416,128]{1,0:T(8,128)(2,1)}, bf16[416,128]{1,0:T(8,128)(2,1)S(1)}, u32[]{:S(2)}) copy-start(bf16[416,128]{1,0:T(8,128)(2,1)S(1)} %collective-permute-done.20.refs_0_) | copy-start | bytes 319492
  206.5 5.8 %collective-permute-start.22 = (bf16[416,128]{1,0:T(8,128)(2,1)}, bf16[416,128]{1,0:T(8,128)(2,1)S(1)}, u32[]{:S(2)}, u32[]{:S(2)}) collective-permute-start(bf16[416,128]{1,0:T(8,128)(2,1)} %get-tuple-element.53), channel_id=1, source_target_pairs={{0,24},{8,16},{16,8},{24,0},{1,25},{9,17},{17,9},{25,1},{2,26},{10... | collective-permute-start | bytes 319496 | tf_op jit(solution)/shard_map/ppermute | solution.py:520
  208.7 3.7 %copy-start.20 = (bf16[416,128]{1,0:T(8,128)(2,1)}, bf16[416,128]{1,0:T(8,128)(2,1)S(1)}, u32[]{:S(2)}) copy-start(bf16[416,128]{1,0:T(8,128)(2,1)S(1)} %collective-permute-done.21.refs_1_) | copy-start | bytes 319492
  214.8 10.3 %collective-permute-start.23 = (bf16[160,128]{1,0:T(8,128)(2,1)}, bf16[160,128]{1,0:T(8,128)(2,1)S(1)}, u32[]{:S(2)}, u32[]{:S(2)}) collective-permute-start(bf16[160,128]{1,0:T(8,128)(2,1)} %get-tuple-element.55.refs_0_), channel_id=1, source_target_pairs={{0,2},{1,3},{2,0},{3,1},{4,6},{5,7},{6,4},{7,5},{8,10},{9,11},{10,... | collective-permute-start | bytes 122888 | tf_op jit(solution)/shard_map/ppermute | solution.py:520
  217.8 7.3 %collective-permute-start.24 = (bf16[160,128]{1,0:T(8,128)(2,1)}, bf16[160,128]{1,0:T(8,128)(2,1)S(1)}, u32[]{:S(2)}, u32[]{:S(2)}) collective-permute-start(bf16[160,128]{1,0:T(8,128)(2,1)} %get-tuple-element.55.refs_0_), channel_id=1, source_target_pairs={{0,4},{1,5},{2,6},{3,7},{4,0},{5,1},{6,2},{7,3},{8,12},{9,13},{10,... | collective-permute-start | bytes 122888 | tf_op jit(solution)/shard_map/ppermute | solution.py:520
  218.8 1.6 copy-start.7
  218.8 6.3 %collective-permute-start.25 = (bf16[160,128]{1,0:T(8,128)(2,1)}, bf16[160,128]{1,0:T(8,128)(2,1)S(1)}, u32[]{:S(2)}, u32[]{:S(2)}) collective-permute-start(bf16[160,128]{1,0:T(8,128)(2,1)} %get-tuple-element.55.refs_0_), channel_id=1, source_target_pairs={{0,6},{1,7},{2,4},{3,5},{4,2},{5,3},{6,0},{7,1},{8,14},{9,15},{10,... | collective-permute-start | bytes 122888 | tf_op jit(solution)/shard_map/ppermute | solution.py:520
  220.3 1.0 copy-start.9
  (11 other events, 8.1 us)
